TPU v7x, 128 devices: a whole 4x4x4 slice. The times are simulated.
128 devices in a mesh: resp: 4 (over z_hi, core), ctx: 32 (over x, z_lo, y).
Axes of the slice: x: 4, y: 4, z: 4 (z_hi: 2, z_lo: 2; z = z_hi * 2 + z_lo), core: 2. Of those that a mesh axis runs over, the one named last changes fastest.
Arguments:
- queries: bfloat16 [4, 4096, 32, 128], P('resp', 'ctx'), may hold values from -12 to 12
- resp_keys: bfloat16 [4, 4096, 4, 128], P('resp', 'ctx'), may hold values from -6 to 6
- resp_values: bfloat16 [4, 4096, 4, 128], P('resp', 'ctx'), may hold values from -6 to 6
- prompt_keys: bfloat16 [512, 4, 128], P('ctx', 'resp'), may hold values from -6 to 6
- prompt_values: bfloat16 [512, 4, 128], P('ctx', 'resp'), may hold values from -6 to 6
- grad_out: bfloat16 [4, 4096, 32, 128], P('resp', 'ctx'), may hold values from -24 to 24
- attn_out: bfloat16 [4, 4096, 32, 128], P('resp', 'ctx'), may hold values from -6 to 6
- logsumexp: float32 [4, 4096, 32], P('resp', 'ctx'), as said below
- order: int32 [4, 4096], P('resp'), may hold values from 0 to 4095, as said below
- lengths: int32 [4], P('resp'), may hold values from 1024 to 4096, as said below
Outputs:
- grad_queries: bfloat16 [4, 4096, 32, 128], P('resp', 'ctx')
- grad_resp_keys: bfloat16 [4, 4096, 4, 128], P('resp', 'ctx')
- grad_resp_values: bfloat16 [4, 4096, 4, 128], P('resp', 'ctx')
- grad_prompt_keys: bfloat16 [512, 4, 128], P('ctx', 'resp')
- grad_prompt_values: bfloat16 [512, 4, 128], P('ctx', 'resp')
Inputs may be any that keep to these rules, and one draw needn't show every extreme that they name: `order`: each row is a permutation of 0 to 4095. Cut the positions into runs of 64; the 128 slots of one index of ctx hold run a and then run 2 * 32 - 1 - a, each in rising order, with a drawn afresh for each response. `lengths`: slots whose position is at or past the length are padding; in every draw some response has all 4096 tokens live. `logsumexp`: the log of the sum of exp(scores) over the visible keys of each live slot and head, computed in float32 by the forward pass; 0 at padding slots.
All inputs are finite; a program needn't handle non-finite values.
Results may differ from a plain program's by a relative error of at most 0.0051.
Values may be sent and summed in bfloat16 or wider, within the bound.
No kernel may reach another device: no remote copies, remote signals or barrier semaphores. Data moves between devices by JAX's collectives and lax.ppermute only.
A program may use at most 320 MiB of HBM per device.

v0:
```python
import jax
import jax.numpy as jnp
from jax import lax
from jax.sharding import PartitionSpec as P


def block_grads(
    query_four,
    grad_four,
    lse_three,
    delta_three,
    query_pos,
    query_live,
    key_block,
    value_block,
    key_pos,
    score_scale,
):
    scores = (
        jnp.einsum("tgrd,kgd->gtrk", query_four, key_block, preferred_element_type=jnp.float32)
        * score_scale
    )
    visible = (key_pos[None, :] <= query_pos[:, None]) & query_live[:, None]
    probs = jnp.where(visible[None, :, None, :], jnp.exp(scores - lse_three[..., None]), 0.0)
    dprobs = jnp.einsum(
        "tgrd,kgd->gtrk", grad_four, value_block, preferred_element_type=jnp.float32
    )
    dscores = probs * (dprobs - delta_three[..., None])
    probs_b = probs.astype(jnp.bfloat16)
    dscores_b = dscores.astype(jnp.bfloat16)
    query_grad = (
        jnp.einsum("gtrk,kgd->tgrd", dscores_b, key_block, preferred_element_type=jnp.float32)
        * score_scale
    )
    key_grad = (
        jnp.einsum("gtrk,tgrd->kgd", dscores_b, query_four, preferred_element_type=jnp.float32)
        * score_scale
    )
    value_grad = jnp.einsum(
        "gtrk,tgrd->kgd", probs_b, grad_four, preferred_element_type=jnp.float32
    )
    return (query_grad, key_grad, value_grad)


def shards(
    queries,
    resp_keys,
    resp_values,
    prompt_keys,
    prompt_values,
    grad_out,
    attn_out,
    logsumexp,
    order,
    lengths,
):
    token_rows = queries.shape[1]
    head_count = queries.shape[2]
    head_dim = queries.shape[3]
    kv_count = resp_keys.shape[2]
    group_size = head_count // kv_count
    prompt_rows = prompt_keys.shape[0]
    score_scale = head_dim ** (-0.5)
    position = lax.axis_index("ctx")
    order_row = order[0]
    length_total = order_row.shape[0]
    query_pos = lax.dynamic_slice_in_dim(order_row, position * token_rows, token_rows)
    query_live = query_pos < lengths[0]
    query_four = queries[0].reshape(token_rows, kv_count, group_size, head_dim)
    grad_four = grad_out[0].reshape(token_rows, kv_count, group_size, head_dim)
    delta = jnp.sum(grad_out[0].astype(jnp.float32) * attn_out[0].astype(jnp.float32), axis=-1)
    delta_three = delta.reshape(token_rows, kv_count, group_size).transpose(1, 0, 2)
    lse_three = logsumexp[0].reshape(token_rows, kv_count, group_size).transpose(1, 0, 2)
    prompt_key_all, prompt_value_all = (
        lax.all_gather(prompt_keys, "resp", axis=1, tiled=True),
        lax.all_gather(prompt_values, "resp", axis=1, tiled=True),
    )
    key_local = jnp.concatenate([prompt_key_all, resp_keys[0]], axis=0)
    value_local = jnp.concatenate([prompt_value_all, resp_values[0]], axis=0)
    key_count = key_local.shape[0]
    key_piece = lax.all_gather(key_local, "ctx", axis=0, tiled=True)
    value_piece = lax.all_gather(value_local, "ctx", axis=0, tiled=True)
    piece_rows = key_piece.shape[0]
    global_rows = jnp.arange(piece_rows, dtype=jnp.int32)
    owner_dev = global_rows // key_count
    within = global_rows % key_count
    slot_index = jnp.clip(owner_dev * token_rows + within - prompt_rows, 0, length_total - 1)
    key_pos = jnp.where(within < prompt_rows, -1, order_row[slot_index])
    query_part, key_part, value_part = block_grads(
        query_four,
        grad_four,
        lse_three,
        delta_three,
        query_pos,
        query_live,
        key_piece,
        value_piece,
        key_pos,
        score_scale,
    )
    key_all = key_part
    value_all = value_part
    query_grad, key_all, value_all = (query_part, key_all, value_all)
    mine_key, mine_value = (
        lax.psum_scatter(key_all, "ctx", scatter_dimension=0, tiled=True),
        lax.psum_scatter(value_all, "ctx", scatter_dimension=0, tiled=True),
    )
    prompt_key_grad, prompt_value_grad = (
        lax.psum_scatter(mine_key[:prompt_rows], "resp", scatter_dimension=1, tiled=True),
        lax.psum_scatter(mine_value[:prompt_rows], "resp", scatter_dimension=1, tiled=True),
    )
    return (
        query_grad.reshape(token_rows, head_count, head_dim).astype(jnp.bfloat16)[None],
        mine_key[prompt_rows:].astype(jnp.bfloat16)[None],
        mine_value[prompt_rows:].astype(jnp.bfloat16)[None],
        prompt_key_grad.astype(jnp.bfloat16),
        prompt_value_grad.astype(jnp.bfloat16),
    )


def solution(mesh):
    return jax.shard_map(
        shards,
        mesh=mesh,
        in_specs=(
            P("resp", "ctx", None, None),
            P("resp", "ctx", None, None),
            P("resp", "ctx", None, None),
            P("ctx", "resp", None),
            P("ctx", "resp", None),
            P("resp", "ctx", None, None),
            P("resp", "ctx", None, None),
            P("resp", "ctx", None),
            P("resp", None),
            P("resp"),
        ),
        out_specs=(
            P("resp", "ctx", None, None),
            P("resp", "ctx", None, None),
            P("resp", "ctx", None, None),
            P("ctx", "resp", None),
            P("ctx", "resp", None),
        ),
        check_vma=False,
    )
```

profile of v0, /device:TPU:1, one launch (start us, length us, event | category | flops | bytes accessed | tf_op | source)
XLA Modules:
  0.0 824.5 jit_solution(11045930219865563809)
XLA Ops:
  7.2 0.0 copy-start
  7.2 0.0 all-gather.3.cloned.1.call-start
  7.2 1.0 copy.73
  8.2 8.6 %all_gather.12 = bf16[16,4,128]{2,0,1:T(8,128)(2,1)S(1)} all-gather(bf16[16,1,128]{2,0,1:T(8,128)(2,1)} %param.13), channel_id=1, replica_groups=mesh['resp'=4,'ctx'=32] {'resp'}, dimensions={1}, use_global_device_ids=true | all-gather | bytes 20480 | tf_op jit(solution)/shard_map/all_gather | solution.py:75
  16.8 0.7 pad_maximum_fusion
  17.5 0.0 all-gather.3.cloned.1.call-update
  17.5 0.0 all-gather.5.cloned.1.call-start
  17.5 0.9 copy.72
  18.5 7.0 all_gather.14
  25.5 0.7 pad_maximum_fusion.1
  26.1 0.0 all-gather.5.cloned.1.call-update
  26.2 0.0 reduce-scatter.5.cloned.1.call-start
  26.2 2.2 multiply_reduce_fusion
  28.4 0.1 copy.50
  29.1 0.2 fusion.28
  29.3 20.5 %gather_fusion = s32[4608]{0:T(1024)S(1)} fusion(s32[4096]{0:T(1024)} %bitcast.70, s32[5120]{0:T(1024)S(1)} %pad_clamp_fusion), kind=kCustom, calls=%fused_computation | custom fusion | bytes 55296 | tf_op jit(solution)/shard_map/gather | solution.py:88
  49.9 0.7 broadcast_compare_fusion
  50.5 2.1 compare_and_fusion
  52.6 107.3 %all-gather.3.cloned.1.call-done = bf16[4608,4,128]{2,0,1:T(8,128)(2,1)} async-done(((bf16[144,4,128]{2,0,1:T(8,128)(2,1)}), bf16[4608,4,128]{2,0,1:T(8,128)(2,1)}) %all-gather.3.cloned.1.call-update) | async-done | bytes 4718608 | tf_op jit(solution)/shard_map/all_gather | solution.py:81
  159.9 0.0 copy-done
  160.0 0.0 copy-start.1
  160.0 0.0 copy-start.2
  160.0 28.4 %fusion.12 = f32[4,4608,128,8]{2,1,3,0:T(8,128)} fusion(bf16[4608,4,128]{2,0,1:T(8,128)(2,1)} %all-gather.3.cloned.1.call-done, bf16[128,4,8,128]{3,2,1,0:T(8,128)(2,1)S(1)} %bitcast.68), kind=kOutput, calls=%fused_computation.13 | convolution fusion | flops 4831838208 | bytes 81264640 | tf_op jit(solution)/shard_map/tgrd,kgd->gtrk/dot_general | solution.py:20
  188.4 131.6 %all-gather.5.cloned.1.call-done = bf16[4608,4,128]{2,0,1:T(8,128)(2,1)} async-done(((bf16[144,4,128]{2,0,1:T(8,128)(2,1)}), bf16[4608,4,128]{2,0,1:T(8,128)(2,1)}) %all-gather.5.cloned.1.call-update) | async-done | bytes 4718608 | tf_op jit(solution)/shard_map/all_gather | solution.py:82
  320.0 0.0 copy-done.1
  320.0 0.0 copy-done.2
  320.0 43.6 %fusion = bf16[4,128,8,4608]{1,3,2,0:T(8,128)(2,1)} fusion(f32[4,4608,128,8]{2,1,3,0:T(8,128)} %fusion.12, f32[4,128,8]{1,2,0:T(8,128)S(1)} %bitcast.76, f32[4,128,8]{1,2,0:T(8,128)S(1)} %bitcast.77, pred[128,4608]{0,1:T(8,128)(4,1)S(1)} %compare_and_fusion, bf16[4608,4,128]{2,0,1:T(8,128)(2,1)} %all-gather.5.cloned.1.call-done, ...), kind=kOutput, calls=%fused_computation.2 | convolution fusion | flops 4945084416 | bytes 119635968 | tf_op jit(solution)/shard_map/tgrd,kgd->gtrk/dot_general | solution.py:25
  363.6 19.1 %fusion.5 = f32[4608,4,128]{2,0,1:T(8,128)} fusion(bf16[4,128,8,4608]{1,3,2,0:T(8,128)(2,1)} %fusion, bf16[128,4,8,128]{3,2,1,0:T(8,128)(2,1)S(1)} %bitcast.69), kind=kOutput, calls=%fused_computation.8 | convolution fusion | flops 4834197504 | bytes 48234496 | tf_op jit(solution)/shard_map/gtrk,tgrd->kgd/dot_general | solution.py:36
  382.7 0.0 reduce-scatter.5.cloned.1.call-update
  382.7 0.0 reduce-scatter.7.cloned.1.call-start
  382.7 30.0 %fusion.6 = f32[4608,4,128]{2,0,1:T(8,128)} fusion(f32[4,4608,128,8]{2,1,3,0:T(8,128)} %fusion.12, f32[4,128,8]{1,2,0:T(8,128)S(1)} %bitcast.78, pred[128,4608]{0,1:T(8,128)(4,1)S(1)} %compare_and_fusion, bf16[128,4,8,128]{3,2,1,0:T(8,128)(2,1)S(1)} %bitcast.73), kind=kOutput, calls=%fused_computation.9 | convolution fusion | flops 4907335680 | bytes 86589440 | tf_op jit(solution)/shard_map/gtrk,tgrd->kgd/dot_general | solution.py:39
  412.7 0.0 reduce-scatter.7.cloned.1.call-update
  412.7 0.0 reduce-scatter.9.cloned.1.call-start
  412.8 146.8 %reduce-scatter.5.cloned.1.call-done = f32[144,4,128]{2,0,1:T(8,128)} async-done(((f32[4608,4,128]{2,0,1:T(8,128)}), f32[144,4,128]{2,0,1:T(8,128)}) %reduce-scatter.5.cloned.1.call-update) | async-done | bytes 294928 | tf_op jit(solution)/shard_map/reduce_scatter | solution.py:105
  559.6 1.4 slice.22
  560.9 0.0 reduce-scatter.9.cloned.1.call-update
  561.0 0.0 reduce-scatter.11.cloned.1.call-start
  561.0 16.2 %multiply_convert_fusion = bf16[4,128,128,8]{2,1,3,0:T(8,128)(2,1)S(1)} fusion(bf16[4,128,8,4608]{1,3,2,0:T(8,128)(2,1)} %fusion, bf16[4608,4,128]{2,0,1:T(8,128)(2,1)} %all-gather.3.cloned.1.call-done), kind=kOutput, calls=%fused_computation.16 | convolution fusion | flops 4832886784 | bytes 43515904 | tf_op jit(solution)/shard_map/gtrk,kgd->tgrd/dot_general | solution.py:32
  577.2 1.7 copy.54
  578.9 161.5 %reduce-scatter.7.cloned.1.call-done = f32[144,4,128]{2,0,1:T(8,128)} async-done(((f32[4608,4,128]{2,0,1:T(8,128)}), f32[144,4,128]{2,0,1:T(8,128)}) %reduce-scatter.7.cloned.1.call-update) | async-done | bytes 294928 | tf_op jit(solution)/shard_map/reduce_scatter | solution.py:106
  740.4 1.4 slice.23
  741.8 0.0 reduce-scatter.11.cloned.1.call-update
  741.8 1.0 fusion.20
  742.8 1.0 fusion.21
  743.8 0.8 copy.55
  744.5 0.8 copy.56
  745.3 42.9 %reduce-scatter.9.cloned.1.call-done = f32[16,1,128]{2,0,1:T(8,128)} async-done(((f32[16,4,128]{2,0,1:T(8,128)}), f32[16,1,128]{2,0,1:T(8,128)}) %reduce-scatter.9.cloned.1.call-update) | async-done | bytes 8208 | tf_op jit(solution)/shard_map/reduce_scatter | solution.py:109
  788.2 1.3 convert_element_type.45
  789.5 26.9 %reduce-scatter.11.cloned.1.call-done = f32[16,1,128]{2,0,1:T(8,128)} async-done(((f32[16,4,128]{2,0,1:T(8,128)}), f32[16,1,128]{2,0,1:T(8,128)}) %reduce-scatter.11.cloned.1.call-update) | async-done | bytes 8208 | tf_op jit(solution)/shard_map/reduce_scatter | solution.py:110
  816.4 1.3 convert_element_type.46
  (2 shorter events, 0.0 us)
Async XLA Ops:
  7.2 152.8 %copy-start = (bf16[1,128,32,128]{3,2,1,0:T(8,128)(2,1)S(1)}, bf16[1,128,32,128]{3,2,1,0:T(8,128)(2,1)}, u32[]{:S(2)}) copy-start(bf16[1,128,32,128]{3,2,1,0:T(8,128)(2,1)} %param.10) | copy-start | bytes 3145732
  7.2 152.8 %all-gather.3.cloned.1.call-start = ((), (), s32[]{:S(2)}) async-start(), calls=%async_computation.4 | async-start | bytes 4866048 | tf_op jit(solution)/shard_map/all_gather | solution.py:81
  17.5 302.5 %all-gather.5.cloned.1.call-start = ((), (), s32[]{:S(2)}) async-start(), calls=%async_computation.5 | async-start | bytes 4866048 | tf_op jit(solution)/shard_map/all_gather | solution.py:82
  26.2 533.4 %reduce-scatter.5.cloned.1.call-start = ((), (), s32[]{:S(2)}) async-start(), calls=%async_computation.6 | async-start | bytes 9732096 | tf_op jit(solution)/shard_map/reduce_scatter | solution.py:105
  160.0 160.0 %copy-start.1 = (bf16[1,128,32,128]{3,2,1,0:T(8,128)(2,1)S(1)}, bf16[1,128,32,128]{3,2,1,0:T(8,128)(2,1)}, u32[]{:S(2)}) copy-start(bf16[1,128,32,128]{3,2,1,0:T(8,128)(2,1)} %param.15) | copy-start | bytes 3145732
  160.0 160.0 %copy-start.2 = (f32[1,128,32]{1,2,0:T(8,128)S(1)}, f32[1,128,32]{1,2,0:T(8,128)}, u32[]{:S(2)}) copy-start(f32[1,128,32]{1,2,0:T(8,128)} %param.17) | copy-start | bytes 49156
  382.7 357.7 %reduce-scatter.7.cloned.1.call-start = ((), (), s32[]{:S(2)}) async-start(), calls=%async_computation.7 | async-start | bytes 9732096 | tf_op jit(solution)/shard_map/reduce_scatter | solution.py:106
  412.7 375.5 %reduce-scatter.9.cloned.1.call-start = ((), (), s32[]{:S(2)}) async-start(), calls=%async_computation.8 | async-start | bytes 40960 | tf_op jit(solution)/shard_map/reduce_scatter | solution.py:109
  561.0 255.4 %reduce-scatter.11.cloned.1.call-start = ((), (), s32[]{:S(2)}) async-start(), calls=%async_computation.9 | async-start | bytes 40960 | tf_op jit(solution)/shard_map/reduce_scatter | solution.py:110
Sparse Core Ops, SparseCore 0:
  17.6 142.2 all-gather.2
  161.6 158.3 all-gather.4
  382.8 176.7 reduce-scatter.4
  561.8 178.5 reduce-scatter.6
  742.8 45.3 reduce-scatter.8
  790.7 25.5 reduce-scatter.10
where the time goes:
time: 825 us; the launch traced here: 824 us
  waiting for transfers between devices  617 us (75%)
  matrix products  137 us (17%)
  local copies, waits for them, and re-layouts  30.4 us (4%)
  blocking collectives  15.6 us (2%)
  between operations  14.9 us (2%)
  other arithmetic  9.02 us (1%)
    reduce_scatter x1, waiting for transfers between devices, shards(): lax.psum_scatter(value_all, 'ctx', scatter_dimension=0, tiled=True)  161 us
    reduce_scatter x1, waiting for transfers between devices, shards(): lax.psum_scatter(key_all, 'ctx', scatter_dimension=0, tiled=True)  147 us
    all_gather x1, waiting for transfers between devices, shards(): value_piece = lax.all_gather(value_local, 'ctx', axis=0, tiled=True)  132 us
    all_gather x1, waiting for transfers between devices, shards(): key_piece = lax.all_gather(key_local, 'ctx', axis=0, tiled=True)  107 us
    dot_general x1, matrix products, block_grads(): jnp.einsum('tgrd,kgd->gtrk', grad_four, value_block, preferred_element_ty...  43.6 us
    reduce_scatter x1, waiting for transfers between devices, shards(): lax.psum_scatter(mine_key[:prompt_rows], 'resp', scatter_dimension=1, til...  42.9 us
    dot_general x1, matrix products, block_grads(): jnp.einsum('gtrk,tgrd->kgd', probs_b, grad_four, preferred_element_type=j...  30 us
    dot_general x1, matrix products, block_grads(): jnp.einsum('tgrd,kgd->gtrk', query_four, key_block, preferred_element_typ...  28.4 us
  transfers between devices with their start and end apart: 6, of which 6 were waited for; matrix products, arithmetic and copies ran while one was open for 13% of the time, Pallas kernels for 0%

commit v1 on v0

v1 whole, which is shorter than its diff:
```python
import functools

import jax
import jax.numpy as jnp
from jax import lax
from jax.experimental import pallas as pl
from jax.experimental.pallas import tpu as pltpu
from jax.sharding import PartitionSpec as P

F32 = jnp.float32
BF16 = jnp.bfloat16
AXES = ("resp", "ctx")
LOG2E = 1.4426950408889634
RUN = 64
NT = (((1,), (1,)), ((), ()))
NN = (((1,), (0,)), ((), ()))
TN = (((0,), (0,)), ((), ()))
FAR = 1 << 20


def coords(r, c):
    return c // 8, (c // 4) % 2, c % 4, r % 2


def device_pairs(move):
    pairs = []
    for r in range(4):
        for c in range(32):
            x, z, y, _ = coords(r, c)
            r2, x2, z2, y2 = move(r, x, z, y)
            pairs.append((r * 32 + c, (r2 % 4) * 32 + (x2 % 4) * 8 + (z2 % 2) * 4 + y2 % 4))
    return pairs


def along_heads(s):
    return device_pairs(lambda r, x, z, y: (r, x, z, y + s) if r % 2 == 0 else (r, x + s, z, y))


def along_blocks(s):
    return device_pairs(lambda r, x, z, y: (r, x + s, z, y) if r % 2 == 0 else (r, x, z, y + s))


def along_z():
    return device_pairs(lambda r, x, z, y: (r, x, z + 1, y))


def along_resp(s):
    return device_pairs(lambda r, x, z, y: (r + s, x, z, y))


def send(value, pairs):
    return lax.ppermute(value, AXES, pairs)


def dot(a, b, dims):
    return lax.dot_general(a, b, dims, preferred_element_type=F32)


def grads_kernel(
    first,
    last,
    scale,
    slot_ref,
    pos_ref,
    qpos_ref,
    c0_ref,
    c1_ref,
    c2_ref,
    c3_ref,
    kv_ref,
    *rest,
):
    if first:
        dq_out, dkv_out, chunk, dkv, dq_acc = rest
        dq_in = None
    else:
        dq_in, dq_out, dkv_out, chunk, dkv, dq_acc = rest
    rows = 512
    for i, ref in enumerate((c0_ref, c1_ref, c2_ref, c3_ref)):
        chunk[pl.ds(i * 2096, 2096), :] = ref[...]
    dkv[...] = jnp.zeros_like(dkv)
    key_base = 16
    value_base = 144 + 16

    def one_run(i, _):
        base = (i // 2) * 2096
        half = i % 2
        q_rows = pl.ds(pl.multiple_of(base + half * rows, 16), rows)
        g_rows = pl.ds(pl.multiple_of(base + 1024 + half * rows, 16), rows)
        own = qpos_ref[i]
        stats = []
        for j in range(2):
            piece = chunk[pl.ds(pl.multiple_of(base + 2048, 16), 48), :].astype(F32)
            total = piece[24 * j : 24 * j + 8] + piece[24 * j + 8 : 24 * j + 16] + piece[24 * j + 16 : 24 * j + 24]
            picked = jnp.where(half == 0, total[0:4], total[4:8])
            stats.append(jnp.concatenate([picked[k : k + 1] for k in range(4)], axis=1))
        lse2, delta = stats
        acc_rows = pl.ds(pl.multiple_of(i * 128, 128), 128)
        if first:
            dq_acc[...] = jnp.zeros_like(dq_acc)
        else:
            dq_acc[...] = dq_in[acc_rows, :]

        def tile(keys, values, key_pos):
            q = chunk[q_rows, :]
            g = chunk[g_rows, :]
            s = dot(keys, q, NT)
            p = jnp.exp2(s * (scale * LOG2E) - lse2)
            if key_pos is not None:
                row_pos = own * RUN + (lax.broadcasted_iota(jnp.int32, (1, rows), 1) >> 3)
                p = jnp.where(key_pos <= row_pos, p, 0.0)
            dp = dot(values, g, NT)
            ds = (p * (dp - delta)).astype(BF16)
            dv = dot(p.astype(BF16), g, NN)
            dk = dot(ds, q, NN)
            dq_acc[...] += dot(keys, ds, TN)
            return dk, dv

        def gather(entries):
            keys = jnp.concatenate([kv_ref[pl.ds(k, n), :] for k, n, _ in entries], axis=0)
            values = jnp.concatenate([kv_ref[pl.ds(k + 144, n), :] for k, n, _ in entries], axis=0)
            return keys, values

        def scatter(entries, dk, dv):
            at = 0
            for k, n, _ in entries:
                dkv[pl.ds(k, n), :] += dk[at : at + n]
                dkv[pl.ds(k + 144, n), :] += dv[at : at + n]
                at += n

        def positions(entries):
            parts = []
            for _, n, where in entries:
                if where is None:
                    parts.append(jnp.full((n, 1), -1, jnp.int32))
                else:
                    parts.append(lax.broadcasted_iota(jnp.int32, (n, 1), 0) + where * RUN)
            return jnp.concatenate(parts, axis=0)

        def run_entry(j):
            slot = slot_ref[j]
            start = (slot // 2) * 288 + 16 + (slot % 2) * RUN
            return (pl.multiple_of(start, 16), RUN, pos_ref[j])

        def do(entries, masked):
            keys, values = gather(entries)
            dk, dv = tile(keys, values, positions(entries) if masked else None)
            scatter(entries, dk, dv)

        seen = 0
        for j in range(16):
            seen = seen + jnp.where(pos_ref[j] <= own, 1, 0)
        do([(e * 288, 16, None) for e in range(8)] + [run_entry(0), run_entry(1)], True)
        more = jnp.maximum(seen - 2, 0)
        full = jnp.maximum((more - 1) // 4, 0)

        def full_tile(t, _):
            do([run_entry(2 + 4 * t + m) for m in range(4)], False)
            return 0

        lax.fori_loop(0, full, full_tile, 0)

        @pl.when(more > 0)
        def _():
            do([run_entry(2 + 4 * full + m) for m in range(4)], True)

        if last:
            out_rows = pl.ds(pl.multiple_of(i * rows, rows), rows)
            dq_out[out_rows, :] = (dq_acc[...].T * scale).astype(BF16)
        else:
            dq_out[acc_rows, :] = dq_acc[...]
        return 0

    lax.fori_loop(0, 8, one_run, 0)
    for e in range(8):
        k_rows = pl.ds(e * 288, 144)
        v_rows = pl.ds(e * 288 + 144, 144)
        dkv_out[k_rows, :] = (dkv[k_rows, :] * scale).astype(dkv_out.dtype)
        dkv_out[v_rows, :] = dkv[v_rows, :].astype(dkv_out.dtype)


def block_grads(first, last, wide, scale, slots, poss, qpos, chunks, kv, dq):
    vmem = pl.BlockSpec(memory_space=pltpu.VMEM)
    smem = pl.BlockSpec(memory_space=pltpu.SMEM)
    operands = [slots, poss, qpos, *chunks, kv]
    specs = [smem] * 3 + [vmem] * 5
    if not first:
        operands.append(dq)
        specs.append(vmem)
    dq_shape = jax.ShapeDtypeStruct((4096, 128), BF16) if last else jax.ShapeDtypeStruct((1024, 512), F32)
    return pl.pallas_call(
        functools.partial(grads_kernel, first, last, scale),
        out_shape=[dq_shape, jax.ShapeDtypeStruct((2304, 128), F32 if wide else BF16)],
        in_specs=specs,
        out_specs=[vmem] * 2,
        scratch_shapes=[
            pltpu.VMEM((4 * 2096, 128), BF16),
            pltpu.VMEM((2304, 128), F32),
            pltpu.VMEM((128, 512), F32),
        ],
        compiler_params=pltpu.CompilerParams(vmem_limit_bytes=32 * 2**20),
        cost_estimate=pl.CostEstimate(flops=12_000_000_000, bytes_accessed=8_000_000, transcendentals=3_000_000),
    )(*operands)


def pick(stacked, index):
    return lax.dynamic_index_in_dim(stacked, index, 0, keepdims=False)


def thirds(value):
    hi = lax.reduce_precision(value, 8, 7)
    rest = value - hi
    mid = lax.reduce_precision(rest, 8, 7)
    return [hi.astype(BF16), mid.astype(BF16), (rest - mid).astype(BF16)]


def shards(
    queries,
    resp_keys,
    resp_values,
    prompt_keys,
    prompt_values,
    grad_out,
    attn_out,
    logsumexp,
    order,
    lengths,
):
    scale = queries.shape[3] ** (-0.5)
    r = lax.axis_index("resp")
    c = lax.axis_index("ctx")
    x, z, y, core = coords(r, c)
    head = jnp.where(core == 0, y, x)
    block = jnp.where(core == 0, x, y)

    prompt = jnp.stack([prompt_keys[:, 0], prompt_values[:, 0]])
    prompts = jnp.stack([prompt] + [send(prompt, along_resp(s)) for s in (1, 2, 3)])
    resp_kv = jnp.stack([resp_keys[0], resp_values[0]]).transpose(2, 0, 1, 3)

    def kv_chunk(g):
        rows = jnp.concatenate([pick(prompts, (r - g) % 4), pick(resp_kv, g)], axis=1)
        return rows.reshape(288, 128)

    pieces = [kv_chunk(head)]
    for s in (1, 2, 3):
        pieces.append(send(kv_chunk((head + s) % 4), along_heads(s)))
    near = jnp.concatenate(pieces, axis=0)
    kv_own = jnp.concatenate([near, send(near, along_z())], axis=0)
    kv_blocks = {0: kv_own}
    for s in (1, 3, 2):
        kv_blocks[s] = send(kv_own, along_blocks(s))

    query_pos = lax.dynamic_slice_in_dim(order[0], c * 128, 128)
    live = query_pos < lengths[0]
    delta = jnp.sum(grad_out[0].astype(F32) * attn_out[0].astype(F32), axis=-1)
    lse2 = jnp.where(live[:, None], logsumexp[0] * LOG2E, 1e30)
    stats = jnp.stack([lse2, delta]).reshape(2, 128, 4, 8).transpose(2, 0, 1, 3).reshape(4, 2, 8, 128)
    stats = jnp.stack(thirds(stats), axis=2).reshape(4, 48, 128)
    q_four = queries[0].reshape(128, 4, 8, 128)
    g_four = grad_out[0].reshape(128, 4, 8, 128)

    def q_chunk(g):
        q = lax.dynamic_index_in_dim(q_four, g, 1, keepdims=False).reshape(1024, 128)
        do = lax.dynamic_index_in_dim(g_four, g, 1, keepdims=False).reshape(1024, 128)
        return jnp.concatenate([q, do, pick(stats, g)], axis=0)

    chunks = [q_chunk(head)]
    for s in (1, 2, 3):
        chunks.append(send(q_chunk((head + s) % 4), along_heads(s)))

    run_pos = order[0].reshape(32, 2, RUN)[:, :, 0] // RUN
    shift_b = lax.broadcasted_iota(jnp.int32, (4, 2, 4, 1), 0)
    shift_z = lax.broadcasted_iota(jnp.int32, (4, 2, 4, 1), 1)
    shift_h = lax.broadcasted_iota(jnp.int32, (4, 2, 4, 1), 2)
    from_b = (block - shift_b) % 4
    from_h = (head - shift_h) % 4
    from_z = (z + shift_z) % 2
    owner = jnp.where(core == 0, from_b * 8 + from_h, from_h * 8 + from_b) + from_z * 4
    hit = owner[..., None] == jnp.arange(32, dtype=jnp.int32).reshape(1, 1, 1, 1, 32)
    runs = jnp.sum(jnp.where(hit, run_pos.T.reshape(1, 1, 1, 2, 32), 0), axis=-1)
    qpos = runs[0, 0].reshape(8)
    runs = runs.reshape(4, 16)
    rank = jnp.sum((runs[:, None, :] < runs[:, :, None]).astype(jnp.int32), axis=-1)
    place = rank[:, None, :] == jnp.arange(16, dtype=jnp.int32)[None, :, None]
    slots = jnp.sum(jnp.where(place, jnp.arange(16, dtype=jnp.int32)[None, None, :], 0), axis=-1)
    poss = jnp.sum(jnp.where(place, runs[:, None, :], 0), axis=-1)
    slots = jnp.pad(slots, ((0, 0), (0, 4)))
    poss = jnp.pad(poss, ((0, 0), (0, 4)), constant_values=FAR)

    dq = None
    totals = None
    turns = (0, 1, 3, 2)
    for i, s in enumerate(turns):
        dq, dkv = block_grads(
            i == 0, i == 3, s == 0, scale, slots[s], poss[s], qpos, chunks, kv_blocks[s], dq
        )
        if s == 0:
            totals = dkv
        else:
            totals = totals + send(dkv, along_blocks(4 - s)).astype(F32)

    back = [dq[:1024]]
    for s in (1, 2, 3):
        back.append(send(dq[1024 * s : 1024 * (s + 1)], along_heads(4 - s)))
    back = jnp.stack(back).reshape(4, 128, 8, 128)
    turn = (4 - head) % 4
    grad_queries = lax.dynamic_slice_in_dim(jnp.concatenate([back, back[:3]], axis=0), turn, 4, 0)
    grad_queries = grad_queries.transpose(1, 0, 2, 3).reshape(1, 128, 32, 128)

    mine = totals[:1152] + send(totals[1152:].astype(BF16), along_z()).astype(F32)
    mine = mine.astype(BF16).reshape(4, 2, 144, 128)
    rows = [mine[0]]
    for s in (1, 2, 3):
        rows.append(send(mine[s], along_heads(4 - s)))
    rows = jnp.stack(rows)
    rows = lax.dynamic_slice_in_dim(jnp.concatenate([rows, rows[:3]], axis=0), turn, 4, 0)
    grad_resp = rows[:, :, 16:].transpose(1, 2, 0, 3)
    parts = rows[:, :, :16]
    prompt_sum = pick(parts, r).astype(F32)
    for s in (1, 2, 3):
        prompt_sum = prompt_sum + send(pick(parts, (r + s) % 4), along_resp(s)).astype(F32)
    prompt_sum = prompt_sum.astype(BF16)
    return (
        grad_queries,
        grad_resp[0][None],
        grad_resp[1][None],
        prompt_sum[0][:, None],
        prompt_sum[1][:, None],
    )


def solution(mesh):
    wide = P("resp", "ctx", None, None)
    prompt = P("ctx", "resp", None)
    return jax.shard_map(
        shards,
        mesh=mesh,
        in_specs=(
            wide,
            wide,
            wide,
            prompt,
            prompt,
            wide,
            wide,
            P("resp", "ctx", None),
            P("resp", None),
            P("resp"),
        ),
        out_specs=(wide, wide, wide, prompt, prompt),
        check_vma=False,
    )
```

time: 825 us -> 151 us (0.18)
  waiting for transfers between devices: 617 us -> 35.8 us
  matrix products: 137 us -> 0 us
  Pallas kernels: 0 us -> 49.9 us
  starting transfers between devices: 0.25 us -> 42.2 us
  local copies, waits for them, and re-layouts: 30.4 us -> 13.4 us
  blocking collectives: 15.6 us -> 0 us
  between operations: 14.9 us -> 1.92 us
    reduce_scatter x4 -> x0, waiting for transfers between devices: 378 us -> none  [the longest x1 161 us: shards(): lax.psum_scatter(value_all, 'ctx', scatter_dimension=0, tiled=True)]
    all_gather x2 -> x0, waiting for transfers between devices: 239 us -> none  [the longest x1 132 us: shards(): value_piece = lax.all_gather(value_local, 'ctx', axis=0, tiled=True)]
    dot_general x5 -> x0, matrix products: 137 us -> none  [the longest x1 43.6 us: block_grads(): jnp.einsum('tgrd,kgd->gtrk', grad_four, value_block, preferred_element_ty...]
    pallas_call x0 -> x4, Pallas kernels: none -> 49.9 us  [block_grads(): pl.pallas_call(functools.partial(grads_kernel, first, last, scale), out_s...]
    ppermute x0 -> x26, starting transfers between devices: none -> 42.2 us  [send(): return lax.ppermute(value, AXES, pairs)]
    ppermute x0 -> x26, waiting for transfers between devices: none -> 35.8 us  [send(): return lax.ppermute(value, AXES, pairs)]
    gather x1 -> x0, local copies, waits for them, and re-layouts: 20.5 us -> none  [shards(): key_pos = jnp.where(within < prompt_rows, -1, order_row[slot_index])]
    all_gather x2 -> x0, blocking collectives: 15.6 us -> none  [the longest x1 8.56 us: shards(): lax.all_gather(prompt_keys, 'resp', axis=1, tiled=True)]
  transfers between devices with their start and end apart: 6 -> 26, of which waited for: 6 -> 13; matrix products, arithmetic and copies ran while one was open for 13% -> 8% of each run, Pallas kernels for 0% -> 25%
where the time goes in v1:
time: 151 us; the launch traced here: 150 us
  Pallas kernels  49.9 us (33%)
  starting transfers between devices  42.2 us (28%)
  waiting for transfers between devices  35.8 us (24%)
  local copies, waits for them, and re-layouts  13.4 us (9%)
  other arithmetic  6.87 us (5%)
  between operations  1.92 us (1%)
    pallas_call x4, Pallas kernels, block_grads(): pl.pallas_call(functools.partial(grads_kernel, first, last, scale), out_s...  49.9 us
    ppermute x26, starting transfers between devices, send(): return lax.ppermute(value, AXES, pairs)  42.2 us
    ppermute x26, waiting for transfers between devices, send(): return lax.ppermute(value, AXES, pairs)  35.8 us
    unnamed x51, local copies, waits for them, and re-layouts  8.39 us
  transfers between devices with their start and end apart: 26, of which 13 were waited for; matrix products, arithmetic and copies ran while one was open for 8% of the time, Pallas kernels for 25%

profile of v1, /device:TPU:1, one launch (start us, length us, event | category | flops | bytes accessed | tf_op | source)
XLA Modules:
  0.0 150.0 jit_solution(2498414924006212794)
XLA Ops:
  0.6 0.7 fusion.19
  1.3 5.0 %collective-permute-start.3 = (bf16[2,16,128]{2,1,0:T(8,128)(2,1)S(1)}, bf16[2,16,128]{2,1,0:T(8,128)(2,1)S(1)}, u32[]{:S(2)}, u32[]{:S(2)}) collective-permute-start(bf16[2,16,128]{2,1,0:T(8,128)(2,1)S(1)} %get-tuple-element.86), channel_id=1, source_target_pairs={{0,32},{1,33},{2,34},{3,35},{4,36},{5,37},{6,38},{7,39},{8,40},{9,... | collective-permute-start | bytes 24584 | tf_op jit(solution)/shard_map/ppermute | solution.py:52
  6.3 0.4 collective-permute-start.5
  7.4 2.2 %multiply_reduce_fusion = f32[128,32]{1,0:T(8,128)S(1)} fusion(bf16[1,128,32,128]{3,2,1,0:T(8,128)(2,1)} %param.16, bf16[1,128,32,128]{3,2,1,0:T(8,128)(2,1)} %param.15), kind=kLoop, calls=%fused_computation | loop fusion | flops 2093056 | bytes 2113536 | tf_op jit(solution)/shard_map/reduce_sum | solution.py:255
  9.8 0.2 copy.95
  10.0 0.3 reshape.214
  10.4 0.5 copy-done.8
  10.9 1.1 dynamic-slice_bitcast_fusion.2
  12.0 2.5 %collective-permute-start.2 = (bf16[2096,128]{1,0:T(8,128)(2,1)S(1)}, bf16[2096,128]{1,0:T(8,128)(2,1)S(1)}, u32[]{:S(2)}, u32[]{:S(2)}) collective-permute-start(bf16[2096,128]{1,0:T(8,128)(2,1)S(1)} %pad_maximum_fusion.3), channel_id=1, source_target_pairs={{0,3},{1,0},{2,1},{3,2},{4,7},{5,4},{6,5},{7,6},{8,11},{9,8},{10,9... | collective-permute-start | bytes 1609736 | tf_op jit(solution)/shard_map/ppermute | solution.py:52
  14.6 0.9 pad_maximum_fusion.2
  15.4 0.5 collective-permute-start.1
  16.3 0.5 broadcast.226
  16.9 0.7 reduce.4
  17.7 0.4 select_reduce_fusion.2
  18.1 0.1 copy.88
  18.3 0.2 convert_reduce_fusion
  18.5 0.2 select_reduce_fusion
  18.8 0.8 pad_maximum_fusion.1
  20.0 0.9 collective-permute-start.8
  21.0 1.7 %collective-permute-start.7 = (bf16[288,128]{1,0:T(8,128)(2,1)S(1)}, bf16[288,128]{1,0:T(8,128)(2,1)S(1)}, u32[]{:S(2)}, u32[]{:S(2)}) collective-permute-start(bf16[288,128]{1,0:T(8,128)(2,1)S(1)} %bitcast.167), channel_id=1, source_target_pairs={{0,2},{1,3},{2,0},{3,1},{4,6},{5,7},{6,4},{7,5},{8,10},{9,11},{10,... | collective-permute-start | bytes 221192 | tf_op jit(solution)/shard_map/ppermute | solution.py:52
  22.7 0.8 collective-permute-start.6
  23.4 4.7 %collective-permute-done.8 = bf16[288,128]{1,0:T(8,128)(2,1)S(1)} collective-permute-done((bf16[288,128]{1,0:T(8,128)(2,1)S(1)}, bf16[288,128]{1,0:T(8,128)(2,1)S(1)}, u32[]{:S(2)}, u32[]{:S(2)}) %collective-permute-start.8) | collective-permute-done | bytes 73760 | tf_op jit(solution)/shard_map/ppermute | solution.py:52
  28.2 1.1 collective-permute-start
  29.3 0.8 collective-permute-start.9
  30.1 4.8 %collective-permute-done.9 = bf16[1152,128]{1,0:T(8,128)(2,1)S(1)} collective-permute-done((bf16[1152,128]{1,0:T(8,128)(2,1)S(1)}, bf16[1152,128]{1,0:T(8,128)(2,1)S(1)}, u32[]{:S(2)}, u32[]{:S(2)}) %collective-permute-start.9) | collective-permute-done | bytes 294944 | tf_op jit(solution)/shard_map/ppermute | solution.py:52
  35.0 1.4 collective-permute-start.12
  36.3 1.5 %collective-permute-start.11 = (bf16[2304,128]{1,0:T(8,128)(2,1)S(1)}, bf16[2304,128]{1,0:T(8,128)(2,1)S(1)}, u32[]{:S(2)}, u32[]{:S(2)}) collective-permute-start(bf16[2304,128]{1,0:T(8,128)(2,1)S(1)} %constant_dynamic-update-slice_fusion.kv_ref), channel_id=1, source_target_pairs={{0,24},{1,25},{2,26},{3,27},{4,28},{5,29},{6,30},{7,31},{8,0},{9,1... | collective-permute-start | bytes 1769480 | tf_op jit(solution)/shard_map/ppermute | solution.py:52
  37.8 0.8 copy-done.2
  38.7 1.6 %collective-permute-start.10 = (bf16[2304,128]{1,0:T(8,128)(2,1)S(1)}, bf16[2304,128]{1,0:T(8,128)(2,1)S(1)}, u32[]{:S(2)}, u32[]{:S(2)}) collective-permute-start(bf16[2304,128]{1,0:T(8,128)(2,1)S(1)} %constant_dynamic-update-slice_fusion.kv_ref), channel_id=1, source_target_pairs={{0,16},{1,17},{2,18},{3,19},{4,20},{5,21},{6,22},{7,23},{8,24},{9,... | collective-permute-start | bytes 1769480 | tf_op jit(solution)/shard_map/ppermute | solution.py:52
  40.2 0.8 copy-done.5
  41.1 1.0 copy-done.3
  42.1 1.0 copy-done.6
  43.2 12.6 %shard_map.137 = (f32[1024,512]{1,0:T(8,128)S(1)}, f32[2304,128]{1,0:T(8,128)S(1)}) custom-call(s32[20]{0:T(128)S(1)} %get-tuple-element.91.slot_ref, s32[20]{0:T(128)S(1)} %get-tuple-element.87.pos_ref, s32[8]{0:T(128)S(1)} %reshape_squeeze.13.qpos_ref, bf16[2096,128]{1,0:T(8,128)(2,1)S(1)} %pad_maximum_fusion.c0_ref, ...), custom_call_target="tpu_custom_call" | custom-call | flops 12000000000 | bytes 8000000 | tf_op jit(solution)/shard_map/pallas_call | solution.py:191
  55.8 12.1 %shard_map.138 = (f32[1024,512]{1,0:T(8,128)S(1)}, bf16[2304,128]{1,0:T(8,128)(2,1)S(1)}) custom-call(s32[20]{0:T(128)S(1)} %get-tuple-element.93.slot_ref, s32[20]{0:T(128)S(1)} %get-tuple-element.89.pos_ref, s32[8]{0:T(128)S(1)} %reshape_squeeze.13.qpos_ref, bf16[2096,128]{1,0:T(8,128)(2,1)S(1)} %pad_maximum_fusion.c0_ref, ...), custom_call_target="tpu_custom_call" | custom-call | flops 12000000000 | bytes 8000000 | tf_op jit(solution)/shard_map/pallas_call | solution.py:191
  67.9 12.6 %shard_map.139 = (f32[1024,512]{1,0:T(8,128)S(1)}, bf16[2304,128]{1,0:T(8,128)(2,1)S(1)}) custom-call(s32[20]{0:T(128)S(1)} %get-tuple-element.92.slot_ref, s32[20]{0:T(128)S(1)} %get-tuple-element.88.pos_ref, s32[8]{0:T(128)S(1)} %reshape_squeeze.13.qpos_ref, bf16[2096,128]{1,0:T(8,128)(2,1)S(1)} %pad_maximum_fusion.c0_ref, ...), custom_call_target="tpu_custom_call" | custom-call | flops 12000000000 | bytes 8000000 | tf_op jit(solution)/shard_map/pallas_call | solution.py:191
  80.6 0.8 copy-done
  81.4 12.5 %shard_map.140 = (bf16[4096,128]{1,0:T(8,128)(2,1)S(1)}, bf16[2304,128]{1,0:T(8,128)(2,1)S(1)}) custom-call(s32[20]{0:T(128)S(1)} %get-tuple-element.94.slot_ref, s32[20]{0:T(128)S(1)} %get-tuple-element.90.pos_ref, s32[8]{0:T(128)S(1)} %reshape_squeeze.13.qpos_ref, bf16[2096,128]{1,0:T(8,128)(2,1)S(1)} %pad_maximum_fusion.c0_ref, ...), custom_call_target="tpu_custom_call" | custom-call | flops 12000000000 | bytes 8000000 | tf_op jit(solution)/shard_map/pallas_call | solution.py:191
  93.9 0.8 copy-done.1
  94.7 0.9 fusion.20
  95.7 2.5 %collective-permute-start.13 = (bf16[1024,128]{1,0:T(8,128)(2,1)}, bf16[1024,128]{1,0:T(8,128)(2,1)S(1)}, u32[]{:S(2)}, u32[]{:S(2)}) collective-permute-start(bf16[1024,128]{1,0:T(8,128)(2,1)} %get-tuple-element.50), channel_id=1, source_target_pairs={{0,3},{1,0},{2,1},{3,2},{4,7},{5,4},{6,5},{7,6},{8,11},{9,8},{10,9... | collective-permute-start | bytes 786440 | tf_op jit(solution)/shard_map/ppermute | solution.py:52
  98.2 1.2 collective-permute-start.14
  99.4 1.3 collective-permute-start.18
  100.7 2.7 %collective-permute-start.16 = (bf16[2304,128]{1,0:T(8,128)(2,1)S(1)}, bf16[2304,128]{1,0:T(8,128)(2,1)S(1)}, u32[]{:S(2)}, u32[]{:S(2)}) collective-permute-start(bf16[2304,128]{1,0:T(8,128)(2,1)S(1)} %get-tuple-element.18), channel_id=1, source_target_pairs={{0,24},{1,25},{2,26},{3,27},{4,28},{5,29},{6,30},{7,31},{8,0},{9,1... | collective-permute-start | bytes 1769480 | tf_op jit(solution)/shard_map/ppermute | solution.py:52
  103.4 1.2 collective-permute-done.13
  104.7 0.4 collective-permute-done.14
  105.2 8.0 %collective-permute-done.15 = bf16[1024,128]{1,0:T(8,128)(2,1)S(1)} collective-permute-done((bf16[1024,128]{1,0:T(8,128)(2,1)}, bf16[1024,128]{1,0:T(8,128)(2,1)S(1)}, u32[]{:S(2)}, u32[]{:S(2)}) %collective-permute-start.15) | collective-permute-done | bytes 262176 | tf_op jit(solution)/shard_map/ppermute | solution.py:52
  113.3 6.0 %collective-permute-done.17 = bf16[2304,128]{1,0:T(8,128)(2,1)S(1)} collective-permute-done((bf16[2304,128]{1,0:T(8,128)(2,1)}, bf16[2304,128]{1,0:T(8,128)(2,1)S(1)}, u32[]{:S(2)}, u32[]{:S(2)}) %collective-permute-start.17) | collective-permute-done | bytes 589856 | tf_op jit(solution)/shard_map/ppermute | solution.py:52
  119.3 0.7 collective-permute-done.16
  120.0 0.2 convert_add_fusion
  120.3 1.8 %collective-permute-start.19 = (bf16[1152,128]{1,0:T(8,128)(2,1)S(1)}, bf16[1152,128]{1,0:T(8,128)(2,1)S(1)}, u32[]{:S(2)}, u32[]{:S(2)}) collective-permute-start(bf16[1152,128]{1,0:T(8,128)(2,1)S(1)} %slice.161), channel_id=1, source_target_pairs={{0,4},{1,5},{2,6},{3,7},{4,0},{5,1},{6,2},{7,3},{8,12},{9,13},{10,... | collective-permute-start | bytes 884744 | tf_op jit(solution)/shard_map/ppermute | solution.py:52
  122.2 1.2 copy_bitcast_fusion
  123.3 2.9 %collective-permute-done.19 = bf16[1152,128]{1,0:T(8,128)(2,1)S(1)} collective-permute-done((bf16[1152,128]{1,0:T(8,128)(2,1)S(1)}, bf16[1152,128]{1,0:T(8,128)(2,1)S(1)}, u32[]{:S(2)}, u32[]{:S(2)}) %collective-permute-start.19) | collective-permute-done | bytes 294944 | tf_op jit(solution)/shard_map/ppermute | solution.py:52
  126.4 0.3 collective-permute-start.20
  126.7 2.4 %collective-permute-start.21 = (bf16[2,144,128]{2,1,0:T(8,128)(2,1)S(1)}, bf16[2,144,128]{2,1,0:T(8,128)(2,1)S(1)}, u32[]{:S(2)}, u32[]{:S(2)}) collective-permute-start(bf16[2,144,128]{2,1,0:T(8,128)(2,1)S(1)} %bitcast.165), channel_id=1, source_target_pairs={{0,2},{1,3},{2,0},{3,1},{4,6},{5,7},{6,4},{7,5},{8,10},{9,11},{10,... | collective-permute-start | bytes 221192 | tf_op jit(solution)/shard_map/ppermute | solution.py:52
  129.0 0.9 collective-permute-done.20
  129.9 1.4 collective-permute-done.21
  131.4 2.1 %collective-permute-done.22 = bf16[2,144,128]{2,1,0:T(8,128)(2,1)S(1)} collective-permute-done((bf16[2,144,128]{2,1,0:T(8,128)(2,1)S(1)}, bf16[2,144,128]{2,1,0:T(8,128)(2,1)S(1)}, u32[]{:S(2)}, u32[]{:S(2)}) %collective-permute-start.22) | collective-permute-done | bytes 73760 | tf_op jit(solution)/shard_map/ppermute | solution.py:52
  133.5 11.3 %collective-permute-start.23 = (bf16[2,16,128]{2,1,0:T(8,128)(2,1)S(1)}, bf16[2,16,128]{2,1,0:T(8,128)(2,1)S(1)}, u32[]{:S(2)}, u32[]{:S(2)}) collective-permute-start(bf16[2,16,128]{2,1,0:T(8,128)(2,1)S(1)} %get-tuple-element.59), channel_id=1, source_target_pairs={{0,32},{1,33},{2,34},{3,35},{4,36},{5,37},{6,38},{7,39},{8,40},{9,... | collective-permute-start | bytes 24584 | tf_op jit(solution)/shard_map/ppermute | solution.py:52
  144.8 0.5 collective-permute-start.25
  145.3 0.8 copy.106
  146.1 0.8 copy.107
  146.9 1.9 %collective-permute-done.24 = bf16[2,16,128]{2,1,0:T(8,128)(2,1)S(1)} collective-permute-done((bf16[2,16,128]{2,1,0:T(8,128)(2,1)S(1)}, bf16[2,16,128]{2,1,0:T(8,128)(2,1)S(1)}, u32[]{:S(2)}, u32[]{:S(2)}) %collective-permute-start.24) | collective-permute-done | bytes 8224 | tf_op jit(solution)/shard_map/ppermute | solution.py:52
  148.8 0.6 collective-permute-done.25
  149.4 0.6 slice_bitcast_fusion
  (103 shorter events, 1.7 us)
Async XLA Ops:
  1.3 18.6 %collective-permute-start.3 = (bf16[2,16,128]{2,1,0:T(8,128)(2,1)S(1)}, bf16[2,16,128]{2,1,0:T(8,128)(2,1)S(1)}, u32[]{:S(2)}, u32[]{:S(2)}) collective-permute-start(bf16[2,16,128]{2,1,0:T(8,128)(2,1)S(1)} %get-tuple-element.86), channel_id=1, source_target_pairs={{0,32},{1,33},{2,34},{3,35},{4,36},{5,37},{6,38},{7,39},{8,40},{9,... | collective-permute-start | bytes 24584 | tf_op jit(solution)/shard_map/ppermute | solution.py:52
  6.3 13.6 %collective-permute-start.4 = (bf16[2,16,128]{2,1,0:T(8,128)(2,1)S(1)}, bf16[2,16,128]{2,1,0:T(8,128)(2,1)S(1)}, u32[]{:S(2)}, u32[]{:S(2)}) collective-permute-start(bf16[2,16,128]{2,1,0:T(8,128)(2,1)S(1)} %get-tuple-element.86), channel_id=1, source_target_pairs={{0,64},{1,65},{2,66},{3,67},{4,68},{5,69},{6,70},{7,71},{8,72},{9,... | collective-permute-start | bytes 24584 | tf_op jit(solution)/shard_map/ppermute | solution.py:52
  6.3 13.6 %collective-permute-start.5 = (bf16[2,16,128]{2,1,0:T(8,128)(2,1)S(1)}, bf16[2,16,128]{2,1,0:T(8,128)(2,1)S(1)}, u32[]{:S(2)}, u32[]{:S(2)}) collective-permute-start(bf16[2,16,128]{2,1,0:T(8,128)(2,1)S(1)} %get-tuple-element.86), channel_id=1, source_target_pairs={{0,96},{1,97},{2,98},{3,99},{4,100},{5,101},{6,102},{7,103},{8,104... | collective-permute-start | bytes 24584 | tf_op jit(solution)/shard_map/ppermute | solution.py:52
  6.8 3.0 %copy-start.13 = (s32[1,4096]{1,0:T(1,128)S(1)}, s32[1,4096]{1,0:T(1,128)}, u32[]{:S(2)}) copy-start(s32[1,4096]{1,0:T(1,128)} %param.18) | copy-start | bytes 49156
  6.8 3.0 %copy-start.14 = (f32[1,128,32]{1,2,0:T(8,128)S(1)}, f32[1,128,32]{1,2,0:T(8,128)}, u32[]{:S(2)}) copy-start(f32[1,128,32]{1,2,0:T(8,128)} %param.17) | copy-start | bytes 49156
  7.4 3.0 %copy-start.9 = (bf16[1,128,32,128]{3,2,1,0:T(8,128)(2,1)S(1)}, bf16[1,128,32,128]{3,2,1,0:T(8,128)(2,1)}, u32[]{:S(2)}) copy-start(bf16[1,128,32,128]{3,2,1,0:T(8,128)(2,1)} %param.10) | copy-start | bytes 3145732
  9.7 1.2 copy-start.8
  12.0 4.1 %copy-start.11 = (bf16[1,128,4,128]{3,2,1,0:T(4,128)(2,1)S(1)}, bf16[1,128,4,128]{3,2,1,0:T(4,128)(2,1)}, u32[]{:S(2)}) copy-start(bf16[1,128,4,128]{3,2,1,0:T(4,128)(2,1)} %param.11) | copy-start | bytes 393220
  12.0 4.1 %copy-start.12 = (bf16[1,128,4,128]{3,2,1,0:T(4,128)(2,1)S(1)}, bf16[1,128,4,128]{3,2,1,0:T(4,128)(2,1)}, u32[]{:S(2)}) copy-start(bf16[1,128,4,128]{3,2,1,0:T(4,128)(2,1)} %param.12) | copy-start | bytes 393220
  12.0 25.8 %collective-permute-start.2 = (bf16[2096,128]{1,0:T(8,128)(2,1)S(1)}, bf16[2096,128]{1,0:T(8,128)(2,1)S(1)}, u32[]{:S(2)}, u32[]{:S(2)}) collective-permute-start(bf16[2096,128]{1,0:T(8,128)(2,1)S(1)} %pad_maximum_fusion.3), channel_id=1, source_target_pairs={{0,3},{1,0},{2,1},{3,2},{4,7},{5,4},{6,5},{7,6},{8,11},{9,8},{10,9... | collective-permute-start | bytes 1609736 | tf_op jit(solution)/shard_map/ppermute | solution.py:52
  14.6 4.2 %copy-start.10 = (bf16[1024,128]{1,0:T(8,128)(2,1)S(1)}, bf16[1024,128]{1,0:T(8,128)(2,1)}, u32[]{:S(2)}) copy-start(bf16[1024,128]{1,0:T(8,128)(2,1)} %get-tuple-element.104) | copy-start | bytes 786436
  15.4 24.8 %collective-permute-start.1 = (bf16[2096,128]{1,0:T(8,128)(2,1)}, bf16[2096,128]{1,0:T(8,128)(2,1)S(1)}, u32[]{:S(2)}, u32[]{:S(2)}) collective-permute-start(bf16[2096,128]{1,0:T(8,128)(2,1)} %pad_maximum_fusion.2), channel_id=1, source_target_pairs={{0,2},{1,3},{2,0},{3,1},{4,6},{5,7},{6,4},{7,5},{8,10},{9,11},{10,... | collective-permute-start | bytes 1609736 | tf_op jit(solution)/shard_map/ppermute | solution.py:52
  20.0 8.1 %collective-permute-start.8 = (bf16[288,128]{1,0:T(8,128)(2,1)S(1)}, bf16[288,128]{1,0:T(8,128)(2,1)S(1)}, u32[]{:S(2)}, u32[]{:S(2)}) collective-permute-start(bf16[288,128]{1,0:T(8,128)(2,1)S(1)} %bitcast.168), channel_id=1, source_target_pairs={{0,3},{1,0},{2,1},{3,2},{4,7},{5,4},{6,5},{7,6},{8,11},{9,8},{10,9... | collective-permute-start | bytes 221192 | tf_op jit(solution)/shard_map/ppermute | solution.py:52
  21.0 8.3 %collective-permute-start.7 = (bf16[288,128]{1,0:T(8,128)(2,1)S(1)}, bf16[288,128]{1,0:T(8,128)(2,1)S(1)}, u32[]{:S(2)}, u32[]{:S(2)}) collective-permute-start(bf16[288,128]{1,0:T(8,128)(2,1)S(1)} %bitcast.167), channel_id=1, source_target_pairs={{0,2},{1,3},{2,0},{3,1},{4,6},{5,7},{6,4},{7,5},{8,10},{9,11},{10,... | collective-permute-start | bytes 221192 | tf_op jit(solution)/shard_map/ppermute | solution.py:52
  22.7 6.6 %collective-permute-start.6 = (bf16[288,128]{1,0:T(8,128)(2,1)S(1)}, bf16[288,128]{1,0:T(8,128)(2,1)S(1)}, u32[]{:S(2)}, u32[]{:S(2)}) collective-permute-start(bf16[288,128]{1,0:T(8,128)(2,1)S(1)} %bitcast.169), channel_id=1, source_target_pairs={{0,1},{1,2},{2,3},{3,0},{4,5},{5,6},{6,7},{7,4},{8,9},{9,10},{10,1... | collective-permute-start | bytes 221192 | tf_op jit(solution)/shard_map/ppermute | solution.py:52
  28.2 12.9 %collective-permute-start = (bf16[2096,128]{1,0:T(8,128)(2,1)}, bf16[2096,128]{1,0:T(8,128)(2,1)S(1)}, u32[]{:S(2)}, u32[]{:S(2)}) collective-permute-start(bf16[2096,128]{1,0:T(8,128)(2,1)} %pad_maximum_fusion.1), channel_id=1, source_target_pairs={{0,1},{1,2},{2,3},{3,0},{4,5},{5,6},{6,7},{7,4},{8,9},{9,10},{10,1... | collective-permute-start | bytes 1609736 | tf_op jit(solution)/shard_map/ppermute | solution.py:52
  29.3 5.7 %collective-permute-start.9 = (bf16[1152,128]{1,0:T(8,128)(2,1)S(1)}, bf16[1152,128]{1,0:T(8,128)(2,1)S(1)}, u32[]{:S(2)}, u32[]{:S(2)}) collective-permute-start(bf16[1152,128]{1,0:T(8,128)(2,1)S(1)} %pad_maximum_fusion.4), channel_id=1, source_target_pairs={{0,4},{1,5},{2,6},{3,7},{4,0},{5,1},{6,2},{7,3},{8,12},{9,13},{10,... | collective-permute-start | bytes 884744 | tf_op jit(solution)/shard_map/ppermute | solution.py:52
  35.0 20.8 %collective-permute-start.12 = (bf16[2304,128]{1,0:T(8,128)(2,1)S(1)}, bf16[2304,128]{1,0:T(8,128)(2,1)S(1)}, u32[]{:S(2)}, u32[]{:S(2)}) collective-permute-start(bf16[2304,128]{1,0:T(8,128)(2,1)S(1)} %constant_dynamic-update-slice_fusion.kv_ref), channel_id=1, source_target_pairs={{0,8},{1,9},{2,10},{3,11},{4,12},{5,13},{6,14},{7,15},{8,16},{9,17... | collective-permute-start | bytes 1769480 | tf_op jit(solution)/shard_map/ppermute | solution.py:52
  36.3 31.6 %collective-permute-start.11 = (bf16[2304,128]{1,0:T(8,128)(2,1)S(1)}, bf16[2304,128]{1,0:T(8,128)(2,1)S(1)}, u32[]{:S(2)}, u32[]{:S(2)}) collective-permute-start(bf16[2304,128]{1,0:T(8,128)(2,1)S(1)} %constant_dynamic-update-slice_fusion.kv_ref), channel_id=1, source_target_pairs={{0,24},{1,25},{2,26},{3,27},{4,28},{5,29},{6,30},{7,31},{8,0},{9,1... | collective-permute-start | bytes 1769480 | tf_op jit(solution)/shard_map/ppermute | solution.py:52
  37.8 0.8 copy-start.2
  38.7 42.7 %collective-permute-start.10 = (bf16[2304,128]{1,0:T(8,128)(2,1)S(1)}, bf16[2304,128]{1,0:T(8,128)(2,1)S(1)}, u32[]{:S(2)}, u32[]{:S(2)}) collective-permute-start(bf16[2304,128]{1,0:T(8,128)(2,1)S(1)} %constant_dynamic-update-slice_fusion.kv_ref), channel_id=1, source_target_pairs={{0,16},{1,17},{2,18},{3,19},{4,20},{5,21},{6,22},{7,23},{8,24},{9,... | collective-permute-start | bytes 1769480 | tf_op jit(solution)/shard_map/ppermute | solution.py:52
  40.2 0.8 copy-start.5
  41.1 1.0 copy-start.3
  42.1 1.0 copy-start.6
  43.2 12.6 %copy-start.4 = (bf16[2096,128]{1,0:T(8,128)(2,1)S(1)}, bf16[2096,128]{1,0:T(8,128)(2,1)}, u32[]{:S(2)}) copy-start(bf16[2096,128]{1,0:T(8,128)(2,1)} %copy-done.2) | copy-start | bytes 1609732
  43.2 12.6 %copy-start.7 = (bf16[2096,128]{1,0:T(8,128)(2,1)S(1)}, bf16[2096,128]{1,0:T(8,128)(2,1)}, u32[]{:S(2)}) copy-start(bf16[2096,128]{1,0:T(8,128)(2,1)} %copy-done.5) | copy-start | bytes 1609732
  80.6 0.8 copy-start
  93.9 0.8 copy-start.1
  95.7 9.0 %collective-permute-start.13 = (bf16[1024,128]{1,0:T(8,128)(2,1)}, bf16[1024,128]{1,0:T(8,128)(2,1)S(1)}, u32[]{:S(2)}, u32[]{:S(2)}) collective-permute-start(bf16[1024,128]{1,0:T(8,128)(2,1)} %get-tuple-element.50), channel_id=1, source_target_pairs={{0,3},{1,0},{2,1},{3,2},{4,7},{5,4},{6,5},{7,6},{8,11},{9,8},{10,9... | collective-permute-start | bytes 786440 | tf_op jit(solution)/shard_map/ppermute | solution.py:52
  98.2 6.9 %collective-permute-start.14 = (bf16[1024,128]{1,0:T(8,128)(2,1)}, bf16[1024,128]{1,0:T(8,128)(2,1)S(1)}, u32[]{:S(2)}, u32[]{:S(2)}) collective-permute-start(bf16[1024,128]{1,0:T(8,128)(2,1)} %get-tuple-element.49), channel_id=1, source_target_pairs={{0,2},{1,3},{2,0},{3,1},{4,6},{5,7},{6,4},{7,5},{8,10},{9,11},{10,... | collective-permute-start | bytes 786440 | tf_op jit(solution)/shard_map/ppermute | solution.py:52
  99.4 13.9 %collective-permute-start.18 = (bf16[2304,128]{1,0:T(8,128)(2,1)}, bf16[2304,128]{1,0:T(8,128)(2,1)S(1)}, u32[]{:S(2)}, u32[]{:S(2)}) collective-permute-start(bf16[2304,128]{1,0:T(8,128)(2,1)} %copy-done.1), channel_id=1, source_target_pairs={{0,16},{1,17},{2,18},{3,19},{4,20},{5,21},{6,22},{7,23},{8,24},{9,... | collective-permute-start | bytes 1769480 | tf_op jit(solution)/shard_map/ppermute | solution.py:52
  100.7 18.6 %collective-permute-start.17 = (bf16[2304,128]{1,0:T(8,128)(2,1)}, bf16[2304,128]{1,0:T(8,128)(2,1)S(1)}, u32[]{:S(2)}, u32[]{:S(2)}) collective-permute-start(bf16[2304,128]{1,0:T(8,128)(2,1)} %copy-done), channel_id=1, source_target_pairs={{0,8},{1,9},{2,10},{3,11},{4,12},{5,13},{6,14},{7,15},{8,16},{9,17... | collective-permute-start | bytes 1769480 | tf_op jit(solution)/shard_map/ppermute | solution.py:52
  100.7 19.3 %collective-permute-start.16 = (bf16[2304,128]{1,0:T(8,128)(2,1)S(1)}, bf16[2304,128]{1,0:T(8,128)(2,1)S(1)}, u32[]{:S(2)}, u32[]{:S(2)}) collective-permute-start(bf16[2304,128]{1,0:T(8,128)(2,1)S(1)} %get-tuple-element.18), channel_id=1, source_target_pairs={{0,24},{1,25},{2,26},{3,27},{4,28},{5,29},{6,30},{7,31},{8,0},{9,1... | collective-permute-start | bytes 1769480 | tf_op jit(solution)/shard_map/ppermute | solution.py:52
  104.7 8.5 %collective-permute-start.15 = (bf16[1024,128]{1,0:T(8,128)(2,1)}, bf16[1024,128]{1,0:T(8,128)(2,1)S(1)}, u32[]{:S(2)}, u32[]{:S(2)}) collective-permute-start(bf16[1024,128]{1,0:T(8,128)(2,1)} %get-tuple-element.48), channel_id=1, source_target_pairs={{0,1},{1,2},{2,3},{3,0},{4,5},{5,6},{6,7},{7,4},{8,9},{9,10},{10,1... | collective-permute-start | bytes 786440 | tf_op jit(solution)/shard_map/ppermute | solution.py:52
  120.3 5.9 %collective-permute-start.19 = (bf16[1152,128]{1,0:T(8,128)(2,1)S(1)}, bf16[1152,128]{1,0:T(8,128)(2,1)S(1)}, u32[]{:S(2)}, u32[]{:S(2)}) collective-permute-start(bf16[1152,128]{1,0:T(8,128)(2,1)S(1)} %slice.161), channel_id=1, source_target_pairs={{0,4},{1,5},{2,6},{3,7},{4,0},{5,1},{6,2},{7,3},{8,12},{9,13},{10,... | collective-permute-start | bytes 884744 | tf_op jit(solution)/shard_map/ppermute | solution.py:52
  126.4 3.6 %collective-permute-start.20 = (bf16[2,144,128]{2,1,0:T(8,128)(2,1)S(1)}, bf16[2,144,128]{2,1,0:T(8,128)(2,1)S(1)}, u32[]{:S(2)}, u32[]{:S(2)}) collective-permute-start(bf16[2,144,128]{2,1,0:T(8,128)(2,1)S(1)} %bitcast.166), channel_id=1, source_target_pairs={{0,3},{1,0},{2,1},{3,2},{4,7},{5,4},{6,5},{7,6},{8,11},{9,8},{10,9... | collective-permute-start | bytes 221192 | tf_op jit(solution)/shard_map/ppermute | solution.py:52
  126.7 4.7 %collective-permute-start.21 = (bf16[2,144,128]{2,1,0:T(8,128)(2,1)S(1)}, bf16[2,144,128]{2,1,0:T(8,128)(2,1)S(1)}, u32[]{:S(2)}, u32[]{:S(2)}) collective-permute-start(bf16[2,144,128]{2,1,0:T(8,128)(2,1)S(1)} %bitcast.165), channel_id=1, source_target_pairs={{0,2},{1,3},{2,0},{3,1},{4,6},{5,7},{6,4},{7,5},{8,10},{9,11},{10,... | collective-permute-start | bytes 221192 | tf_op jit(solution)/shard_map/ppermute | solution.py:52
  129.0 4.4 %collective-permute-start.22 = (bf16[2,144,128]{2,1,0:T(8,128)(2,1)S(1)}, bf16[2,144,128]{2,1,0:T(8,128)(2,1)S(1)}, u32[]{:S(2)}, u32[]{:S(2)}) collective-permute-start(bf16[2,144,128]{2,1,0:T(8,128)(2,1)S(1)} %bitcast.164), channel_id=1, source_target_pairs={{0,1},{1,2},{2,3},{3,0},{4,5},{5,6},{6,7},{7,4},{8,9},{9,10},{10,1... | collective-permute-start | bytes 221192 | tf_op jit(solution)/shard_map/ppermute | solution.py:52
  133.5 13.3 %collective-permute-start.23 = (bf16[2,16,128]{2,1,0:T(8,128)(2,1)S(1)}, bf16[2,16,128]{2,1,0:T(8,128)(2,1)S(1)}, u32[]{:S(2)}, u32[]{:S(2)}) collective-permute-start(bf16[2,16,128]{2,1,0:T(8,128)(2,1)S(1)} %get-tuple-element.59), channel_id=1, source_target_pairs={{0,32},{1,33},{2,34},{3,35},{4,36},{5,37},{6,38},{7,39},{8,40},{9,... | collective-permute-start | bytes 24584 | tf_op jit(solution)/shard_map/ppermute | solution.py:52
  144.8 4.0 %collective-permute-start.24 = (bf16[2,16,128]{2,1,0:T(8,128)(2,1)S(1)}, bf16[2,16,128]{2,1,0:T(8,128)(2,1)S(1)}, u32[]{:S(2)}, u32[]{:S(2)}) collective-permute-start(bf16[2,16,128]{2,1,0:T(8,128)(2,1)S(1)} %get-tuple-element.60), channel_id=1, source_target_pairs={{0,64},{1,65},{2,66},{3,67},{4,68},{5,69},{6,70},{7,71},{8,72},{9,... | collective-permute-start | bytes 24584 | tf_op jit(solution)/shard_map/ppermute | solution.py:52
  144.8 4.6 %collective-permute-start.25 = (bf16[2,16,128]{2,1,0:T(8,128)(2,1)S(1)}, bf16[2,16,128]{2,1,0:T(8,128)(2,1)S(1)}, u32[]{:S(2)}, u32[]{:S(2)}) collective-permute-start(bf16[2,16,128]{2,1,0:T(8,128)(2,1)S(1)} %get-tuple-element.61), channel_id=1, source_target_pairs={{0,96},{1,97},{2,98},{3,99},{4,100},{5,101},{6,102},{7,103},{8,104... | collective-permute-start | bytes 24584 | tf_op jit(solution)/shard_map/ppermute | solution.py:52

commit v2 on v1

v2 whole, which is shorter than its diff:
```python
import functools

import jax
import jax.numpy as jnp
from jax import lax
from jax.experimental import pallas as pl
from jax.experimental.pallas import tpu as pltpu
from jax.sharding import PartitionSpec as P

F32 = jnp.float32
BF16 = jnp.bfloat16
AXES = ("resp", "ctx")
LOG2E = 1.4426950408889634
RUN = 64
NT = (((1,), (1,)), ((), ()))
NN = (((1,), (0,)), ((), ()))
TN = (((0,), (0,)), ((), ()))


def coords(r, c):
    return c // 8, (c // 4) % 2, c % 4, r % 2


def device_pairs(move):
    pairs = []
    for r in range(4):
        for c in range(32):
            x, z, y, _ = coords(r, c)
            r2, x2, z2, y2 = move(r, x, z, y)
            pairs.append((r * 32 + c, (r2 % 4) * 32 + (x2 % 4) * 8 + (z2 % 2) * 4 + y2 % 4))
    return pairs


def along_heads(s):
    return device_pairs(lambda r, x, z, y: (r, x, z, y + s) if r % 2 == 0 else (r, x + s, z, y))


def along_blocks(s):
    return device_pairs(lambda r, x, z, y: (r, x + s, z, y) if r % 2 == 0 else (r, x, z, y + s))


def along_z():
    return device_pairs(lambda r, x, z, y: (r, x, z + 1, y))


def along_both(s):
    return device_pairs(lambda r, x, z, y: (r, x + s, z + 1, y) if r % 2 == 0 else (r, x, z + 1, y + s))


def along_resp(s):
    return device_pairs(lambda r, x, z, y: (r + s, x, z, y))


def across_cores():
    return device_pairs(lambda r, x, z, y: (r ^ 1, x, z, y))


def across_z_hi():
    return device_pairs(lambda r, x, z, y: (r ^ 2, x, z, y))


def send(value, pairs):
    return lax.ppermute(value, AXES, pairs)


def dot(a, b, dims):
    return lax.dot_general(a, b, dims, preferred_element_type=F32)


def grads_kernel(shift, members, first, last, scale, received, at_ref, stats_ref, c0_ref, c1_ref, c2_ref, c3_ref, *rest):
    parts = members // 4
    rest = list(rest)
    kv_refs = [rest.pop(0) for _ in range(parts)]
    dq_in = None if first else rest.pop(0)
    held = [rest.pop(0) for _ in range(received)]
    dq_out = rest.pop(0)
    outs = [rest.pop(0) for _ in range(parts)]
    chunk, keys, values, dkeys, dvalues, stage, meta_ref = rest[:7]
    dq = rest[7] if last else dq_out
    core, head, block, z = [at_ref[64 + i] for i in range(4)]

    def runs_of(from_b, from_h, from_z):
        c = jnp.where(core == 0, from_b * 8 + from_h, from_h * 8 + from_b) + from_z * 4
        one, two = at_ref[2 * c], at_ref[2 * c + 1]
        return jnp.minimum(one, two), jnp.where(one > two, 1, 0)

    if members == 8:
        places_in = [(zz * 1152, zz, e) for zz in range(2) for e in range(4)]
    else:
        places_in = [(0, 0 if last else 1, e) for e in range(4)]
    found = [runs_of((block - shift) & 3, (head - e) & 3, (z + zz) & 1) for _, zz, e in places_in]
    for j, (early_j, swap_j) in enumerate(found):
        rank = 0
        for i, (early_i, _) in enumerate(found):
            if i != j:
                rank = rank + jnp.where(early_i < early_j, 1, 0)
        start = places_in[j][0] + 288 * places_in[j][2]
        meta_ref[rank] = early_j
        meta_ref[8 + rank] = start + RUN * swap_j
        meta_ref[16 + rank] = start + RUN * (1 - swap_j)
    for e in range(4):
        meta_ref[24 + e], meta_ref[28 + e] = runs_of(block, (head - e) & 3, z)
    rows = 512
    prompt = 16 * members
    for i, ref in enumerate((c0_ref, c1_ref, c2_ref, c3_ref)):
        chunk[pl.ds(i * 2048, 2048), :] = ref[...]
    if first:
        dq[...] = jnp.zeros_like(dq)
    else:
        dq[...] = dq_in[...]
    dkeys[...] = jnp.zeros_like(dkeys)
    dvalues[...] = jnp.zeros_like(dvalues)

    def places(u):
        for late in range(2):
            at = meta_ref[8 + 8 * late + u]
            yield at, pl.ds(prompt + (late * members + u) * RUN, RUN)

    for part in range(parts):
        stage[pl.ds(part * 1152, 1152), :] = kv_refs[part][...]
    for e in range(members):
        to = pl.ds(16 * e, 16)
        keys[to, :] = stage[pl.ds(288 * e + 256, 16), :]
        values[to, :] = stage[pl.ds(288 * e + 272, 16), :]
    for u in range(members):
        for at, to in places(u):
            keys[to, :] = stage[pl.ds(pl.multiple_of(at, 16), RUN), :]
            values[to, :] = stage[pl.ds(pl.multiple_of(at + 128, 16), RUN), :]

    slope = lax.broadcasted_iota(jnp.int32, (RUN, rows), 0) - (
        lax.broadcasted_iota(jnp.int32, (RUN, rows), 1) >> 3
    )

    def one_chunk(i, _):
        base = i * 2048
        early = meta_ref[24 + i]
        early_half = meta_ref[28 + i]
        piece = stats_ref[pl.ds(pl.multiple_of(i * 48, 16), 48), :].astype(F32)

        def tile(half, key_row, count, marks):
            q_rows = pl.ds(pl.multiple_of(base + half * rows, 16), rows)
            g_rows = pl.ds(pl.multiple_of(base + 1024 + half * rows, 16), rows)
            stats = []
            for j in range(2):
                total = piece[24 * j : 24 * j + 8] + piece[24 * j + 8 : 24 * j + 16] + piece[24 * j + 16 : 24 * j + 24]
                picked = jnp.where(half == 0, total[0:4], total[4:8])
                stats.append(jnp.concatenate([picked[k : k + 1] for k in range(4)], axis=1))
            lse2, delta = stats
            k_rows = pl.ds(key_row, count)
            kt = keys[k_rows, :]
            q = chunk[q_rows, :]
            g = chunk[g_rows, :]
            p = jnp.exp2(dot(kt, q, NT) * (scale * LOG2E) - lse2)
            if marks:
                cut = [p[: marks[0][0]]] if marks[0][0] else []
                for at, limit in marks:
                    cut.append(jnp.where(slope <= limit, p[at : at + RUN], 0.0))
                p = jnp.concatenate(cut, axis=0)
            ds = (p * (dot(values[k_rows, :], g, NT) - delta)).astype(BF16)
            dvalues[k_rows, :] += dot(p.astype(BF16), g, NN)
            dkeys[k_rows, :] += dot(ds, q, NN)
            acc = pl.ds(pl.multiple_of((2 * i + half) * 128, 128), 128)
            dq[acc, :] += dot(kt, ds, TN)

        def early_limit(u):
            return (early - meta_ref[u]) * RUN

        def late_limit(u):
            return (meta_ref[u] - early) * RUN

        late_half = 1 - early_half
        late_row = prompt + members * RUN
        tile(late_half, 0, late_row, [])
        tile(early_half, 0, prompt + 256, [(prompt + RUN * u, early_limit(u)) for u in range(4)])
        if members == 8:
            seen = 0
            for u in range(8):
                seen = seen + jnp.where(meta_ref[u] <= early, 1, 0)
            more = seen > 4
            tile(
                jnp.where(more, early_half, late_half),
                pl.multiple_of(jnp.where(more, prompt + 256, late_row), 16),
                256,
                [(RUN * u, jnp.where(more, early_limit(4 + u), late_limit(u))) for u in range(4)],
            )
        top = members - 4
        tile(late_half, late_row + RUN * top, 256, [(RUN * u, late_limit(top + u)) for u in range(4)])
        return 0

    lax.fori_loop(0, 4, one_chunk, 0)

    if last:
        for i in range(8):
            dq_out[pl.ds(i * rows, rows), :] = (dq[pl.ds(i * 128, 128), :].T * scale).astype(BF16)

    wide = outs[0].dtype
    total = outs[0] if last else stage
    for e in range(members):
        at = pl.ds(16 * e, 16)
        total[pl.ds(288 * e + 256, 16), :] = (dkeys[at, :] * scale).astype(wide)
        total[pl.ds(288 * e + 272, 16), :] = dvalues[at, :].astype(wide)
    for u in range(members):
        for at, frm in places(u):
            total[pl.ds(pl.multiple_of(at, 16), RUN), :] = (dkeys[frm, :] * scale).astype(wide)
            total[pl.ds(pl.multiple_of(at + 128, 16), RUN), :] = dvalues[frm, :].astype(wide)
    if not last:
        for part in range(parts):
            outs[part][...] = stage[pl.ds(part * 1152, 1152), :]
    for ref in held if last else []:
        outs[0][...] += ref[...].astype(F32)


def block_grads(shift, first, last, scale, at, stats, chunks, kv, dq, held):
    parts = len(kv)
    members = 4 * parts
    vmem = pl.BlockSpec(memory_space=pltpu.VMEM)
    smem = pl.BlockSpec(memory_space=pltpu.SMEM)
    operands = [at, stats, *chunks, *kv] + ([] if first else [dq]) + list(held)
    specs = [smem] + [vmem] * (5 + parts + (0 if first else 1))
    specs += [vmem if last else pl.BlockSpec(memory_space=pl.ANY)] * len(held)
    dq_shape = jax.ShapeDtypeStruct((4096, 128), BF16) if last else jax.ShapeDtypeStruct((1024, 512), F32)
    sorted_rows = 144 * members
    scratch = [
        pltpu.VMEM((4 * 2048, 128), BF16),
        pltpu.VMEM((sorted_rows, 128), BF16),
        pltpu.VMEM((sorted_rows, 128), BF16),
        pltpu.VMEM((sorted_rows, 128), F32),
        pltpu.VMEM((sorted_rows, 128), F32),
        pltpu.VMEM((1152 * parts, 128), BF16),
        pltpu.SMEM((32,), jnp.int32),
    ]
    if last:
        scratch.append(pltpu.VMEM((1024, 512), F32))
    return pl.pallas_call(
        functools.partial(grads_kernel, shift, members, first, last, scale, len(held)),
        out_shape=[dq_shape] + [jax.ShapeDtypeStruct((1152, 128), F32 if last else BF16)] * parts,
        in_specs=specs,
        out_specs=[vmem] * (1 + parts),
        scratch_shapes=scratch,
        compiler_params=pltpu.CompilerParams(vmem_limit_bytes=32 * 2**20),
        cost_estimate=pl.CostEstimate(
            flops=5_000_000_000 * parts, bytes_accessed=8_000_000, transcendentals=1_500_000 * parts
        ),
    )(*operands)


def chunks_kernel(at_ref, x_ref, kv_ref, p0_ref, p1_ref, p2_ref, p3_ref, o0_ref, o1_ref, o2_ref, o3_ref, prompts):
    head, r = at_ref[65], at_ref[68]
    for i, ref in enumerate((p0_ref, p1_ref, p2_ref, p3_ref)):
        prompts[i] = ref[...]
    terms = []
    for j in range(2):
        rest = x_ref[j]
        for _ in range(3):
            term = rest.astype(BF16)
            terms.append(term)
            rest = rest - term.astype(F32)
    terms = jnp.concatenate(terms, axis=0)
    slot = lax.broadcasted_iota(jnp.int32, (768, 128), 0)
    lane = lax.broadcasted_iota(jnp.int32, (768, 128), 1)
    here = (slot & 15) == (lane >> 3)
    to_row = lax.broadcasted_iota(jnp.int32, (48, 768), 0)
    from_slot = lax.broadcasted_iota(jnp.int32, (48, 768), 1)
    gather = (to_row == (from_slot >> 4)).astype(BF16)
    from_head = lax.broadcasted_iota(jnp.int32, (32, 128), 0)
    to_head = lax.broadcasted_iota(jnp.int32, (32, 128), 1) & 7
    for s, ref in enumerate((o0_ref, o1_ref, o2_ref, o3_ref)):
        g = (head + s) & 3
        spread = dot(terms, (from_head == to_head + 8 * g).astype(BF16), NN)
        ref[pl.ds(0, 256), :] = kv_ref[g]
        ref[pl.ds(256, 32), :] = prompts[(r - g) & 3]
        ref[pl.ds(288, 48), :] = dot(gather, jnp.where(here, spread, 0.0).astype(BF16), NN).astype(BF16)


def pick(stacked, index):
    return lax.dynamic_index_in_dim(stacked, index, 0, keepdims=False)


def make_chunks(at, x, kv, prompts):
    vmem = pl.BlockSpec(memory_space=pltpu.VMEM)
    return pl.pallas_call(
        chunks_kernel,
        out_shape=[jax.ShapeDtypeStruct((336, 128), BF16)] * 4,
        in_specs=[pl.BlockSpec(memory_space=pltpu.SMEM)] + [vmem] * 6,
        out_specs=[vmem] * 4,
        scratch_shapes=[pltpu.VMEM((4, 32, 128), BF16)],
        compiler_params=pltpu.CompilerParams(vmem_limit_bytes=16 * 2**20),
        cost_estimate=pl.CostEstimate(flops=200_000_000, bytes_accessed=1_000_000, transcendentals=0),
    )(at, x, kv, *prompts)


def shards(
    queries,
    resp_keys,
    resp_values,
    prompt_keys,
    prompt_values,
    grad_out,
    attn_out,
    logsumexp,
    order,
    lengths,
):
    scale = queries.shape[3] ** (-0.5)
    r = lax.axis_index("resp")
    c = lax.axis_index("ctx")
    x, z, y, core = coords(r, c)
    head = jnp.where(core == 0, y, x)
    block = jnp.where(core == 0, x, y)

    q_four = queries[0].reshape(128, 4, 8, 128)
    g_four = grad_out[0].reshape(128, 4, 8, 128)

    def q_chunk(g):
        q = lax.dynamic_index_in_dim(q_four, g, 1, keepdims=False).reshape(1024, 128)
        do = lax.dynamic_index_in_dim(g_four, g, 1, keepdims=False).reshape(1024, 128)
        return jnp.concatenate([q, do], axis=0)

    chunks = [q_chunk(head)] + [send(q_chunk((head + s) % 4), along_heads(s)) for s in (1, 3)]
    far_chunk = q_chunk((head + 2) % 4)

    prompt = jnp.concatenate([prompt_keys[:, 0], prompt_values[:, 0]], axis=0)
    prompts = [prompt] + [send(prompt, along_resp(s)) for s in (1, 2, 3)]
    query_pos = lax.dynamic_slice_in_dim(order[0], c * 128, 128)
    live = query_pos < lengths[0]
    delta = jnp.sum(grad_out[0].astype(F32) * attn_out[0].astype(F32), axis=-1)
    x_stats = jnp.stack([jnp.where(live[:, None], logsumexp[0] * LOG2E, 1e30), delta])
    resp_kv = jnp.stack([resp_keys[0], resp_values[0]]).transpose(2, 0, 1, 3).reshape(4, 256, 128)
    run_pos = order[0].reshape(64, RUN)[:, 0] // RUN
    at = jnp.concatenate([run_pos, jnp.stack([core, head, block, z, r])])
    pieces = make_chunks(at, x_stats, resp_kv, prompts)
    pieces = [pieces[0]] + [send(pieces[s], along_heads(s)) for s in (1, 2, 3)]
    near = jnp.concatenate([piece[:288] for piece in pieces], axis=0)
    stats = jnp.concatenate([piece[288:] for piece in pieces], axis=0)
    near, far_chunk, *chunks = lax.optimization_barrier((near, far_chunk, *chunks))
    chunks = [chunks[0], chunks[1], send(far_chunk, along_heads(2)), chunks[2]]
    far = send(near, along_z())
    own = jnp.concatenate([near, far], axis=0)
    kv_blocks = {s: send(own, along_blocks(s)) for s in (1, 3, 2)}

    dq, sent = block_grads(0, True, False, scale, at, stats, chunks, [far], None, [])
    got = {0: [send(sent, along_z())]}
    for i, s in enumerate((1, 3, 2)):
        held = got[0] if i == 1 else got[1] if i == 2 else []
        half = kv_blocks[s]
        dq, near_part, far_part = block_grads(
            s, False, False, scale, at, stats, chunks, [half[:1152], half[1152:]], dq, held
        )
        got[s] = [send(near_part, along_blocks(4 - s)), send(far_part, along_both(4 - s))]
    dq, totals = block_grads(0, False, True, scale, at, stats, chunks, [near], dq, got[0] + got[1] + got[3])

    dq, *late = lax.optimization_barrier((dq, *got[2]))
    back = [dq[:1024]]
    for s in (1, 2, 3):
        back.append(send(dq[1024 * s : 1024 * (s + 1)], along_heads(4 - s)))
    back = jnp.stack(back).reshape(4, 128, 8, 128)
    turn = (4 - head) % 4
    grad_queries = lax.dynamic_slice_in_dim(jnp.concatenate([back, back[:3]], axis=0), turn, 4, 0)
    grad_queries = grad_queries.transpose(1, 0, 2, 3).reshape(1, 128, 32, 128)

    for part in late:
        totals = totals + part.astype(F32)
    mine = totals.astype(BF16).reshape(4, 288, 128)
    rows = [mine[0]]
    for s in (1, 2, 3):
        rows.append(send(mine[s], along_heads(4 - s)))
    rows = jnp.stack(rows)
    rows = lax.dynamic_slice_in_dim(jnp.concatenate([rows, rows[:3]], axis=0), turn, 4, 0)
    grad_resp = rows[:, :256].reshape(4, 2, 128, 128).transpose(1, 2, 0, 3)
    parts = rows[:, 256:]
    mine_pair = pick(parts.reshape(2, 2, 32, 128).transpose(1, 0, 2, 3), core).astype(F32)
    theirs = pick(parts.reshape(2, 2, 32, 128).transpose(1, 0, 2, 3), 1 - core)
    mine_pair = mine_pair + send(theirs, across_cores()).astype(F32)
    prompt_sum = pick(mine_pair, r // 2) + send(pick(mine_pair, 1 - r // 2), across_z_hi())
    prompt_sum = prompt_sum.astype(BF16).reshape(2, 16, 128)
    return (
        grad_queries,
        grad_resp[0][None],
        grad_resp[1][None],
        prompt_sum[0][:, None],
        prompt_sum[1][:, None],
    )


def solution(mesh):
    wide = P("resp", "ctx", None, None)
    prompt = P("ctx", "resp", None)
    return jax.shard_map(
        shards,
        mesh=mesh,
        in_specs=(
            wide,
            wide,
            wide,
            prompt,
            prompt,
            wide,
            wide,
            P("resp", "ctx", None),
            P("resp", None),
            P("resp"),
        ),
        out_specs=(wide, wide, wide, prompt, prompt),
        check_vma=False,
    )
```

time: 151 us -> 121 us (0.80)
  waiting for transfers between devices: 35.8 us -> 9.63 us
  Pallas kernels: 49.9 us -> 44 us
  starting transfers between devices: 42.2 us -> 47.7 us
  local copies, waits for them, and re-layouts: 13.4 us -> 9.6 us
    ppermute x26 -> x28, waiting for transfers between devices: 35.8 us -> 9.63 us  [send(): return lax.ppermute(value, AXES, pairs)]
    unnamed x51 -> x30, local copies, waits for them, and re-layouts: 8.39 us -> 2.36 us
    pallas_call x4 -> x6, Pallas kernels: 49.9 us -> 44 us  [the longest x5 42.4 us: block_grads(): pl.pallas_call(functools.partial(grads_kernel, shift, members, first, las...]
    ppermute x26 -> x28, starting transfers between devices: 42.2 us -> 47.7 us  [send(): return lax.ppermute(value, AXES, pairs)]
    concatenate x9 -> x7, other arithmetic: 1.82 us -> 4.31 us  [the longest x4 3.58 us: q_chunk(): return jnp.concatenate([q, do], axis=0)]
    reduce_sum x1, other arithmetic: 2.24 us -> 0.63 us  [shards(): delta = jnp.sum(grad_out[0].astype(F32) * attn_out[0].astype(F32), axis=-1)]
  transfers between devices with their start and end apart: 26 -> 28, of which waited for: 13 -> 6; matrix products, arithmetic and copies ran while one was open for 8% -> 11% of each run, Pallas kernels for 25% -> 37%
where the time goes in v2:
time: 121 us; the launch traced here: 120 us
  starting transfers between devices  47.7 us (39%)
  Pallas kernels  44 us (36%)
  waiting for transfers between devices  9.63 us (8%)
  local copies, waits for them, and re-layouts  9.6 us (8%)
  other arithmetic  7.02 us (6%)
  between operations  1.78 us (1%)
    ppermute x28, starting transfers between devices, send(): return lax.ppermute(value, AXES, pairs)  47.7 us
    pallas_call x5, Pallas kernels, block_grads(): pl.pallas_call(functools.partial(grads_kernel, shift, members, first, las...  42.4 us
    ppermute x28, waiting for transfers between devices, send(): return lax.ppermute(value, AXES, pairs)  9.63 us
    concatenate x4, other arithmetic, q_chunk(): return jnp.concatenate([q, do], axis=0)  3.58 us
    reshape x1, local copies, waits for them, and re-layouts, q_chunk(): lax.dynamic_index_in_dim(g_four, g, 1, keepdims=False).reshape(1024, 128)  2.52 us
  transfers between devices with their start and end apart: 28, of which 6 were waited for; matrix products, arithmetic and copies ran while one was open for 11% of the time, Pallas kernels for 37%

profile of v2, /device:TPU:1, one launch (start us, length us, event | category | flops | bytes accessed | tf_op | source)
XLA Modules:
  0.0 119.7 jit_solution(16539941750204994796)
XLA Ops:
  0.6 0.7 pad_maximum_fusion.7.p0_ref
  1.3 1.4 %collective-permute-start.2 = (bf16[32,128]{1,0:T(8,128)(2,1)S(1)}, bf16[32,128]{1,0:T(8,128)(2,1)S(1)}, u32[]{:S(2)}, u32[]{:S(2)}) collective-permute-start(bf16[32,128]{1,0:T(8,128)(2,1)S(1)} %pad_maximum_fusion.7.p0_ref), channel_id=1, source_target_pairs={{0,96},{1,97},{2,98},{3,99},{4,100},{5,101},{6,102},{7,103},{8,104... | collective-permute-start | bytes 24584 | tf_op jit(solution)/shard_map/ppermute | solution.py:63
  2.8 3.7 %collective-permute-start.1 = (bf16[32,128]{1,0:T(8,128)(2,1)S(1)}, bf16[32,128]{1,0:T(8,128)(2,1)S(1)}, u32[]{:S(2)}, u32[]{:S(2)}) collective-permute-start(bf16[32,128]{1,0:T(8,128)(2,1)S(1)} %pad_maximum_fusion.7.p0_ref), channel_id=1, source_target_pairs={{0,64},{1,65},{2,66},{3,67},{4,68},{5,69},{6,70},{7,71},{8,72},{9,... | collective-permute-start | bytes 24584 | tf_op jit(solution)/shard_map/ppermute | solution.py:63
  6.4 2.9 %collective-permute-start = (bf16[32,128]{1,0:T(8,128)(2,1)S(1)}, bf16[32,128]{1,0:T(8,128)(2,1)S(1)}, u32[]{:S(2)}, u32[]{:S(2)}) collective-permute-start(bf16[32,128]{1,0:T(8,128)(2,1)S(1)} %pad_maximum_fusion.7.p0_ref), channel_id=1, source_target_pairs={{0,32},{1,33},{2,34},{3,35},{4,36},{5,37},{6,38},{7,39},{8,40},{9,... | collective-permute-start | bytes 24584 | tf_op jit(solution)/shard_map/ppermute | solution.py:63
  9.3 2.5 %dynamic-slice_bitcast_fusion.1 = (bf16[1024,128]{1,0:T(8,128)(2,1)S(1)}, bf16[1024,128]{1,0:T(8,128)(2,1)S(1)}, bf16[1024,128]{1,0:T(8,128)(2,1)}, bf16[1024,12...) fusion(bf16[128,4,8,128]{3,2,1,0:T(8,128)(2,1)} %bitcast.109, ...), kind=kLoop, calls=%fused_computation.18 | loop fusion | bytes 4194320 | tf_op jit(solution)/shard_map/reshape | solution.py:316
  11.8 0.8 pad_maximum_fusion.2
  12.7 1.2 %collective-permute-start.6 = (bf16[2048,128]{1,0:T(8,128)(2,1)}, bf16[2048,128]{1,0:T(8,128)(2,1)S(1)}, u32[]{:S(2)}, u32[]{:S(2)}) collective-permute-start(bf16[2048,128]{1,0:T(8,128)(2,1)} %pad_maximum_fusion.2), channel_id=1, source_target_pairs={{0,1},{1,2},{2,3},{3,0},{4,5},{5,6},{6,7},{7,4},{8,9},{9,10},{10,1... | collective-permute-start | bytes 1572872 | tf_op jit(solution)/shard_map/ppermute | solution.py:63
  13.9 0.8 pad_maximum_fusion.3
  14.7 1.5 %collective-permute-start.7 = (bf16[2048,128]{1,0:T(8,128)(2,1)}, bf16[2048,128]{1,0:T(8,128)(2,1)S(1)}, u32[]{:S(2)}, u32[]{:S(2)}) collective-permute-start(bf16[2048,128]{1,0:T(8,128)(2,1)} %pad_maximum_fusion.3), channel_id=1, source_target_pairs={{0,3},{1,0},{2,1},{3,2},{4,7},{5,4},{6,5},{7,6},{8,11},{9,8},{10,9... | collective-permute-start | bytes 1572872 | tf_op jit(solution)/shard_map/ppermute | solution.py:63
  16.8 0.5 broadcast.37
  17.3 0.7 reduce.4
  18.0 0.1 reshape_squeeze.9
  18.1 0.1 copy.68
  18.2 0.6 multiply_reduce_fusion
  18.9 0.1 copy.56
  19.0 0.1 multiply_select_fusion
  19.1 1.2 maximum_bitcast_fusion
  20.2 1.1 pad_maximum_fusion.1.c0_ref
  21.4 0.1 concatenate.41.at_ref
  21.5 1.6 %shard_map.137 = (bf16[336,128]{1,0:T(8,128)(2,1)S(1)}, bf16[336,128]{1,0:T(8,128)(2,1)S(1)}, bf16[336,128]{1,0:T(8,128)(2,1)S(1)}, bf16[336,128]{1,0:T(8,128)(2,1)S(1)}) custom-call(s32[69]{0:T(128)S(1)} %concatenate.41.at_ref, f32[2,128,32]{2,1,0:T(8,128)S(1)} %pad_maximum_fusion.5.x_ref, bf16[4,256,128]{2,1,0:T(8,128)(2,1)S(1)} %bitcast.108, ...), custom_call_target="tpu_custom_call" | custom-call | flops 200000000 | bytes 1000000 | tf_op jit(solution)/shard_map/pallas_call | solution.py:281
  23.1 0.1 collective-permute-start.3
  23.2 2.4 %collective-permute-start.4 = (bf16[336,128]{1,0:T(8,128)(2,1)S(1)}, bf16[336,128]{1,0:T(8,128)(2,1)S(1)}, u32[]{:S(2)}, u32[]{:S(2)}) collective-permute-start(bf16[336,128]{1,0:T(8,128)(2,1)S(1)} %get-tuple-element.32), channel_id=1, source_target_pairs={{0,2},{1,3},{2,0},{3,1},{4,6},{5,7},{6,4},{7,5},{8,10},{9,11},{10,... | collective-permute-start | bytes 258056 | tf_op jit(solution)/shard_map/ppermute | solution.py:63
  25.6 1.2 collective-permute-start.5
  26.8 0.9 pad_maximum_fusion
  27.7 1.0 collective-permute-done.3
  28.7 0.5 collective-permute-done.5
  29.2 0.1 copy-done.3
  29.4 0.6 copy-done.4
  29.9 0.7 collective-permute-start.9
  30.7 1.8 %collective-permute-start.8 = (bf16[2048,128]{1,0:T(8,128)(2,1)}, bf16[2048,128]{1,0:T(8,128)(2,1)S(1)}, u32[]{:S(2)}, u32[]{:S(2)}) collective-permute-start(bf16[2048,128]{1,0:T(8,128)(2,1)} %pad_maximum_fusion), channel_id=1, source_target_pairs={{0,2},{1,3},{2,0},{3,1},{4,6},{5,7},{6,4},{7,5},{8,10},{9,11},{10,... | collective-permute-start | bytes 1572872 | tf_op jit(solution)/shard_map/ppermute | solution.py:63
  32.5 0.7 constant_dynamic-update-slice_fusion.1
  33.2 5.4 %collective-permute-done.9.rest_0_ = bf16[1152,128]{1,0:T(8,128)(2,1)S(1)} collective-permute-done((bf16[1152,128]{1,0:T(8,128)(2,1)S(1)}, bf16[1152,128]{1,0:T(8,128)(2,1)S(1)}, u32[]{:S(2)}, u32[]{:S(2)}) %collective-permute-start.9) | collective-permute-done | bytes 294944 | tf_op jit(solution)/shard_map/ppermute | solution.py:63
  38.7 0.7 constant_dynamic-update-slice_fusion
  39.4 1.4 %collective-permute-start.12 = (bf16[2304,128]{1,0:T(8,128)(2,1)}, bf16[2304,128]{1,0:T(8,128)(2,1)S(1)}, u32[]{:S(2)}, u32[]{:S(2)}) collective-permute-start(bf16[2304,128]{1,0:T(8,128)(2,1)} %constant_dynamic-update-slice_fusion), channel_id=1, source_target_pairs={{0,8},{1,9},{2,10},{3,11},{4,12},{5,13},{6,14},{7,15},{8,16},{9,17... | collective-permute-start | bytes 1769480 | tf_op jit(solution)/shard_map/ppermute | solution.py:63
  40.8 0.7 slice.133
  41.6 1.5 %collective-permute-start.11 = (bf16[2304,128]{1,0:T(8,128)(2,1)}, bf16[2304,128]{1,0:T(8,128)(2,1)S(1)}, u32[]{:S(2)}, u32[]{:S(2)}) collective-permute-start(bf16[2304,128]{1,0:T(8,128)(2,1)} %constant_dynamic-update-slice_fusion), channel_id=1, source_target_pairs={{0,24},{1,25},{2,26},{3,27},{4,28},{5,29},{6,30},{7,31},{8,0},{9,1... | collective-permute-start | bytes 1769480 | tf_op jit(solution)/shard_map/ppermute | solution.py:63
  43.1 1.3 %collective-permute-start.10 = (bf16[2304,128]{1,0:T(8,128)(2,1)}, bf16[2304,128]{1,0:T(8,128)(2,1)S(1)}, u32[]{:S(2)}, u32[]{:S(2)}) collective-permute-start(bf16[2304,128]{1,0:T(8,128)(2,1)} %constant_dynamic-update-slice_fusion), channel_id=1, source_target_pairs={{0,16},{1,17},{2,18},{3,19},{4,20},{5,21},{6,22},{7,23},{8,24},{9,... | collective-permute-start | bytes 1769480 | tf_op jit(solution)/shard_map/ppermute | solution.py:63
  44.4 6.4 %shard_map.138 = (f32[1024,512]{1,0:T(8,128)S(1)}, bf16[1152,128]{1,0:T(8,128)(2,1)S(1)}) custom-call(s32[69]{0:T(128)S(1)} %concatenate.41.at_ref, bf16[192,128]{1,0:T(8,128)(2,1)S(1)} %pad_maximum_fusion.6.stats_ref, bf16[2048,128]{1,0:T(8,128)(2,1)S(1)} %pad_maximum_fusion.1.c0_ref, bf16[2048,128]{1,0:T(8,128)(2,1)S(1)} %collective-permute-done.6.c1_ref, ...), custom_call_target="tpu_custom_call" | custom-call | flops 5000000000 | bytes 8000000 | tf_op jit(solution)/shard_map/pallas_call | solution.py:234
  50.7 0.8 collective-permute-start.13
  51.6 9.6 %shard_map.139 = (f32[1024,512]{1,0:T(8,128)S(1)}, bf16[1152,128]{1,0:T(8,128)(2,1)S(1)}, bf16[1152,128]{1,0:T(8,128)(2,1)S(1)}) custom-call(s32[69]{0:T(128)S(1)} %concatenate.41.at_ref, bf16[192,128]{1,0:T(8,128)(2,1)S(1)} %pad_maximum_fusion.6.stats_ref, bf16[2048,128]{1,0:T(8,128)(2,1)S(1)} %pad_maximum_fusion.1.c0_ref, ...), custom_call_target="tpu_custom_call" | custom-call | flops 10000000000 | bytes 8000000 | tf_op jit(solution)/shard_map/pallas_call | solution.py:234
  61.2 1.4 %collective-permute-start.14 = (bf16[1152,128]{1,0:T(8,128)(2,1)S(1)}, bf16[1152,128]{1,0:T(8,128)(2,1)S(1)}, u32[]{:S(2)}, u32[]{:S(2)}) collective-permute-start(bf16[1152,128]{1,0:T(8,128)(2,1)S(1)} %get-tuple-element.43), channel_id=1, source_target_pairs={{0,24},{1,25},{2,26},{3,27},{4,28},{5,29},{6,30},{7,31},{8,0},{9,1... | collective-permute-start | bytes 884744 | tf_op jit(solution)/shard_map/ppermute | solution.py:63
  62.6 1.3 %collective-permute-start.15 = (bf16[1152,128]{1,0:T(8,128)(2,1)S(1)}, bf16[1152,128]{1,0:T(8,128)(2,1)S(1)}, u32[]{:S(2)}, u32[]{:S(2)}) collective-permute-start(bf16[1152,128]{1,0:T(8,128)(2,1)S(1)} %get-tuple-element.44), channel_id=1, source_target_pairs={{0,28},{1,29},{2,30},{3,31},{4,24},{5,25},{6,26},{7,27},{8,4},{9,5... | collective-permute-start | bytes 884744 | tf_op jit(solution)/shard_map/ppermute | solution.py:63
  64.0 9.6 %shard_map.140 = (f32[1024,512]{1,0:T(8,128)S(1)}, bf16[1152,128]{1,0:T(8,128)(2,1)S(1)}, bf16[1152,128]{1,0:T(8,128)(2,1)S(1)}) custom-call(s32[69]{0:T(128)S(1)} %concatenate.41.at_ref, bf16[192,128]{1,0:T(8,128)(2,1)S(1)} %pad_maximum_fusion.6.stats_ref, bf16[2048,128]{1,0:T(8,128)(2,1)S(1)} %pad_maximum_fusion.1.c0_ref, ...), custom_call_target="tpu_custom_call" | custom-call | flops 10000000000 | bytes 8000000 | tf_op jit(solution)/shard_map/pallas_call | solution.py:234
  73.6 0.7 collective-permute-start.16
  74.3 0.8 collective-permute-start.17
  75.1 9.6 %shard_map.141 = (f32[1024,512]{1,0:T(8,128)S(1)}, bf16[1152,128]{1,0:T(8,128)(2,1)S(1)}, bf16[1152,128]{1,0:T(8,128)(2,1)S(1)}) custom-call(s32[69]{0:T(128)S(1)} %concatenate.41.at_ref, bf16[192,128]{1,0:T(8,128)(2,1)S(1)} %pad_maximum_fusion.6.stats_ref, bf16[2048,128]{1,0:T(8,128)(2,1)S(1)} %pad_maximum_fusion.1.c0_ref, ...), custom_call_target="tpu_custom_call" | custom-call | flops 10000000000 | bytes 8000000 | tf_op jit(solution)/shard_map/pallas_call | solution.py:234
  84.7 3.0 %collective-permute-start.18 = (bf16[1152,128]{1,0:T(8,128)(2,1)S(1)}, bf16[1152,128]{1,0:T(8,128)(2,1)S(1)}, u32[]{:S(2)}, u32[]{:S(2)}) collective-permute-start(bf16[1152,128]{1,0:T(8,128)(2,1)S(1)} %get-tuple-element.49), channel_id=1, source_target_pairs={{0,16},{1,17},{2,18},{3,19},{4,20},{5,21},{6,22},{7,23},{8,24},{9,... | collective-permute-start | bytes 884744 | tf_op jit(solution)/shard_map/ppermute | solution.py:63
  87.7 0.6 collective-permute-start.19
  88.3 7.2 %shard_map.142 = (bf16[4096,128]{1,0:T(8,128)(2,1)S(1)}, f32[1152,128]{1,0:T(8,128)S(1)}) custom-call(s32[69]{0:T(128)S(1)} %concatenate.41.at_ref, bf16[192,128]{1,0:T(8,128)(2,1)S(1)} %pad_maximum_fusion.6.stats_ref, bf16[2048,128]{1,0:T(8,128)(2,1)S(1)} %pad_maximum_fusion.1.c0_ref, bf16[2048,128]{1,0:T(8,128)(2,1)S(1)} %collective-permute-done.6.c1_ref, ...), custom_call_target="tpu_custom_call" | custom-call | flops 5000000000 | bytes 8000000 | tf_op jit(solution)/shard_map/pallas_call | solution.py:234
  95.5 0.2 collective-permute-done.19
  95.7 0.1 fusion.3
  95.8 0.1 add_convert_fusion
  95.9 3.2 %collective-permute-start.23 = (bf16[288,128]{1,0:T(8,128)(2,1)S(1)}, bf16[288,128]{1,0:T(8,128)(2,1)S(1)}, u32[]{:S(2)}, u32[]{:S(2)}) collective-permute-start(bf16[288,128]{1,0:T(8,128)(2,1)S(1)} %get-tuple-element.74), channel_id=1, source_target_pairs={{0,3},{1,0},{2,1},{3,2},{4,7},{5,4},{6,5},{7,6},{8,11},{9,8},{10,9... | collective-permute-start | bytes 221192 | tf_op jit(solution)/shard_map/ppermute | solution.py:63
  99.1 7.4 %collective-permute-start.24 = (bf16[288,128]{1,0:T(8,128)(2,1)S(1)}, bf16[288,128]{1,0:T(8,128)(2,1)S(1)}, u32[]{:S(2)}, u32[]{:S(2)}) collective-permute-start(bf16[288,128]{1,0:T(8,128)(2,1)S(1)} %get-tuple-element.73), channel_id=1, source_target_pairs={{0,2},{1,3},{2,0},{3,1},{4,6},{5,7},{6,4},{7,5},{8,10},{9,11},{10,... | collective-permute-start | bytes 221192 | tf_op jit(solution)/shard_map/ppermute | solution.py:63
  106.5 1.9 %collective-permute-start.21 = (bf16[1024,128]{1,0:T(8,128)(2,1)S(1)}, bf16[1024,128]{1,0:T(8,128)(2,1)S(1)}, u32[]{:S(2)}, u32[]{:S(2)}) collective-permute-start(bf16[1024,128]{1,0:T(8,128)(2,1)S(1)} %get-tuple-element.56), channel_id=1, source_target_pairs={{0,2},{1,3},{2,0},{3,1},{4,6},{5,7},{6,4},{7,5},{8,10},{9,11},{10,... | collective-permute-start | bytes 786440 | tf_op jit(solution)/shard_map/ppermute | solution.py:63
  108.4 0.8 collective-permute-start.20
  109.4 3.0 %collective-permute-start.26 = (bf16[2,32,128]{2,1,0:T(8,128)(2,1)S(1)}, bf16[2,32,128]{2,1,0:T(8,128)(2,1)S(1)}, u32[]{:S(2)}, u32[]{:S(2)}) collective-permute-start(bf16[2,32,128]{2,1,0:T(8,128)(2,1)S(1)} %dynamic-slice_bitcast_fusion.10), channel_id=1, source_target_pairs={{0,32},{1,33},{2,34},{3,35},{4,36},{5,37},{6,38},{7,39},{8,40},{9,... | collective-permute-start | bytes 49160 | tf_op jit(solution)/shard_map/ppermute | solution.py:63
  112.4 0.2 copy.79
  112.6 0.6 collective-permute-done.26
  113.2 1.9 %collective-permute-start.27 = (f32[32,128]{1,0:T(8,128)S(1)}, f32[32,128]{1,0:T(8,128)S(1)}, u32[]{:S(2)}, u32[]{:S(2)}) collective-permute-start(f32[32,128]{1,0:T(8,128)S(1)} %dynamic-slice_bitcast_fusion.9), channel_id=1, source_target_pairs={{0,64},{1,65},{2,66},{3,67},{4,68},{5,69},{6,70},{7,71},{8,72},{9,... | collective-permute-start | bytes 49160 | tf_op jit(solution)/shard_map/ppermute | solution.py:63
  115.1 0.8 fusion.8
  115.8 1.8 %collective-permute-done.27 = f32[32,128]{1,0:T(8,128)S(1)} collective-permute-done((f32[32,128]{1,0:T(8,128)S(1)}, f32[32,128]{1,0:T(8,128)S(1)}, u32[]{:S(2)}, u32[]{:S(2)}) %collective-permute-start.27) | collective-permute-done | bytes 16416 | tf_op jit(solution)/shard_map/ppermute | solution.py:63
  117.7 0.6 slice_bitcast_fusion.1
  118.5 1.2 copy_bitcast_fusion
  (74 shorter events, 0.8 us)
Async XLA Ops:
  1.3 20.2 %collective-permute-start.2 = (bf16[32,128]{1,0:T(8,128)(2,1)S(1)}, bf16[32,128]{1,0:T(8,128)(2,1)S(1)}, u32[]{:S(2)}, u32[]{:S(2)}) collective-permute-start(bf16[32,128]{1,0:T(8,128)(2,1)S(1)} %pad_maximum_fusion.7.p0_ref), channel_id=1, source_target_pairs={{0,96},{1,97},{2,98},{3,99},{4,100},{5,101},{6,102},{7,103},{8,104... | collective-permute-start | bytes 24584 | tf_op jit(solution)/shard_map/ppermute | solution.py:63
  2.8 18.7 %collective-permute-start.1 = (bf16[32,128]{1,0:T(8,128)(2,1)S(1)}, bf16[32,128]{1,0:T(8,128)(2,1)S(1)}, u32[]{:S(2)}, u32[]{:S(2)}) collective-permute-start(bf16[32,128]{1,0:T(8,128)(2,1)S(1)} %pad_maximum_fusion.7.p0_ref), channel_id=1, source_target_pairs={{0,64},{1,65},{2,66},{3,67},{4,68},{5,69},{6,70},{7,71},{8,72},{9,... | collective-permute-start | bytes 24584 | tf_op jit(solution)/shard_map/ppermute | solution.py:63
  6.4 15.1 %collective-permute-start = (bf16[32,128]{1,0:T(8,128)(2,1)S(1)}, bf16[32,128]{1,0:T(8,128)(2,1)S(1)}, u32[]{:S(2)}, u32[]{:S(2)}) collective-permute-start(bf16[32,128]{1,0:T(8,128)(2,1)S(1)} %pad_maximum_fusion.7.p0_ref), channel_id=1, source_target_pairs={{0,32},{1,33},{2,34},{3,35},{4,36},{5,37},{6,38},{7,39},{8,40},{9,... | collective-permute-start | bytes 24584 | tf_op jit(solution)/shard_map/ppermute | solution.py:63
  11.8 5.5 %copy-start.5 = (s32[1,4096]{1,0:T(1,128)S(1)}, s32[1,4096]{1,0:T(1,128)}, u32[]{:S(2)}) copy-start(s32[1,4096]{1,0:T(1,128)} %param.18) | copy-start | bytes 49156
  11.8 6.4 %copy-start = (bf16[1,128,32,128]{3,2,1,0:T(8,128)(2,1)S(1)}, bf16[1,128,32,128]{3,2,1,0:T(8,128)(2,1)}, u32[]{:S(2)}) copy-start(bf16[1,128,32,128]{3,2,1,0:T(8,128)(2,1)} %param.15) | copy-start | bytes 3145732
  11.8 6.4 %copy-start.1 = (bf16[1,128,32,128]{3,2,1,0:T(8,128)(2,1)S(1)}, bf16[1,128,32,128]{3,2,1,0:T(8,128)(2,1)}, u32[]{:S(2)}) copy-start(bf16[1,128,32,128]{3,2,1,0:T(8,128)(2,1)} %param.16) | copy-start | bytes 3145732
  12.7 6.2 %copy-start.6 = (f32[1,128,32]{1,2,0:T(8,128)S(1)}, f32[1,128,32]{1,2,0:T(8,128)}, u32[]{:S(2)}) copy-start(f32[1,128,32]{1,2,0:T(8,128)} %param.17) | copy-start | bytes 49156
  12.7 16.7 %collective-permute-start.6 = (bf16[2048,128]{1,0:T(8,128)(2,1)}, bf16[2048,128]{1,0:T(8,128)(2,1)S(1)}, u32[]{:S(2)}, u32[]{:S(2)}) collective-permute-start(bf16[2048,128]{1,0:T(8,128)(2,1)} %pad_maximum_fusion.2), channel_id=1, source_target_pairs={{0,1},{1,2},{2,3},{3,0},{4,5},{5,6},{6,7},{7,4},{8,9},{9,10},{10,1... | collective-permute-start | bytes 1572872 | tf_op jit(solution)/shard_map/ppermute | solution.py:63
  14.7 14.7 %collective-permute-start.7 = (bf16[2048,128]{1,0:T(8,128)(2,1)}, bf16[2048,128]{1,0:T(8,128)(2,1)S(1)}, u32[]{:S(2)}, u32[]{:S(2)}) collective-permute-start(bf16[2048,128]{1,0:T(8,128)(2,1)} %pad_maximum_fusion.3), channel_id=1, source_target_pairs={{0,3},{1,0},{2,1},{3,2},{4,7},{5,4},{6,5},{7,6},{8,11},{9,8},{10,9... | collective-permute-start | bytes 1572872 | tf_op jit(solution)/shard_map/ppermute | solution.py:63
  18.8 7.9 %copy-start.2 = (bf16[1024,128]{1,0:T(8,128)(2,1)S(1)}, bf16[1024,128]{1,0:T(8,128)(2,1)}, u32[]{:S(2)}) copy-start(bf16[1024,128]{1,0:T(8,128)(2,1)} %get-tuple-element.79) | copy-start | bytes 786436
  23.1 5.5 %collective-permute-start.3 = (bf16[336,128]{1,0:T(8,128)(2,1)S(1)}, bf16[336,128]{1,0:T(8,128)(2,1)S(1)}, u32[]{:S(2)}, u32[]{:S(2)}) collective-permute-start(bf16[336,128]{1,0:T(8,128)(2,1)S(1)} %get-tuple-element.31), channel_id=1, source_target_pairs={{0,1},{1,2},{2,3},{3,0},{4,5},{5,6},{6,7},{7,4},{8,9},{9,10},{10,1... | collective-permute-start | bytes 258056 | tf_op jit(solution)/shard_map/ppermute | solution.py:63
  23.2 5.5 %collective-permute-start.4 = (bf16[336,128]{1,0:T(8,128)(2,1)S(1)}, bf16[336,128]{1,0:T(8,128)(2,1)S(1)}, u32[]{:S(2)}, u32[]{:S(2)}) collective-permute-start(bf16[336,128]{1,0:T(8,128)(2,1)S(1)} %get-tuple-element.32), channel_id=1, source_target_pairs={{0,2},{1,3},{2,0},{3,1},{4,6},{5,7},{6,4},{7,5},{8,10},{9,11},{10,... | collective-permute-start | bytes 258056 | tf_op jit(solution)/shard_map/ppermute | solution.py:63
  25.6 3.6 %collective-permute-start.5 = (bf16[336,128]{1,0:T(8,128)(2,1)S(1)}, bf16[336,128]{1,0:T(8,128)(2,1)S(1)}, u32[]{:S(2)}, u32[]{:S(2)}) collective-permute-start(bf16[336,128]{1,0:T(8,128)(2,1)S(1)} %get-tuple-element.33), channel_id=1, source_target_pairs={{0,3},{1,0},{2,1},{3,2},{4,7},{5,4},{6,5},{7,6},{8,11},{9,8},{10,9... | collective-permute-start | bytes 258056 | tf_op jit(solution)/shard_map/ppermute | solution.py:63
  28.7 0.6 copy-start.3
  29.3 0.6 copy-start.4
  29.3 12.2 %slice-start = ((bf16[336,128]{1,0:T(8,128)(2,1)}), bf16[48,128]{1,0:T(8,128)(2,1)S(1)}, s32[]{:S(2)}) async-start(bf16[336,128]{1,0:T(8,128)(2,1)} %copy-done.3), calls=%async_computation | async-start | bytes 24576 | tf_op jit(solution)/shard_map/slice | solution.py:334
  29.9 8.7 %collective-permute-start.9 = (bf16[1152,128]{1,0:T(8,128)(2,1)S(1)}, bf16[1152,128]{1,0:T(8,128)(2,1)S(1)}, u32[]{:S(2)}, u32[]{:S(2)}) collective-permute-start(bf16[1152,128]{1,0:T(8,128)(2,1)S(1)} %pad_maximum_fusion.4.rest_0_), channel_id=1, source_target_pairs={{0,4},{1,5},{2,6},{3,7},{4,0},{5,1},{6,2},{7,3},{8,12},{9,13},{10,... | collective-permute-start | bytes 884744 | tf_op jit(solution)/shard_map/ppermute | solution.py:63
  30.7 13.7 %collective-permute-start.8 = (bf16[2048,128]{1,0:T(8,128)(2,1)}, bf16[2048,128]{1,0:T(8,128)(2,1)S(1)}, u32[]{:S(2)}, u32[]{:S(2)}) collective-permute-start(bf16[2048,128]{1,0:T(8,128)(2,1)} %pad_maximum_fusion), channel_id=1, source_target_pairs={{0,2},{1,3},{2,0},{3,1},{4,6},{5,7},{6,4},{7,5},{8,10},{9,11},{10,... | collective-permute-start | bytes 1572872 | tf_op jit(solution)/shard_map/ppermute | solution.py:63
  39.4 12.2 %collective-permute-start.12 = (bf16[2304,128]{1,0:T(8,128)(2,1)}, bf16[2304,128]{1,0:T(8,128)(2,1)S(1)}, u32[]{:S(2)}, u32[]{:S(2)}) collective-permute-start(bf16[2304,128]{1,0:T(8,128)(2,1)} %constant_dynamic-update-slice_fusion), channel_id=1, source_target_pairs={{0,8},{1,9},{2,10},{3,11},{4,12},{5,13},{6,14},{7,15},{8,16},{9,17... | collective-permute-start | bytes 1769480 | tf_op jit(solution)/shard_map/ppermute | solution.py:63
  41.6 22.4 %collective-permute-start.11 = (bf16[2304,128]{1,0:T(8,128)(2,1)}, bf16[2304,128]{1,0:T(8,128)(2,1)S(1)}, u32[]{:S(2)}, u32[]{:S(2)}) collective-permute-start(bf16[2304,128]{1,0:T(8,128)(2,1)} %constant_dynamic-update-slice_fusion), channel_id=1, source_target_pairs={{0,24},{1,25},{2,26},{3,27},{4,28},{5,29},{6,30},{7,31},{8,0},{9,1... | collective-permute-start | bytes 1769480 | tf_op jit(solution)/shard_map/ppermute | solution.py:63
  43.1 32.0 %collective-permute-start.10 = (bf16[2304,128]{1,0:T(8,128)(2,1)}, bf16[2304,128]{1,0:T(8,128)(2,1)S(1)}, u32[]{:S(2)}, u32[]{:S(2)}) collective-permute-start(bf16[2304,128]{1,0:T(8,128)(2,1)} %constant_dynamic-update-slice_fusion), channel_id=1, source_target_pairs={{0,16},{1,17},{2,18},{3,19},{4,20},{5,21},{6,22},{7,23},{8,24},{9,... | collective-permute-start | bytes 1769480 | tf_op jit(solution)/shard_map/ppermute | solution.py:63
  50.7 13.2 %collective-permute-start.13 = (bf16[1152,128]{1,0:T(8,128)(2,1)S(1)}, bf16[1152,128]{1,0:T(8,128)(2,1)S(1)}, u32[]{:S(2)}, u32[]{:S(2)}) collective-permute-start(bf16[1152,128]{1,0:T(8,128)(2,1)S(1)} %get-tuple-element.41), channel_id=1, source_target_pairs={{0,4},{1,5},{2,6},{3,7},{4,0},{5,1},{6,2},{7,3},{8,12},{9,13},{10,... | collective-permute-start | bytes 884744 | tf_op jit(solution)/shard_map/ppermute | solution.py:63
  61.2 13.9 %collective-permute-start.14 = (bf16[1152,128]{1,0:T(8,128)(2,1)S(1)}, bf16[1152,128]{1,0:T(8,128)(2,1)S(1)}, u32[]{:S(2)}, u32[]{:S(2)}) collective-permute-start(bf16[1152,128]{1,0:T(8,128)(2,1)S(1)} %get-tuple-element.43), channel_id=1, source_target_pairs={{0,24},{1,25},{2,26},{3,27},{4,28},{5,29},{6,30},{7,31},{8,0},{9,1... | collective-permute-start | bytes 884744 | tf_op jit(solution)/shard_map/ppermute | solution.py:63
  62.6 12.5 %collective-permute-start.15 = (bf16[1152,128]{1,0:T(8,128)(2,1)S(1)}, bf16[1152,128]{1,0:T(8,128)(2,1)S(1)}, u32[]{:S(2)}, u32[]{:S(2)}) collective-permute-start(bf16[1152,128]{1,0:T(8,128)(2,1)S(1)} %get-tuple-element.44), channel_id=1, source_target_pairs={{0,28},{1,29},{2,30},{3,31},{4,24},{5,25},{6,26},{7,27},{8,4},{9,5... | collective-permute-start | bytes 884744 | tf_op jit(solution)/shard_map/ppermute | solution.py:63
  73.6 14.7 %collective-permute-start.16 = (bf16[1152,128]{1,0:T(8,128)(2,1)S(1)}, bf16[1152,128]{1,0:T(8,128)(2,1)S(1)}, u32[]{:S(2)}, u32[]{:S(2)}) collective-permute-start(bf16[1152,128]{1,0:T(8,128)(2,1)S(1)} %get-tuple-element.46), channel_id=1, source_target_pairs={{0,8},{1,9},{2,10},{3,11},{4,12},{5,13},{6,14},{7,15},{8,16},{9,17... | collective-permute-start | bytes 884744 | tf_op jit(solution)/shard_map/ppermute | solution.py:63
  74.3 14.0 %collective-permute-start.17 = (bf16[1152,128]{1,0:T(8,128)(2,1)S(1)}, bf16[1152,128]{1,0:T(8,128)(2,1)S(1)}, u32[]{:S(2)}, u32[]{:S(2)}) collective-permute-start(bf16[1152,128]{1,0:T(8,128)(2,1)S(1)} %get-tuple-element.47), channel_id=1, source_target_pairs={{0,12},{1,13},{2,14},{3,15},{4,8},{5,9},{6,10},{7,11},{8,20},{9,21... | collective-permute-start | bytes 884744 | tf_op jit(solution)/shard_map/ppermute | solution.py:63
  84.7 10.8 %collective-permute-start.18 = (bf16[1152,128]{1,0:T(8,128)(2,1)S(1)}, bf16[1152,128]{1,0:T(8,128)(2,1)S(1)}, u32[]{:S(2)}, u32[]{:S(2)}) collective-permute-start(bf16[1152,128]{1,0:T(8,128)(2,1)S(1)} %get-tuple-element.49), channel_id=1, source_target_pairs={{0,16},{1,17},{2,18},{3,19},{4,20},{5,21},{6,22},{7,23},{8,24},{9,... | collective-permute-start | bytes 884744 | tf_op jit(solution)/shard_map/ppermute | solution.py:63
  87.7 8.0 %collective-permute-start.19 = (bf16[1152,128]{1,0:T(8,128)(2,1)S(1)}, bf16[1152,128]{1,0:T(8,128)(2,1)S(1)}, u32[]{:S(2)}, u32[]{:S(2)}) collective-permute-start(bf16[1152,128]{1,0:T(8,128)(2,1)S(1)} %get-tuple-element.50), channel_id=1, source_target_pairs={{0,20},{1,21},{2,22},{3,23},{4,16},{5,17},{6,18},{7,19},{8,28},{9,... | collective-permute-start | bytes 884744 | tf_op jit(solution)/shard_map/ppermute | solution.py:63
  95.9 12.5 %collective-permute-start.23 = (bf16[288,128]{1,0:T(8,128)(2,1)S(1)}, bf16[288,128]{1,0:T(8,128)(2,1)S(1)}, u32[]{:S(2)}, u32[]{:S(2)}) collective-permute-start(bf16[288,128]{1,0:T(8,128)(2,1)S(1)} %get-tuple-element.74), channel_id=1, source_target_pairs={{0,3},{1,0},{2,1},{3,2},{4,7},{5,4},{6,5},{7,6},{8,11},{9,8},{10,9... | collective-permute-start | bytes 221192 | tf_op jit(solution)/shard_map/ppermute | solution.py:63
  99.1 10.1 %collective-permute-start.25 = (bf16[288,128]{1,0:T(8,128)(2,1)S(1)}, bf16[288,128]{1,0:T(8,128)(2,1)S(1)}, u32[]{:S(2)}, u32[]{:S(2)}) collective-permute-start(bf16[288,128]{1,0:T(8,128)(2,1)S(1)} %get-tuple-element.72), channel_id=1, source_target_pairs={{0,1},{1,2},{2,3},{3,0},{4,5},{5,6},{6,7},{7,4},{8,9},{9,10},{10,1... | collective-permute-start | bytes 221192 | tf_op jit(solution)/shard_map/ppermute | solution.py:63
  99.1 10.1 %collective-permute-start.24 = (bf16[288,128]{1,0:T(8,128)(2,1)S(1)}, bf16[288,128]{1,0:T(8,128)(2,1)S(1)}, u32[]{:S(2)}, u32[]{:S(2)}) collective-permute-start(bf16[288,128]{1,0:T(8,128)(2,1)S(1)} %get-tuple-element.73), channel_id=1, source_target_pairs={{0,2},{1,3},{2,0},{3,1},{4,6},{5,7},{6,4},{7,5},{8,10},{9,11},{10,... | collective-permute-start | bytes 221192 | tf_op jit(solution)/shard_map/ppermute | solution.py:63
  106.5 11.8 %collective-permute-start.22 = (bf16[1024,128]{1,0:T(8,128)(2,1)S(1)}, bf16[1024,128]{1,0:T(8,128)(2,1)S(1)}, u32[]{:S(2)}, u32[]{:S(2)}) collective-permute-start(bf16[1024,128]{1,0:T(8,128)(2,1)S(1)} %get-tuple-element.55), channel_id=1, source_target_pairs={{0,1},{1,2},{2,3},{3,0},{4,5},{5,6},{6,7},{7,4},{8,9},{9,10},{10,1... | collective-permute-start | bytes 786440 | tf_op jit(solution)/shard_map/ppermute | solution.py:63
  106.5 11.8 %collective-permute-start.21 = (bf16[1024,128]{1,0:T(8,128)(2,1)S(1)}, bf16[1024,128]{1,0:T(8,128)(2,1)S(1)}, u32[]{:S(2)}, u32[]{:S(2)}) collective-permute-start(bf16[1024,128]{1,0:T(8,128)(2,1)S(1)} %get-tuple-element.56), channel_id=1, source_target_pairs={{0,2},{1,3},{2,0},{3,1},{4,6},{5,7},{6,4},{7,5},{8,10},{9,11},{10,... | collective-permute-start | bytes 786440 | tf_op jit(solution)/shard_map/ppermute | solution.py:63
  108.4 9.9 %collective-permute-start.20 = (bf16[1024,128]{1,0:T(8,128)(2,1)S(1)}, bf16[1024,128]{1,0:T(8,128)(2,1)S(1)}, u32[]{:S(2)}, u32[]{:S(2)}) collective-permute-start(bf16[1024,128]{1,0:T(8,128)(2,1)S(1)} %get-tuple-element.57), channel_id=1, source_target_pairs={{0,3},{1,0},{2,1},{3,2},{4,7},{5,4},{6,5},{7,6},{8,11},{9,8},{10,9... | collective-permute-start | bytes 786440 | tf_op jit(solution)/shard_map/ppermute | solution.py:63
  109.4 3.8 %collective-permute-start.26 = (bf16[2,32,128]{2,1,0:T(8,128)(2,1)S(1)}, bf16[2,32,128]{2,1,0:T(8,128)(2,1)S(1)}, u32[]{:S(2)}, u32[]{:S(2)}) collective-permute-start(bf16[2,32,128]{2,1,0:T(8,128)(2,1)S(1)} %dynamic-slice_bitcast_fusion.10), channel_id=1, source_target_pairs={{0,32},{1,33},{2,34},{3,35},{4,36},{5,37},{6,38},{7,39},{8,40},{9,... | collective-permute-start | bytes 49160 | tf_op jit(solution)/shard_map/ppermute | solution.py:63
  113.2 4.5 %collective-permute-start.27 = (f32[32,128]{1,0:T(8,128)S(1)}, f32[32,128]{1,0:T(8,128)S(1)}, u32[]{:S(2)}, u32[]{:S(2)}) collective-permute-start(f32[32,128]{1,0:T(8,128)S(1)} %dynamic-slice_bitcast_fusion.9), channel_id=1, source_target_pairs={{0,64},{1,65},{2,66},{3,67},{4,68},{5,69},{6,70},{7,71},{8,72},{9,... | collective-permute-start | bytes 49160 | tf_op jit(solution)/shard_map/ppermute | solution.py:63

commit v3 on v2

--- a/solution.py
+++ b/solution.py
@@ -67,16 +67,17 @@
     return lax.dot_general(a, b, dims, preferred_element_type=F32)
 
 
-def grads_kernel(shift, members, first, last, scale, received, at_ref, stats_ref, c0_ref, c1_ref, c2_ref, c3_ref, *rest):
-    parts = members // 4
+def grads_kernel(halves, blocks, first, last, scale, received, at_ref, stats_ref, c0_ref, c1_ref, c2_ref, c3_ref, *rest):
+    parts = len(halves)
+    members = 4 * parts
     rest = list(rest)
-    kv_refs = [rest.pop(0) for _ in range(parts)]
+    kv_refs = [rest.pop(0) for _ in range(blocks)]
     dq_in = None if first else rest.pop(0)
     held = [rest.pop(0) for _ in range(received)]
-    dq_out = rest.pop(0)
+    dq_outs = [rest.pop(0) for _ in range(4 if last else 1)]
     outs = [rest.pop(0) for _ in range(parts)]
     chunk, keys, values, dkeys, dvalues, stage, meta_ref = rest[:7]
-    dq = rest[7] if last else dq_out
+    dq = rest[7] if last else dq_outs[0]
     core, head, block, z = [at_ref[64 + i] for i in range(4)]
 
     def runs_of(from_b, from_h, from_z):
@@ -84,22 +85,21 @@
         one, two = at_ref[2 * c], at_ref[2 * c + 1]
         return jnp.minimum(one, two), jnp.where(one > two, 1, 0)
 
-    if members == 8:
-        places_in = [(zz * 1152, zz, e) for zz in range(2) for e in range(4)]
-    else:
-        places_in = [(0, 0 if last else 1, e) for e in range(4)]
-    found = [runs_of((block - shift) & 3, (head - e) & 3, (z + zz) & 1) for _, zz, e in places_in]
+    places_in = [(part, e) for part in range(parts) for e in range(4)]
+    found = [
+        runs_of((block - halves[part][0]) & 3, (head - e) & 3, (z + halves[part][1]) & 1) for part, e in places_in
+    ]
     for j, (early_j, swap_j) in enumerate(found):
         rank = 0
         for i, (early_i, _) in enumerate(found):
             if i != j:
                 rank = rank + jnp.where(early_i < early_j, 1, 0)
-        start = places_in[j][0] + 288 * places_in[j][2]
+        start = 1152 * places_in[j][0] + 288 * places_in[j][1]
         meta_ref[rank] = early_j
-        meta_ref[8 + rank] = start + RUN * swap_j
-        meta_ref[16 + rank] = start + RUN * (1 - swap_j)
+        meta_ref[16 + rank] = start + RUN * swap_j
+        meta_ref[32 + rank] = start + RUN * (1 - swap_j)
     for e in range(4):
-        meta_ref[24 + e], meta_ref[28 + e] = runs_of(block, (head - e) & 3, z)
+        meta_ref[48 + e], meta_ref[52 + e] = runs_of(block, (head - e) & 3, z)
     rows = 512
     prompt = 16 * members
     for i, ref in enumerate((c0_ref, c1_ref, c2_ref, c3_ref)):
@@ -113,11 +113,13 @@
 
     def places(u):
         for late in range(2):
-            at = meta_ref[8 + 8 * late + u]
+            at = meta_ref[16 + 16 * late + u]
             yield at, pl.ds(prompt + (late * members + u) * RUN, RUN)
 
-    for part in range(parts):
-        stage[pl.ds(part * 1152, 1152), :] = kv_refs[part][...]
+    at = 0
+    for ref in kv_refs:
+        stage[pl.ds(at, ref.shape[0]), :] = ref[...]
+        at += ref.shape[0]
     for e in range(members):
         to = pl.ds(16 * e, 16)
         keys[to, :] = stage[pl.ds(288 * e + 256, 16), :]
@@ -133,11 +135,11 @@
 
     def one_chunk(i, _):
         base = i * 2048
-        early = meta_ref[24 + i]
-        early_half = meta_ref[28 + i]
+        early = meta_ref[48 + i]
+        early_half = meta_ref[52 + i]
         piece = stats_ref[pl.ds(pl.multiple_of(i * 48, 16), 48), :].astype(F32)
 
-        def tile(half, key_row, count, marks):
+        def tile(half, spans, marks):
             q_rows = pl.ds(pl.multiple_of(base + half * rows, 16), rows)
             g_rows = pl.ds(pl.multiple_of(base + 1024 + half * rows, 16), rows)
             stats = []
@@ -146,19 +148,27 @@
                 picked = jnp.where(half == 0, total[0:4], total[4:8])
                 stats.append(jnp.concatenate([picked[k : k + 1] for k in range(4)], axis=1))
             lse2, delta = stats
-            k_rows = pl.ds(key_row, count)
-            kt = keys[k_rows, :]
+            spans = [pl.ds(at, count) for at, count in spans]
+            kt = jnp.concatenate([keys[span, :] for span in spans], axis=0)
+            vt = jnp.concatenate([values[span, :] for span in spans], axis=0)
             q = chunk[q_rows, :]
             g = chunk[g_rows, :]
-            p = jnp.exp2(dot(kt, q, NT) * (scale * LOG2E) - lse2)
+            s = dot(kt, q, NT)
+            dp = dot(vt, g, NT)
+            p = jnp.exp2(s * (scale * LOG2E) - lse2)
             if marks:
                 cut = [p[: marks[0][0]]] if marks[0][0] else []
                 for at, limit in marks:
                     cut.append(jnp.where(slope <= limit, p[at : at + RUN], 0.0))
                 p = jnp.concatenate(cut, axis=0)
-            ds = (p * (dot(values[k_rows, :], g, NT) - delta)).astype(BF16)
-            dvalues[k_rows, :] += dot(p.astype(BF16), g, NN)
-            dkeys[k_rows, :] += dot(ds, q, NN)
+            ds = (p * (dp - delta)).astype(BF16)
+            dv = dot(p.astype(BF16), g, NN)
+            dk = dot(ds, q, NN)
+            at = 0
+            for span in spans:
+                dvalues[span, :] += dv[at : at + span.size]
+                dkeys[span, :] += dk[at : at + span.size]
+                at += span.size
             acc = pl.ds(pl.multiple_of((2 * i + half) * 128, 128), 128)
             dq[acc, :] += dot(kt, ds, TN)
 
@@ -170,28 +180,31 @@
 
         late_half = 1 - early_half
         late_row = prompt + members * RUN
-        tile(late_half, 0, late_row, [])
-        tile(early_half, 0, prompt + 256, [(prompt + RUN * u, early_limit(u)) for u in range(4)])
-        if members == 8:
-            seen = 0
-            for u in range(8):
-                seen = seen + jnp.where(meta_ref[u] <= early, 1, 0)
-            more = seen > 4
+        top = members - 4
+        tile(
+            late_half,
+            [(0, late_row), (late_row + RUN * top, 256)],
+            [(late_row + RUN * u, late_limit(top + u)) for u in range(4)],
+        )
+        tile(early_half, [(0, prompt + 256)], [(prompt + RUN * u, early_limit(u)) for u in range(4)])
+        seen = 0
+        for u in range(members):
+            seen = seen + jnp.where(meta_ref[u] <= early, 1, 0)
+        for i_tile in range(1, parts):
+            more = seen > 4 * i_tile
+            low, high = 4 * i_tile, 4 * (i_tile - 1)
             tile(
                 jnp.where(more, early_half, late_half),
-                pl.multiple_of(jnp.where(more, prompt + 256, late_row), 16),
-                256,
-                [(RUN * u, jnp.where(more, early_limit(4 + u), late_limit(u))) for u in range(4)],
+                [(pl.multiple_of(jnp.where(more, prompt + RUN * low, late_row + RUN * high), 16), 256)],
+                [(RUN * u, jnp.where(more, early_limit(low + u), late_limit(high + u))) for u in range(4)],
             )
-        top = members - 4
-        tile(late_half, late_row + RUN * top, 256, [(RUN * u, late_limit(top + u)) for u in range(4)])
         return 0
 
-    lax.fori_loop(0, 4, one_chunk, 0)
+    lax.fori_loop(0, 4, one_chunk, 0, unroll=(4, 2, 1, 1)[parts - 1])
 
     if last:
         for i in range(8):
-            dq_out[pl.ds(i * rows, rows), :] = (dq[pl.ds(i * 128, 128), :].T * scale).astype(BF16)
+            dq_outs[i // 2][pl.ds(i % 2 * rows, rows), :] = (dq[pl.ds(i * 128, 128), :].T * scale).astype(BF16)
 
     wide = outs[0].dtype
     total = outs[0] if last else stage
@@ -210,15 +223,15 @@
         outs[0][...] += ref[...].astype(F32)
 
 
-def block_grads(shift, first, last, scale, at, stats, chunks, kv, dq, held):
-    parts = len(kv)
+def block_grads(halves, first, last, scale, at, stats, chunks, kv, dq, held):
+    parts = len(halves)
     members = 4 * parts
     vmem = pl.BlockSpec(memory_space=pltpu.VMEM)
     smem = pl.BlockSpec(memory_space=pltpu.SMEM)
     operands = [at, stats, *chunks, *kv] + ([] if first else [dq]) + list(held)
-    specs = [smem] + [vmem] * (5 + parts + (0 if first else 1))
+    specs = [smem] + [vmem] * (5 + len(kv) + (0 if first else 1))
     specs += [vmem if last else pl.BlockSpec(memory_space=pl.ANY)] * len(held)
-    dq_shape = jax.ShapeDtypeStruct((4096, 128), BF16) if last else jax.ShapeDtypeStruct((1024, 512), F32)
+    dq_shapes = [jax.ShapeDtypeStruct((1024, 128), BF16)] * 4 if last else [jax.ShapeDtypeStruct((1024, 512), F32)]
     sorted_rows = 144 * members
     scratch = [
         pltpu.VMEM((4 * 2048, 128), BF16),
@@ -227,15 +240,15 @@
         pltpu.VMEM((sorted_rows, 128), F32),
         pltpu.VMEM((sorted_rows, 128), F32),
         pltpu.VMEM((1152 * parts, 128), BF16),
-        pltpu.SMEM((32,), jnp.int32),
+        pltpu.SMEM((64,), jnp.int32),
     ]
     if last:
         scratch.append(pltpu.VMEM((1024, 512), F32))
     return pl.pallas_call(
-        functools.partial(grads_kernel, shift, members, first, last, scale, len(held)),
-        out_shape=[dq_shape] + [jax.ShapeDtypeStruct((1152, 128), F32 if last else BF16)] * parts,
+        functools.partial(grads_kernel, halves, len(kv), first, last, scale, len(held)),
+        out_shape=dq_shapes + [jax.ShapeDtypeStruct((1152, 128), F32 if last else BF16)] * parts,
         in_specs=specs,
-        out_specs=[vmem] * (1 + parts),
+        out_specs=[vmem] * (len(dq_shapes) + parts),
         scratch_shapes=scratch,
         compiler_params=pltpu.CompilerParams(vmem_limit_bytes=32 * 2**20),
         cost_estimate=pl.CostEstimate(
@@ -244,13 +257,38 @@
     )(*operands)
 
 
-def chunks_kernel(at_ref, x_ref, kv_ref, p0_ref, p1_ref, p2_ref, p3_ref, o0_ref, o1_ref, o2_ref, o3_ref, prompts):
-    head, r = at_ref[65], at_ref[68]
+def chunks_kernel(
+    me_ref,
+    order_ref,
+    lengths_ref,
+    lse_ref,
+    delta_ref,
+    kv_ref,
+    p0_ref,
+    p1_ref,
+    p2_ref,
+    p3_ref,
+    o0_ref,
+    o1_ref,
+    o2_ref,
+    o3_ref,
+    at_ref,
+    prompts,
+):
+    head, r, c = me_ref[1], me_ref[4], me_ref[5]
+    for i in range(64):
+        at_ref[i] = order_ref[0, RUN * i] // RUN
+    for i in range(5):
+        at_ref[64 + i] = me_ref[i]
+    slots = lax.broadcasted_iota(jnp.int32, (128, 32), 0)
+    run = jnp.where(slots < RUN, order_ref[0, 128 * c], order_ref[0, 128 * c + RUN])
+    live = run + (slots & (RUN - 1)) < lengths_ref[0]
+    stats = (jnp.where(live, lse_ref[...] * LOG2E, 1e30), delta_ref[...])
     for i, ref in enumerate((p0_ref, p1_ref, p2_ref, p3_ref)):
         prompts[i] = ref[...]
     terms = []
     for j in range(2):
-        rest = x_ref[j]
+        rest = stats[j]
         for _ in range(3):
             term = rest.astype(BF16)
             terms.append(term)
@@ -276,17 +314,18 @@
     return lax.dynamic_index_in_dim(stacked, index, 0, keepdims=False)
 
 
-def make_chunks(at, x, kv, prompts):
+def make_chunks(me, order, lengths, lse, delta, kv, prompts):
     vmem = pl.BlockSpec(memory_space=pltpu.VMEM)
+    smem = pl.BlockSpec(memory_space=pltpu.SMEM)
     return pl.pallas_call(
         chunks_kernel,
-        out_shape=[jax.ShapeDtypeStruct((336, 128), BF16)] * 4,
-        in_specs=[pl.BlockSpec(memory_space=pltpu.SMEM)] + [vmem] * 6,
-        out_specs=[vmem] * 4,
+        out_shape=[jax.ShapeDtypeStruct((336, 128), BF16)] * 4 + [jax.ShapeDtypeStruct((72,), jnp.int32)],
+        in_specs=[smem] * 3 + [vmem] * 7,
+        out_specs=[vmem] * 4 + [smem],
         scratch_shapes=[pltpu.VMEM((4, 32, 128), BF16)],
         compiler_params=pltpu.CompilerParams(vmem_limit_bytes=16 * 2**20),
         cost_estimate=pl.CostEstimate(flops=200_000_000, bytes_accessed=1_000_000, transcendentals=0),
-    )(at, x, kv, *prompts)
+    )(me, order, lengths, lse, delta, kv, *prompts)
 
 
 def shards(
@@ -316,43 +355,52 @@
         do = lax.dynamic_index_in_dim(g_four, g, 1, keepdims=False).reshape(1024, 128)
         return jnp.concatenate([q, do], axis=0)
 
-    chunks = [q_chunk(head)] + [send(q_chunk((head + s) % 4), along_heads(s)) for s in (1, 3)]
+    chunks = [send(q_chunk((head + s) % 4), along_heads(s)) for s in (1, 3)]
     far_chunk = q_chunk((head + 2) % 4)
 
     prompt = jnp.concatenate([prompt_keys[:, 0], prompt_values[:, 0]], axis=0)
     prompts = [prompt] + [send(prompt, along_resp(s)) for s in (1, 2, 3)]
-    query_pos = lax.dynamic_slice_in_dim(order[0], c * 128, 128)
-    live = query_pos < lengths[0]
     delta = jnp.sum(grad_out[0].astype(F32) * attn_out[0].astype(F32), axis=-1)
-    x_stats = jnp.stack([jnp.where(live[:, None], logsumexp[0] * LOG2E, 1e30), delta])
     resp_kv = jnp.stack([resp_keys[0], resp_values[0]]).transpose(2, 0, 1, 3).reshape(4, 256, 128)
-    run_pos = order[0].reshape(64, RUN)[:, 0] // RUN
-    at = jnp.concatenate([run_pos, jnp.stack([core, head, block, z, r])])
-    pieces = make_chunks(at, x_stats, resp_kv, prompts)
+    me = jnp.stack([core, head, block, z, r, c]).astype(jnp.int32)
+    *pieces, at = make_chunks(me, order, lengths, logsumexp[0], delta, resp_kv, prompts)
     pieces = [pieces[0]] + [send(pieces[s], along_heads(s)) for s in (1, 2, 3)]
     near = jnp.concatenate([piece[:288] for piece in pieces], axis=0)
     stats = jnp.concatenate([piece[288:] for piece in pieces], axis=0)
     near, far_chunk, *chunks = lax.optimization_barrier((near, far_chunk, *chunks))
-    chunks = [chunks[0], chunks[1], send(far_chunk, along_heads(2)), chunks[2]]
+    q_own, _ = lax.optimization_barrier((head, near))
+    chunks = [q_chunk(q_own), chunks[0], send(far_chunk, along_heads(2)), chunks[1]]
     far = send(near, along_z())
     own = jnp.concatenate([near, far], axis=0)
-    kv_blocks = {s: send(own, along_blocks(s)) for s in (1, 3, 2)}
-
-    dq, sent = block_grads(0, True, False, scale, at, stats, chunks, [far], None, [])
-    got = {0: [send(sent, along_z())]}
-    for i, s in enumerate((1, 3, 2)):
-        held = got[0] if i == 1 else got[1] if i == 2 else []
-        half = kv_blocks[s]
-        dq, near_part, far_part = block_grads(
-            s, False, False, scale, at, stats, chunks, [half[:1152], half[1152:]], dq, held
-        )
-        got[s] = [send(near_part, along_blocks(4 - s)), send(far_part, along_both(4 - s))]
-    dq, totals = block_grads(0, False, True, scale, at, stats, chunks, [near], dq, got[0] + got[1] + got[3])
-
-    dq, *late = lax.optimization_barrier((dq, *got[2]))
-    back = [dq[:1024]]
-    for s in (1, 2, 3):
-        back.append(send(dq[1024 * s : 1024 * (s + 1)], along_heads(4 - s)))
+    kv_blocks = {s: send(own, along_blocks(s)) for s in (1, 3)}
+
+    dq, sent = block_grads([(0, 1)], True, False, scale, at, stats, chunks, [far], None, [])
+    own, sent = lax.optimization_barrier((own, sent))
+    kv_blocks[2] = send(own, along_blocks(2))
+    got = [send(sent, along_z())]
+    dq, near_1, far_1, near_3, far_3 = block_grads(
+        [(1, 0), (1, 1), (3, 0), (3, 1)],
+        False,
+        False,
+        scale,
+        at,
+        stats,
+        chunks,
+        [kv_blocks[1], kv_blocks[3]],
+        dq,
+        [],
+    )
+    for s, near_part, far_part in ((1, near_1, far_1), (3, near_3, far_3)):
+        got += [send(near_part, along_blocks(4 - s)), send(far_part, along_both(4 - s))]
+    dq, near_part, far_part = block_grads(
+        [(2, 0), (2, 1)], False, False, scale, at, stats, chunks, [kv_blocks[2]], dq, got[:1]
+    )
+    late = [send(near_part, along_blocks(2)), send(far_part, along_both(2))]
+    *dq, totals = block_grads([(0, 0)], False, True, scale, at, stats, chunks, [near], dq, got)
+
+    *dq, late_near, late_far = lax.optimization_barrier((*dq, *late))
+    late = [late_near, late_far]
+    back = [dq[0]] + [send(dq[s], along_heads(4 - s)) for s in (1, 2, 3)]
     back = jnp.stack(back).reshape(4, 128, 8, 128)
     turn = (4 - head) % 4
     grad_queries = lax.dynamic_slice_in_dim(jnp.concatenate([back, back[:3]], axis=0), turn, 4, 0)
@@ -371,7 +419,9 @@
     mine_pair = pick(parts.reshape(2, 2, 32, 128).transpose(1, 0, 2, 3), core).astype(F32)
     theirs = pick(parts.reshape(2, 2, 32, 128).transpose(1, 0, 2, 3), 1 - core)
     mine_pair = mine_pair + send(theirs, across_cores()).astype(F32)
-    prompt_sum = pick(mine_pair, r // 2) + send(pick(mine_pair, 1 - r // 2), across_z_hi())
+    theirs = send(pick(mine_pair, 1 - r // 2), across_z_hi())
+    theirs, grad_queries = lax.optimization_barrier((theirs, grad_queries))
+    prompt_sum = pick(mine_pair, r // 2) + theirs
     prompt_sum = prompt_sum.astype(BF16).reshape(2, 16, 128)
     return (
         grad_queries,

time: 121 us -> 114 us (0.942)
  Pallas kernels: 44 us -> 40 us
  local copies, waits for them, and re-layouts: 9.6 us -> 5.82 us
  starting transfers between devices: 47.7 us -> 51.1 us
  other arithmetic: 7.02 us -> 4.3 us
    pallas_call x5 -> x4, Pallas kernels: 42.4 us -> 37.3 us  [block_grads(): pl.pallas_call(functools.partial(grads_kernel, halves, len(kv), first, la...]
    ppermute x28, starting transfers between devices: 47.7 us -> 51.1 us  [send(): return lax.ppermute(value, AXES, pairs)]
    unnamed x30 -> x26, local copies, waits for them, and re-layouts: 2.36 us -> 0.42 us
    reshape x1 -> x2, local copies, waits for them, and re-layouts: 2.52 us -> 1.15 us  [q_chunk(): lax.dynamic_index_in_dim(g_four, g, 1, keepdims=False).reshape(1024, 128)]
  transfers between devices with their start and end apart: 28 -> 28, of which waited for: 6 -> 7; matrix products, arithmetic and copies ran while one was open for 11% -> 8% of each run, Pallas kernels for 37% -> 35%
where the time goes in v3:
time: 114 us; the launch traced here: 113 us
  starting transfers between devices  51.1 us (45%)
  Pallas kernels  40 us (35%)
  waiting for transfers between devices  10.4 us (9%)
  local copies, waits for them, and re-layouts  5.82 us (5%)
  other arithmetic  4.3 us (4%)
  between operations  1.76 us (2%)
    ppermute x28, starting transfers between devices, send(): return lax.ppermute(value, AXES, pairs)  51.1 us
    pallas_call x4, Pallas kernels, block_grads(): pl.pallas_call(functools.partial(grads_kernel, halves, len(kv), first, la...  37.3 us
    ppermute x28, waiting for transfers between devices, send(): return lax.ppermute(value, AXES, pairs)  10.4 us
    pallas_call x1, Pallas kernels, make_chunks(): pl.pallas_call(chunks_kernel, out_shape=[jax.ShapeDtypeStruct((336, 128),...  2.67 us
    concatenate x4, other arithmetic, q_chunk(): return jnp.concatenate([q, do], axis=0)  2.55 us
  transfers between devices with their start and end apart: 28, of which 7 were waited for; matrix products, arithmetic and copies ran while one was open for 8% of the time, Pallas kernels for 35%

profile of v3, /device:TPU:1, one launch (start us, length us, event | category | flops | bytes accessed | tf_op | source)
XLA Modules:
  0.0 113.3 jit_solution(6933253898902358820)
XLA Ops:
  0.6 0.8 pad_maximum_fusion.6.p0_ref
  1.4 1.4 %collective-permute-start.2 = (bf16[32,128]{1,0:T(8,128)(2,1)S(1)}, bf16[32,128]{1,0:T(8,128)(2,1)S(1)}, u32[]{:S(2)}, u32[]{:S(2)}) collective-permute-start(bf16[32,128]{1,0:T(8,128)(2,1)S(1)} %pad_maximum_fusion.6.p0_ref), channel_id=1, source_target_pairs={{0,96},{1,97},{2,98},{3,99},{4,100},{5,101},{6,102},{7,103},{8,104... | collective-permute-start | bytes 24584 | tf_op jit(solution)/shard_map/ppermute | solution.py:63
  2.9 3.7 %collective-permute-start.1 = (bf16[32,128]{1,0:T(8,128)(2,1)S(1)}, bf16[32,128]{1,0:T(8,128)(2,1)S(1)}, u32[]{:S(2)}, u32[]{:S(2)}) collective-permute-start(bf16[32,128]{1,0:T(8,128)(2,1)S(1)} %pad_maximum_fusion.6.p0_ref), channel_id=1, source_target_pairs={{0,64},{1,65},{2,66},{3,67},{4,68},{5,69},{6,70},{7,71},{8,72},{9,... | collective-permute-start | bytes 24584 | tf_op jit(solution)/shard_map/ppermute | solution.py:63
  6.5 2.9 %collective-permute-start = (bf16[32,128]{1,0:T(8,128)(2,1)S(1)}, bf16[32,128]{1,0:T(8,128)(2,1)S(1)}, u32[]{:S(2)}, u32[]{:S(2)}) collective-permute-start(bf16[32,128]{1,0:T(8,128)(2,1)S(1)} %pad_maximum_fusion.6.p0_ref), channel_id=1, source_target_pairs={{0,32},{1,33},{2,34},{3,35},{4,36},{5,37},{6,38},{7,39},{8,40},{9,... | collective-permute-start | bytes 24584 | tf_op jit(solution)/shard_map/ppermute | solution.py:63
  9.4 1.2 %dynamic-slice_bitcast_fusion.4 = (bf16[1024,128]{1,0:T(8,128)(2,1)S(1)}, bf16[1024,128]{1,0:T(8,128)(2,1)S(1)}, bf16[1024,128]{1,0:T(8,128)(2,1)S(1)}) fusion(bf16[128,4,8,128]{3,2,1,0:T(8,128)(2,1)} %bitcast.101, s32[]{:T(128)S(6)} %select_n.95, s32[]{:T(128)S(6)} %select_n.93, s32[]{:T(128)S(6)} %select_n.91), kind=kLoop, calls=%fused_computation.21 | loop fusion | bytes 1572876 | tf_op jit(solution)/shard_map/reshape | solution.py:354
  10.6 0.0 copy-start.2
  10.6 0.1 dynamic-slice_bitcast_fusion.3
  10.7 0.8 pad_maximum_fusion.1
  11.6 1.2 %collective-permute-start.6 = (bf16[2048,128]{1,0:T(8,128)(2,1)}, bf16[2048,128]{1,0:T(8,128)(2,1)S(1)}, u32[]{:S(2)}, u32[]{:S(2)}) collective-permute-start(bf16[2048,128]{1,0:T(8,128)(2,1)} %pad_maximum_fusion.1), channel_id=1, source_target_pairs={{0,1},{1,2},{2,3},{3,0},{4,5},{5,6},{6,7},{7,4},{8,9},{9,10},{10,1... | collective-permute-start | bytes 1572872 | tf_op jit(solution)/shard_map/ppermute | solution.py:63
  12.8 0.8 pad_maximum_fusion.2
  13.6 1.5 %collective-permute-start.7 = (bf16[2048,128]{1,0:T(8,128)(2,1)}, bf16[2048,128]{1,0:T(8,128)(2,1)S(1)}, u32[]{:S(2)}, u32[]{:S(2)}) collective-permute-start(bf16[2048,128]{1,0:T(8,128)(2,1)} %pad_maximum_fusion.2), channel_id=1, source_target_pairs={{0,3},{1,0},{2,1},{3,2},{4,7},{5,4},{6,5},{7,6},{8,11},{9,8},{10,9... | collective-permute-start | bytes 1572872 | tf_op jit(solution)/shard_map/ppermute | solution.py:63
  15.1 0.6 multiply_reduce_fusion.delta_ref
  15.7 0.2 maximum_bitcast_fusion
  16.6 0.1 copy.15
  16.8 0.1 stack.53.me_ref
  16.9 0.0 collective-permute-done.p1_ref
  16.9 2.7 %shard_map.137 = (bf16[336,128]{1,0:T(8,128)(2,1)S(1)}, bf16[336,128]{1,0:T(8,128)(2,1)S(1)}, bf16[336,128]{1,0:T(8,128)(2,1)S(1)}, bf16[336,128]{1,0:T(8,128)(2,1)S(1)}, s32[72]{0:T(128)S(1)}) custom-call(s32[6]{0:T(128)S(1)} %stack.53.me_ref, s32[1,4096]{1,0:T(1,128)S(1)} %copy-done, s32[1]{0:T(128)S(6)} %copy.51.lengths_ref, f32[128,32]{1,0:T(8,128)S(1)} %bitcast.97, ...), custom_call_target="tpu_custom_call" | custom-call | flops 200000000 | bytes 1000000 | tf_op jit(solution)/shard_map/pallas_call | solution.py:320
  19.6 0.1 collective-permute-start.3
  19.6 2.4 %collective-permute-start.4 = (bf16[336,128]{1,0:T(8,128)(2,1)S(1)}, bf16[336,128]{1,0:T(8,128)(2,1)S(1)}, u32[]{:S(2)}, u32[]{:S(2)}) collective-permute-start(bf16[336,128]{1,0:T(8,128)(2,1)S(1)} %get-tuple-element.43), channel_id=1, source_target_pairs={{0,2},{1,3},{2,0},{3,1},{4,6},{5,7},{6,4},{7,5},{8,10},{9,11},{10,... | collective-permute-start | bytes 258056 | tf_op jit(solution)/shard_map/ppermute | solution.py:63
  22.1 1.2 %collective-permute-start.5 = (bf16[336,128]{1,0:T(8,128)(2,1)S(1)}, bf16[336,128]{1,0:T(8,128)(2,1)S(1)}, u32[]{:S(2)}, u32[]{:S(2)}) collective-permute-start(bf16[336,128]{1,0:T(8,128)(2,1)S(1)} %get-tuple-element.44), channel_id=1, source_target_pairs={{0,3},{1,0},{2,1},{3,2},{4,7},{5,4},{6,5},{7,6},{8,11},{9,8},{10,9... | collective-permute-start | bytes 258056 | tf_op jit(solution)/shard_map/ppermute | solution.py:63
  23.2 0.9 pad_maximum_fusion
  24.1 1.0 collective-permute-done.3
  25.2 0.5 collective-permute-done.5
  25.7 0.0 collective-permute-done.7.c3_ref
  25.8 0.8 collective-permute-start.9
  26.6 1.8 %collective-permute-start.8 = (bf16[2048,128]{1,0:T(8,128)(2,1)}, bf16[2048,128]{1,0:T(8,128)(2,1)S(1)}, u32[]{:S(2)}, u32[]{:S(2)}) collective-permute-start(bf16[2048,128]{1,0:T(8,128)(2,1)} %pad_maximum_fusion), channel_id=1, source_target_pairs={{0,2},{1,3},{2,0},{3,1},{4,6},{5,7},{6,4},{7,5},{8,10},{9,11},{10,... | collective-permute-start | bytes 1572872 | tf_op jit(solution)/shard_map/ppermute | solution.py:63
  28.4 1.0 dynamic-slice_bitcast_fusion.1
  29.4 5.1 %collective-permute-done.9.rest_0_ = bf16[1152,128]{1,0:T(8,128)(2,1)S(1)} collective-permute-done((bf16[1152,128]{1,0:T(8,128)(2,1)S(1)}, bf16[1152,128]{1,0:T(8,128)(2,1)S(1)}, u32[]{:S(2)}, u32[]{:S(2)}) %collective-permute-start.9) | collective-permute-done | bytes 294944 | tf_op jit(solution)/shard_map/ppermute | solution.py:63
  34.6 3.0 %collective-permute-start.12 = (bf16[2304,128]{1,0:T(8,128)(2,1)S(1)}, bf16[2304,128]{1,0:T(8,128)(2,1)S(1)}, u32[]{:S(2)}, u32[]{:S(2)}) collective-permute-start(bf16[2304,128]{1,0:T(8,128)(2,1)S(1)} %constant_dynamic-update-slice_fusion), channel_id=1, source_target_pairs={{0,24},{1,25},{2,26},{3,27},{4,28},{5,29},{6,30},{7,31},{8,0},{9,1... | collective-permute-start | bytes 1769480 | tf_op jit(solution)/shard_map/ppermute | solution.py:63
  37.6 0.0 collective-permute-start.11
  37.7 0.0 collective-permute-done.8.c2_ref
  37.7 5.6 %shard_map.138 = (f32[1024,512]{1,0:T(8,128)S(1)}, bf16[1152,128]{1,0:T(8,128)(2,1)S(1)}) custom-call(s32[72]{0:T(128)S(1)} %get-tuple-element.40.at_ref, bf16[192,128]{1,0:T(8,128)(2,1)S(1)} %pad_maximum_fusion.5.stats_ref, bf16[2048,128]{1,0:T(8,128)(2,1)S(1)} %pad_maximum_fusion.3.c0_ref, bf16[2048,128]{1,0:T(8,128)(2,1)S(1)} %collective-permute-done.6.c1_ref, ...), custom_call_target="tpu_custom_call" | custom-call | flops 5000000000 | bytes 8000000 | tf_op jit(solution)/shard_map/pallas_call | solution.py:247
  43.3 0.8 collective-permute-start.13
  44.1 1.5 %collective-permute-start.10 = (bf16[2304,128]{1,0:T(8,128)(2,1)S(1)}, bf16[2304,128]{1,0:T(8,128)(2,1)S(1)}, u32[]{:S(2)}, u32[]{:S(2)}) collective-permute-start(bf16[2304,128]{1,0:T(8,128)(2,1)S(1)} %constant_dynamic-update-slice_fusion), channel_id=1, source_target_pairs={{0,16},{1,17},{2,18},{3,19},{4,20},{5,21},{6,22},{7,23},{8,24},{9,... | collective-permute-start | bytes 1769480 | tf_op jit(solution)/shard_map/ppermute | solution.py:63
  45.6 2.3 %collective-permute-done.11.rest_0_ = bf16[2304,128]{1,0:T(8,128)(2,1)S(1)} collective-permute-done((bf16[2304,128]{1,0:T(8,128)(2,1)S(1)}, bf16[2304,128]{1,0:T(8,128)(2,1)S(1)}, u32[]{:S(2)}, u32[]{:S(2)}) %collective-permute-start.11) | collective-permute-done | bytes 589856 | tf_op jit(solution)/shard_map/ppermute | solution.py:63
  47.9 16.2 %shard_map.139 = (f32[1024,512]{1,0:T(8,128)S(1)}, bf16[1152,128]{1,0:T(8,128)(2,1)S(1)}, bf16[1152,128]{1,0:T(8,128)(2,1)S(1)}, bf16[1152,128]{1,0:T(8,128)(2,1)S(1)}, bf16[1152,128]{1,0:T(8,128)(2,1)S(1)}) custom-call(s32[72]{0:T(128)S(1)} %get-tuple-element.40.at_ref, bf16[192,128]{1,0:T(8,128)(2,1)S(1)} %pad_maximum_fusion.5.stats_ref, ...), custom_call_target="tpu_custom_call" | custom-call | flops 20000000000 | bytes 8000000 | tf_op jit(solution)/shard_map/pallas_call | solution.py:247
  64.1 0.1 collective-permute-start.14
  64.2 0.5 collective-permute-start.15
  64.7 1.5 %collective-permute-start.16 = (bf16[1152,128]{1,0:T(8,128)(2,1)S(1)}, bf16[1152,128]{1,0:T(8,128)(2,1)S(1)}, u32[]{:S(2)}, u32[]{:S(2)}) collective-permute-start(bf16[1152,128]{1,0:T(8,128)(2,1)S(1)} %get-tuple-element.58), channel_id=1, source_target_pairs={{0,8},{1,9},{2,10},{3,11},{4,12},{5,13},{6,14},{7,15},{8,16},{9,17... | collective-permute-start | bytes 884744 | tf_op jit(solution)/shard_map/ppermute | solution.py:63
  66.1 0.0 collective-permute-done.13.rest_2_
  66.2 1.8 %collective-permute-start.17 = (bf16[1152,128]{1,0:T(8,128)(2,1)S(1)}, bf16[1152,128]{1,0:T(8,128)(2,1)S(1)}, u32[]{:S(2)}, u32[]{:S(2)}) collective-permute-start(bf16[1152,128]{1,0:T(8,128)(2,1)S(1)} %get-tuple-element.59), channel_id=1, source_target_pairs={{0,12},{1,13},{2,14},{3,15},{4,8},{5,9},{6,10},{7,11},{8,20},{9,21... | collective-permute-start | bytes 884744 | tf_op jit(solution)/shard_map/ppermute | solution.py:63
  68.0 9.2 %shard_map.140 = (f32[1024,512]{1,0:T(8,128)S(1)}, bf16[1152,128]{1,0:T(8,128)(2,1)S(1)}, bf16[1152,128]{1,0:T(8,128)(2,1)S(1)}) custom-call(s32[72]{0:T(128)S(1)} %get-tuple-element.40.at_ref, bf16[192,128]{1,0:T(8,128)(2,1)S(1)} %pad_maximum_fusion.5.stats_ref, bf16[2048,128]{1,0:T(8,128)(2,1)S(1)} %pad_maximum_fusion.3.c0_ref, ...), custom_call_target="tpu_custom_call" | custom-call | flops 10000000000 | bytes 8000000 | tf_op jit(solution)/shard_map/pallas_call | solution.py:247
  77.2 1.1 collective-permute-start.18
  78.3 0.0 collective-permute-done.14.rest_3_
  78.3 2.4 %collective-permute-start.19 = (bf16[1152,128]{1,0:T(8,128)(2,1)S(1)}, bf16[1152,128]{1,0:T(8,128)(2,1)S(1)}, u32[]{:S(2)}, u32[]{:S(2)}) collective-permute-start(bf16[1152,128]{1,0:T(8,128)(2,1)S(1)} %get-tuple-element.66), channel_id=1, source_target_pairs={{0,20},{1,21},{2,22},{3,23},{4,16},{5,17},{6,18},{7,19},{8,28},{9,... | collective-permute-start | bytes 884744 | tf_op jit(solution)/shard_map/ppermute | solution.py:63
  80.7 0.0 collective-permute-done.15.rest_4_
  80.7 0.0 collective-permute-done.16.rest_5_
  80.7 0.2 collective-permute-done.17.rest_6_
  80.8 6.4 %shard_map.141 = (bf16[1024,128]{1,0:T(8,128)(2,1)S(1)}, bf16[1024,128]{1,0:T(8,128)(2,1)S(1)}, bf16[1024,128]{1,0:T(8,128)(2,1)S(1)}, bf16[1024,128]{1,0:T(8,128)(2,1)S(1)}, f32[1152,128]{1,0:T(8,128)S(1)}) custom-call(s32[72]{0:T(128)S(1)} %get-tuple-element.40.at_ref, bf16[192,128]{1,0:T(8,128)(2,1)S(1)} %pad_maximum_fusion.5.stats_ref, ...), custom_call_target="tpu_custom_call" | custom-call | flops 5000000000 | bytes 8000000 | tf_op jit(solution)/shard_map/pallas_call | solution.py:247
  87.2 1.0 collective-permute-done.19
  88.2 0.1 add_convert_fusion
  88.4 1.3 %collective-permute-start.22 = (bf16[288,128]{1,0:T(8,128)(2,1)S(1)}, bf16[288,128]{1,0:T(8,128)(2,1)S(1)}, u32[]{:S(2)}, u32[]{:S(2)}) collective-permute-start(bf16[288,128]{1,0:T(8,128)(2,1)S(1)} %get-tuple-element.81), channel_id=1, source_target_pairs={{0,1},{1,2},{2,3},{3,0},{4,5},{5,6},{6,7},{7,4},{8,9},{9,10},{10,1... | collective-permute-start | bytes 221192 | tf_op jit(solution)/shard_map/ppermute | solution.py:63
  89.7 3.2 %collective-permute-start.21 = (bf16[288,128]{1,0:T(8,128)(2,1)S(1)}, bf16[288,128]{1,0:T(8,128)(2,1)S(1)}, u32[]{:S(2)}, u32[]{:S(2)}) collective-permute-start(bf16[288,128]{1,0:T(8,128)(2,1)S(1)} %get-tuple-element.82), channel_id=1, source_target_pairs={{0,2},{1,3},{2,0},{3,1},{4,6},{5,7},{6,4},{7,5},{8,10},{9,11},{10,... | collective-permute-start | bytes 221192 | tf_op jit(solution)/shard_map/ppermute | solution.py:63
  92.9 0.0 collective-permute-start.20
  92.9 0.3 collective-permute-start.25
  93.2 3.0 %collective-permute-start.26 = (bf16[1024,128]{1,0:T(8,128)(2,1)S(1)}, bf16[1024,128]{1,0:T(8,128)(2,1)S(1)}, u32[]{:S(2)}, u32[]{:S(2)}) collective-permute-start(bf16[1024,128]{1,0:T(8,128)(2,1)S(1)} %get-tuple-element.71), channel_id=1, source_target_pairs={{0,2},{1,3},{2,0},{3,1},{4,6},{5,7},{6,4},{7,5},{8,10},{9,11},{10,... | collective-permute-start | bytes 786440 | tf_op jit(solution)/shard_map/ppermute | solution.py:63
  96.2 0.2 collective-permute-done.20
  96.6 0.2 copy.37
  96.9 4.1 %collective-permute-start.23 = (bf16[2,32,128]{2,1,0:T(8,128)(2,1)S(1)}, bf16[2,32,128]{2,1,0:T(8,128)(2,1)S(1)}, u32[]{:S(2)}, u32[]{:S(2)}) collective-permute-start(bf16[2,32,128]{2,1,0:T(8,128)(2,1)S(1)} %dynamic-slice_bitcast_fusion.10), channel_id=1, source_target_pairs={{0,32},{1,33},{2,34},{3,35},{4,36},{5,37},{6,38},{7,39},{8,40},{9,... | collective-permute-start | bytes 49160 | tf_op jit(solution)/shard_map/ppermute | solution.py:63
  101.0 0.8 fusion.4
  101.8 0.0 collective-permute-done.23
  101.9 9.4 %collective-permute-start.24 = (f32[32,128]{1,0:T(8,128)S(1)}, f32[32,128]{1,0:T(8,128)S(1)}, u32[]{:S(2)}, u32[]{:S(2)}) collective-permute-start(f32[32,128]{1,0:T(8,128)S(1)} %dynamic-slice_bitcast_fusion.9), channel_id=1, source_target_pairs={{0,64},{1,65},{2,66},{3,67},{4,68},{5,69},{6,70},{7,71},{8,72},{9,... | collective-permute-start | bytes 49160 | tf_op jit(solution)/shard_map/ppermute | solution.py:63
  111.5 1.2 %copy_bitcast_fusion = bf16[1,128,32,128]{3,2,1,0:T(8,128)(2,1)} fusion(bf16[7,128,8,128]{3,2,1,0:T(8,128)(2,1)S(1)} %bitcast_dynamic-update-slice_fusion.2, s32[]{:T(128)S(6)} %select_n.98), kind=kLoop, calls=%fused_computation.1 | loop fusion | bytes 2097156 | tf_op jit(solution)/shard_map/reshape | solution.py:407
  112.7 0.6 slice_bitcast_fusion.1
  (60 shorter events, 0.7 us)
Async XLA Ops:
  0.6 9.9 %copy-start.1 = (bf16[1,128,32,128]{3,2,1,0:T(8,128)(2,1)S(1)}, bf16[1,128,32,128]{3,2,1,0:T(8,128)(2,1)}, u32[]{:S(2)}) copy-start(bf16[1,128,32,128]{3,2,1,0:T(8,128)(2,1)} %param.15) | copy-start | bytes 3145732
  1.4 15.4 %collective-permute-start.2 = (bf16[32,128]{1,0:T(8,128)(2,1)S(1)}, bf16[32,128]{1,0:T(8,128)(2,1)S(1)}, u32[]{:S(2)}, u32[]{:S(2)}) collective-permute-start(bf16[32,128]{1,0:T(8,128)(2,1)S(1)} %pad_maximum_fusion.6.p0_ref), channel_id=1, source_target_pairs={{0,96},{1,97},{2,98},{3,99},{4,100},{5,101},{6,102},{7,103},{8,104... | collective-permute-start | bytes 24584 | tf_op jit(solution)/shard_map/ppermute | solution.py:63
  2.9 14.0 %collective-permute-start.1 = (bf16[32,128]{1,0:T(8,128)(2,1)S(1)}, bf16[32,128]{1,0:T(8,128)(2,1)S(1)}, u32[]{:S(2)}, u32[]{:S(2)}) collective-permute-start(bf16[32,128]{1,0:T(8,128)(2,1)S(1)} %pad_maximum_fusion.6.p0_ref), channel_id=1, source_target_pairs={{0,64},{1,65},{2,66},{3,67},{4,68},{5,69},{6,70},{7,71},{8,72},{9,... | collective-permute-start | bytes 24584 | tf_op jit(solution)/shard_map/ppermute | solution.py:63
  6.5 10.3 %collective-permute-start = (bf16[32,128]{1,0:T(8,128)(2,1)S(1)}, bf16[32,128]{1,0:T(8,128)(2,1)S(1)}, u32[]{:S(2)}, u32[]{:S(2)}) collective-permute-start(bf16[32,128]{1,0:T(8,128)(2,1)S(1)} %pad_maximum_fusion.6.p0_ref), channel_id=1, source_target_pairs={{0,32},{1,33},{2,34},{3,35},{4,36},{5,37},{6,38},{7,39},{8,40},{9,... | collective-permute-start | bytes 24584 | tf_op jit(solution)/shard_map/ppermute | solution.py:63
  10.6 4.5 %copy-start.2 = (bf16[1,128,32,128]{3,2,1,0:T(8,128)(2,1)S(1)}, bf16[1,128,32,128]{3,2,1,0:T(8,128)(2,1)}, u32[]{:S(2)}) copy-start(bf16[1,128,32,128]{3,2,1,0:T(8,128)(2,1)} %param.16) | copy-start | bytes 3145732
  11.6 4.1 %copy-start.3 = (bf16[1,128,4,128]{3,2,1,0:T(4,128)(2,1)S(1)}, bf16[1,128,4,128]{3,2,1,0:T(4,128)(2,1)}, u32[]{:S(2)}) copy-start(bf16[1,128,4,128]{3,2,1,0:T(4,128)(2,1)} %param.12) | copy-start | bytes 393220
  11.6 4.1 %copy-start.4 = (bf16[1,128,4,128]{3,2,1,0:T(4,128)(2,1)S(1)}, bf16[1,128,4,128]{3,2,1,0:T(4,128)(2,1)}, u32[]{:S(2)}) copy-start(bf16[1,128,4,128]{3,2,1,0:T(4,128)(2,1)} %param.11) | copy-start | bytes 393220
  11.6 14.2 %collective-permute-start.6 = (bf16[2048,128]{1,0:T(8,128)(2,1)}, bf16[2048,128]{1,0:T(8,128)(2,1)S(1)}, u32[]{:S(2)}, u32[]{:S(2)}) collective-permute-start(bf16[2048,128]{1,0:T(8,128)(2,1)} %pad_maximum_fusion.1), channel_id=1, source_target_pairs={{0,1},{1,2},{2,3},{3,0},{4,5},{5,6},{6,7},{7,4},{8,9},{9,10},{10,1... | collective-permute-start | bytes 1572872 | tf_op jit(solution)/shard_map/ppermute | solution.py:63
  12.8 3.8 %copy-start.5 = (f32[1,128,32]{1,2,0:T(8,128)S(1)}, f32[1,128,32]{1,2,0:T(8,128)}, u32[]{:S(2)}) copy-start(f32[1,128,32]{1,2,0:T(8,128)} %param.17) | copy-start | bytes 49156
  13.6 3.3 %copy-start = (s32[1,4096]{1,0:T(1,128)S(1)}, s32[1,4096]{1,0:T(1,128)}, u32[]{:S(2)}) copy-start(s32[1,4096]{1,0:T(1,128)} %order_ref.1) | copy-start | bytes 49156
  13.6 12.1 %collective-permute-start.7 = (bf16[2048,128]{1,0:T(8,128)(2,1)}, bf16[2048,128]{1,0:T(8,128)(2,1)S(1)}, u32[]{:S(2)}, u32[]{:S(2)}) collective-permute-start(bf16[2048,128]{1,0:T(8,128)(2,1)} %pad_maximum_fusion.2), channel_id=1, source_target_pairs={{0,3},{1,0},{2,1},{3,2},{4,7},{5,4},{6,5},{7,6},{8,11},{9,8},{10,9... | collective-permute-start | bytes 1572872 | tf_op jit(solution)/shard_map/ppermute | solution.py:63
  19.6 5.5 %collective-permute-start.3 = (bf16[336,128]{1,0:T(8,128)(2,1)S(1)}, bf16[336,128]{1,0:T(8,128)(2,1)S(1)}, u32[]{:S(2)}, u32[]{:S(2)}) collective-permute-start(bf16[336,128]{1,0:T(8,128)(2,1)S(1)} %get-tuple-element.42), channel_id=1, source_target_pairs={{0,1},{1,2},{2,3},{3,0},{4,5},{5,6},{6,7},{7,4},{8,9},{9,10},{10,1... | collective-permute-start | bytes 258056 | tf_op jit(solution)/shard_map/ppermute | solution.py:63
  19.6 5.5 %collective-permute-start.4 = (bf16[336,128]{1,0:T(8,128)(2,1)S(1)}, bf16[336,128]{1,0:T(8,128)(2,1)S(1)}, u32[]{:S(2)}, u32[]{:S(2)}) collective-permute-start(bf16[336,128]{1,0:T(8,128)(2,1)S(1)} %get-tuple-element.43), channel_id=1, source_target_pairs={{0,2},{1,3},{2,0},{3,1},{4,6},{5,7},{6,4},{7,5},{8,10},{9,11},{10,... | collective-permute-start | bytes 258056 | tf_op jit(solution)/shard_map/ppermute | solution.py:63
  22.1 3.6 %collective-permute-start.5 = (bf16[336,128]{1,0:T(8,128)(2,1)S(1)}, bf16[336,128]{1,0:T(8,128)(2,1)S(1)}, u32[]{:S(2)}, u32[]{:S(2)}) collective-permute-start(bf16[336,128]{1,0:T(8,128)(2,1)S(1)} %get-tuple-element.44), channel_id=1, source_target_pairs={{0,3},{1,0},{2,1},{3,2},{4,7},{5,4},{6,5},{7,6},{8,11},{9,8},{10,9... | collective-permute-start | bytes 258056 | tf_op jit(solution)/shard_map/ppermute | solution.py:63
  25.8 8.8 %collective-permute-start.9 = (bf16[1152,128]{1,0:T(8,128)(2,1)S(1)}, bf16[1152,128]{1,0:T(8,128)(2,1)S(1)}, u32[]{:S(2)}, u32[]{:S(2)}) collective-permute-start(bf16[1152,128]{1,0:T(8,128)(2,1)S(1)} %pad_maximum_fusion.4.rest_0_), channel_id=1, source_target_pairs={{0,4},{1,5},{2,6},{3,7},{4,0},{5,1},{6,2},{7,3},{8,12},{9,13},{10,... | collective-permute-start | bytes 884744 | tf_op jit(solution)/shard_map/ppermute | solution.py:63
  26.6 11.1 %collective-permute-start.8 = (bf16[2048,128]{1,0:T(8,128)(2,1)}, bf16[2048,128]{1,0:T(8,128)(2,1)S(1)}, u32[]{:S(2)}, u32[]{:S(2)}) collective-permute-start(bf16[2048,128]{1,0:T(8,128)(2,1)} %pad_maximum_fusion), channel_id=1, source_target_pairs={{0,2},{1,3},{2,0},{3,1},{4,6},{5,7},{6,4},{7,5},{8,10},{9,11},{10,... | collective-permute-start | bytes 1572872 | tf_op jit(solution)/shard_map/ppermute | solution.py:63
  34.6 11.0 %collective-permute-start.12 = (bf16[2304,128]{1,0:T(8,128)(2,1)S(1)}, bf16[2304,128]{1,0:T(8,128)(2,1)S(1)}, u32[]{:S(2)}, u32[]{:S(2)}) collective-permute-start(bf16[2304,128]{1,0:T(8,128)(2,1)S(1)} %constant_dynamic-update-slice_fusion), channel_id=1, source_target_pairs={{0,24},{1,25},{2,26},{3,27},{4,28},{5,29},{6,30},{7,31},{8,0},{9,1... | collective-permute-start | bytes 1769480 | tf_op jit(solution)/shard_map/ppermute | solution.py:63
  37.6 10.2 %collective-permute-start.11 = (bf16[2304,128]{1,0:T(8,128)(2,1)S(1)}, bf16[2304,128]{1,0:T(8,128)(2,1)S(1)}, u32[]{:S(2)}, u32[]{:S(2)}) collective-permute-start(bf16[2304,128]{1,0:T(8,128)(2,1)S(1)} %constant_dynamic-update-slice_fusion), channel_id=1, source_target_pairs={{0,8},{1,9},{2,10},{3,11},{4,12},{5,13},{6,14},{7,15},{8,16},{9,17... | collective-permute-start | bytes 1769480 | tf_op jit(solution)/shard_map/ppermute | solution.py:63
  43.3 22.9 %collective-permute-start.13 = (bf16[1152,128]{1,0:T(8,128)(2,1)S(1)}, bf16[1152,128]{1,0:T(8,128)(2,1)S(1)}, u32[]{:S(2)}, u32[]{:S(2)}) collective-permute-start(bf16[1152,128]{1,0:T(8,128)(2,1)S(1)} %get-tuple-element.54), channel_id=1, source_target_pairs={{0,4},{1,5},{2,6},{3,7},{4,0},{5,1},{6,2},{7,3},{8,12},{9,13},{10,... | collective-permute-start | bytes 884744 | tf_op jit(solution)/shard_map/ppermute | solution.py:63
  44.1 23.9 %collective-permute-start.10 = (bf16[2304,128]{1,0:T(8,128)(2,1)S(1)}, bf16[2304,128]{1,0:T(8,128)(2,1)S(1)}, u32[]{:S(2)}, u32[]{:S(2)}) collective-permute-start(bf16[2304,128]{1,0:T(8,128)(2,1)S(1)} %constant_dynamic-update-slice_fusion), channel_id=1, source_target_pairs={{0,16},{1,17},{2,18},{3,19},{4,20},{5,21},{6,22},{7,23},{8,24},{9,... | collective-permute-start | bytes 1769480 | tf_op jit(solution)/shard_map/ppermute | solution.py:63
  64.1 14.2 %collective-permute-start.14 = (bf16[1152,128]{1,0:T(8,128)(2,1)S(1)}, bf16[1152,128]{1,0:T(8,128)(2,1)S(1)}, u32[]{:S(2)}, u32[]{:S(2)}) collective-permute-start(bf16[1152,128]{1,0:T(8,128)(2,1)S(1)} %get-tuple-element.56), channel_id=1, source_target_pairs={{0,24},{1,25},{2,26},{3,27},{4,28},{5,29},{6,30},{7,31},{8,0},{9,1... | collective-permute-start | bytes 884744 | tf_op jit(solution)/shard_map/ppermute | solution.py:63
  64.2 16.5 %collective-permute-start.15 = (bf16[1152,128]{1,0:T(8,128)(2,1)S(1)}, bf16[1152,128]{1,0:T(8,128)(2,1)S(1)}, u32[]{:S(2)}, u32[]{:S(2)}) collective-permute-start(bf16[1152,128]{1,0:T(8,128)(2,1)S(1)} %get-tuple-element.57), channel_id=1, source_target_pairs={{0,28},{1,29},{2,30},{3,31},{4,24},{5,25},{6,26},{7,27},{8,4},{9,5... | collective-permute-start | bytes 884744 | tf_op jit(solution)/shard_map/ppermute | solution.py:63
  64.7 16.0 %collective-permute-start.16 = (bf16[1152,128]{1,0:T(8,128)(2,1)S(1)}, bf16[1152,128]{1,0:T(8,128)(2,1)S(1)}, u32[]{:S(2)}, u32[]{:S(2)}) collective-permute-start(bf16[1152,128]{1,0:T(8,128)(2,1)S(1)} %get-tuple-element.58), channel_id=1, source_target_pairs={{0,8},{1,9},{2,10},{3,11},{4,12},{5,13},{6,14},{7,15},{8,16},{9,17... | collective-permute-start | bytes 884744 | tf_op jit(solution)/shard_map/ppermute | solution.py:63
  66.2 14.7 %collective-permute-start.17 = (bf16[1152,128]{1,0:T(8,128)(2,1)S(1)}, bf16[1152,128]{1,0:T(8,128)(2,1)S(1)}, u32[]{:S(2)}, u32[]{:S(2)}) collective-permute-start(bf16[1152,128]{1,0:T(8,128)(2,1)S(1)} %get-tuple-element.59), channel_id=1, source_target_pairs={{0,12},{1,13},{2,14},{3,15},{4,8},{5,9},{6,10},{7,11},{8,20},{9,21... | collective-permute-start | bytes 884744 | tf_op jit(solution)/shard_map/ppermute | solution.py:63
  77.2 10.1 %collective-permute-start.18 = (bf16[1152,128]{1,0:T(8,128)(2,1)S(1)}, bf16[1152,128]{1,0:T(8,128)(2,1)S(1)}, u32[]{:S(2)}, u32[]{:S(2)}) collective-permute-start(bf16[1152,128]{1,0:T(8,128)(2,1)S(1)} %get-tuple-element.65), channel_id=1, source_target_pairs={{0,16},{1,17},{2,18},{3,19},{4,20},{5,21},{6,22},{7,23},{8,24},{9,... | collective-permute-start | bytes 884744 | tf_op jit(solution)/shard_map/ppermute | solution.py:63
  78.3 10.0 %collective-permute-start.19 = (bf16[1152,128]{1,0:T(8,128)(2,1)S(1)}, bf16[1152,128]{1,0:T(8,128)(2,1)S(1)}, u32[]{:S(2)}, u32[]{:S(2)}) collective-permute-start(bf16[1152,128]{1,0:T(8,128)(2,1)S(1)} %get-tuple-element.66), channel_id=1, source_target_pairs={{0,20},{1,21},{2,22},{3,23},{4,16},{5,17},{6,18},{7,19},{8,28},{9,... | collective-permute-start | bytes 884744 | tf_op jit(solution)/shard_map/ppermute | solution.py:63
  88.4 8.1 %collective-permute-start.22 = (bf16[288,128]{1,0:T(8,128)(2,1)S(1)}, bf16[288,128]{1,0:T(8,128)(2,1)S(1)}, u32[]{:S(2)}, u32[]{:S(2)}) collective-permute-start(bf16[288,128]{1,0:T(8,128)(2,1)S(1)} %get-tuple-element.81), channel_id=1, source_target_pairs={{0,1},{1,2},{2,3},{3,0},{4,5},{5,6},{6,7},{7,4},{8,9},{9,10},{10,1... | collective-permute-start | bytes 221192 | tf_op jit(solution)/shard_map/ppermute | solution.py:63
  89.7 6.8 %collective-permute-start.21 = (bf16[288,128]{1,0:T(8,128)(2,1)S(1)}, bf16[288,128]{1,0:T(8,128)(2,1)S(1)}, u32[]{:S(2)}, u32[]{:S(2)}) collective-permute-start(bf16[288,128]{1,0:T(8,128)(2,1)S(1)} %get-tuple-element.82), channel_id=1, source_target_pairs={{0,2},{1,3},{2,0},{3,1},{4,6},{5,7},{6,4},{7,5},{8,10},{9,11},{10,... | collective-permute-start | bytes 221192 | tf_op jit(solution)/shard_map/ppermute | solution.py:63
  92.9 3.5 %collective-permute-start.20 = (bf16[288,128]{1,0:T(8,128)(2,1)S(1)}, bf16[288,128]{1,0:T(8,128)(2,1)S(1)}, u32[]{:S(2)}, u32[]{:S(2)}) collective-permute-start(bf16[288,128]{1,0:T(8,128)(2,1)S(1)} %get-tuple-element.83), channel_id=1, source_target_pairs={{0,3},{1,0},{2,1},{3,2},{4,7},{5,4},{6,5},{7,6},{8,11},{9,8},{10,9... | collective-permute-start | bytes 221192 | tf_op jit(solution)/shard_map/ppermute | solution.py:63
  92.9 18.3 %collective-permute-start.25 = (bf16[1024,128]{1,0:T(8,128)(2,1)S(1)}, bf16[1024,128]{1,0:T(8,128)(2,1)S(1)}, u32[]{:S(2)}, u32[]{:S(2)}) collective-permute-start(bf16[1024,128]{1,0:T(8,128)(2,1)S(1)} %get-tuple-element.70), channel_id=1, source_target_pairs={{0,3},{1,0},{2,1},{3,2},{4,7},{5,4},{6,5},{7,6},{8,11},{9,8},{10,9... | collective-permute-start | bytes 786440 | tf_op jit(solution)/shard_map/ppermute | solution.py:63
  93.2 18.1 %collective-permute-start.26 = (bf16[1024,128]{1,0:T(8,128)(2,1)S(1)}, bf16[1024,128]{1,0:T(8,128)(2,1)S(1)}, u32[]{:S(2)}, u32[]{:S(2)}) collective-permute-start(bf16[1024,128]{1,0:T(8,128)(2,1)S(1)} %get-tuple-element.71), channel_id=1, source_target_pairs={{0,2},{1,3},{2,0},{3,1},{4,6},{5,7},{6,4},{7,5},{8,10},{9,11},{10,... | collective-permute-start | bytes 786440 | tf_op jit(solution)/shard_map/ppermute | solution.py:63
  96.4 14.9 %collective-permute-start.27 = (bf16[1024,128]{1,0:T(8,128)(2,1)S(1)}, bf16[1024,128]{1,0:T(8,128)(2,1)S(1)}, u32[]{:S(2)}, u32[]{:S(2)}) collective-permute-start(bf16[1024,128]{1,0:T(8,128)(2,1)S(1)} %get-tuple-element.72), channel_id=1, source_target_pairs={{0,1},{1,2},{2,3},{3,0},{4,5},{5,6},{6,7},{7,4},{8,9},{9,10},{10,1... | collective-permute-start | bytes 786440 | tf_op jit(solution)/shard_map/ppermute | solution.py:63
  96.9 5.0 %collective-permute-start.23 = (bf16[2,32,128]{2,1,0:T(8,128)(2,1)S(1)}, bf16[2,32,128]{2,1,0:T(8,128)(2,1)S(1)}, u32[]{:S(2)}, u32[]{:S(2)}) collective-permute-start(bf16[2,32,128]{2,1,0:T(8,128)(2,1)S(1)} %dynamic-slice_bitcast_fusion.10), channel_id=1, source_target_pairs={{0,32},{1,33},{2,34},{3,35},{4,36},{5,37},{6,38},{7,39},{8,40},{9,... | collective-permute-start | bytes 49160 | tf_op jit(solution)/shard_map/ppermute | solution.py:63
  101.9 10.8 %collective-permute-start.24 = (f32[32,128]{1,0:T(8,128)S(1)}, f32[32,128]{1,0:T(8,128)S(1)}, u32[]{:S(2)}, u32[]{:S(2)}) collective-permute-start(f32[32,128]{1,0:T(8,128)S(1)} %dynamic-slice_bitcast_fusion.9), channel_id=1, source_target_pairs={{0,64},{1,65},{2,66},{3,67},{4,68},{5,69},{6,70},{7,71},{8,72},{9,... | collective-permute-start | bytes 49160 | tf_op jit(solution)/shard_map/ppermute | solution.py:63

commit v4 on v3

--- a/solution.py
+++ b/solution.py
@@ -67,17 +67,19 @@
     return lax.dot_general(a, b, dims, preferred_element_type=F32)
 
 
-def grads_kernel(halves, blocks, first, last, scale, received, at_ref, stats_ref, c0_ref, c1_ref, c2_ref, c3_ref, *rest):
+def grads_kernel(halves, blocks, first, last, scale, received, at_ref, stats_ref, *rest):
     parts = len(halves)
     members = 4 * parts
     rest = list(rest)
+    chunk_refs = [rest.pop(0) for _ in range(4 if first else 1)]
     kv_refs = [rest.pop(0) for _ in range(blocks)]
     dq_in = None if first else rest.pop(0)
     held = [rest.pop(0) for _ in range(received)]
     dq_outs = [rest.pop(0) for _ in range(4 if last else 1)]
     outs = [rest.pop(0) for _ in range(parts)]
-    chunk, keys, values, dkeys, dvalues, stage, meta_ref = rest[:7]
-    dq = rest[7] if last else dq_outs[0]
+    chunk = rest.pop(0) if first else chunk_refs[0]
+    keys, values, dkeys, dvalues, stage, meta_ref = rest[:6]
+    dq = rest[6] if last else dq_outs[0]
     core, head, block, z = [at_ref[64 + i] for i in range(4)]
 
     def runs_of(from_b, from_h, from_z):
@@ -102,7 +104,7 @@
         meta_ref[48 + e], meta_ref[52 + e] = runs_of(block, (head - e) & 3, z)
     rows = 512
     prompt = 16 * members
-    for i, ref in enumerate((c0_ref, c1_ref, c2_ref, c3_ref)):
+    for i, ref in enumerate(chunk_refs if first else []):
         chunk[pl.ds(i * 2048, 2048), :] = ref[...]
     if first:
         dq[...] = jnp.zeros_like(dq)
@@ -200,7 +202,7 @@
             )
         return 0
 
-    lax.fori_loop(0, 4, one_chunk, 0, unroll=(4, 2, 1, 1)[parts - 1])
+    lax.fori_loop(0, 4, one_chunk, 0, unroll=(4, 4, 1, 1)[parts - 1])
 
     if last:
         for i in range(8):
@@ -229,12 +231,13 @@
     vmem = pl.BlockSpec(memory_space=pltpu.VMEM)
     smem = pl.BlockSpec(memory_space=pltpu.SMEM)
     operands = [at, stats, *chunks, *kv] + ([] if first else [dq]) + list(held)
-    specs = [smem] + [vmem] * (5 + len(kv) + (0 if first else 1))
+    specs = [smem] + [vmem] * (1 + len(chunks) + len(kv) + (0 if first else 1))
     specs += [vmem if last else pl.BlockSpec(memory_space=pl.ANY)] * len(held)
     dq_shapes = [jax.ShapeDtypeStruct((1024, 128), BF16)] * 4 if last else [jax.ShapeDtypeStruct((1024, 512), F32)]
     sorted_rows = 144 * members
+    grad_shapes = [jax.ShapeDtypeStruct((1152, 128), F32 if last else BF16)] * parts
+    shapes = dq_shapes + grad_shapes + ([jax.ShapeDtypeStruct((8192, 128), BF16)] if first else [])
     scratch = [
-        pltpu.VMEM((4 * 2048, 128), BF16),
         pltpu.VMEM((sorted_rows, 128), BF16),
         pltpu.VMEM((sorted_rows, 128), BF16),
         pltpu.VMEM((sorted_rows, 128), F32),
@@ -246,9 +249,9 @@
         scratch.append(pltpu.VMEM((1024, 512), F32))
     return pl.pallas_call(
         functools.partial(grads_kernel, halves, len(kv), first, last, scale, len(held)),
-        out_shape=dq_shapes + [jax.ShapeDtypeStruct((1152, 128), F32 if last else BF16)] * parts,
+        out_shape=shapes,
         in_specs=specs,
-        out_specs=[vmem] * (len(dq_shapes) + parts),
+        out_specs=[vmem] * len(shapes),
         scratch_shapes=scratch,
         compiler_params=pltpu.CompilerParams(vmem_limit_bytes=32 * 2**20),
         cost_estimate=pl.CostEstimate(
@@ -355,8 +358,8 @@
         do = lax.dynamic_index_in_dim(g_four, g, 1, keepdims=False).reshape(1024, 128)
         return jnp.concatenate([q, do], axis=0)
 
-    chunks = [send(q_chunk((head + s) % 4), along_heads(s)) for s in (1, 3)]
-    far_chunk = q_chunk((head + 2) % 4)
+    chunks = [send(q_chunk((head + s) % 4), along_heads(s)) for s in (1, 2)]
+    last_chunk = q_chunk((head + 3) % 4)
 
     prompt = jnp.concatenate([prompt_keys[:, 0], prompt_values[:, 0]], axis=0)
     prompts = [prompt] + [send(prompt, along_resp(s)) for s in (1, 2, 3)]
@@ -367,14 +370,15 @@
     pieces = [pieces[0]] + [send(pieces[s], along_heads(s)) for s in (1, 2, 3)]
     near = jnp.concatenate([piece[:288] for piece in pieces], axis=0)
     stats = jnp.concatenate([piece[288:] for piece in pieces], axis=0)
-    near, far_chunk, *chunks = lax.optimization_barrier((near, far_chunk, *chunks))
+    near, last_chunk, *chunks = lax.optimization_barrier((near, last_chunk, *chunks))
     q_own, _ = lax.optimization_barrier((head, near))
-    chunks = [q_chunk(q_own), chunks[0], send(far_chunk, along_heads(2)), chunks[1]]
+    chunks = [q_chunk(q_own), chunks[0], chunks[1], send(last_chunk, along_heads(3))]
     far = send(near, along_z())
     own = jnp.concatenate([near, far], axis=0)
     kv_blocks = {s: send(own, along_blocks(s)) for s in (1, 3)}
 
-    dq, sent = block_grads([(0, 1)], True, False, scale, at, stats, chunks, [far], None, [])
+    dq, sent, chunk = block_grads([(0, 1)], True, False, scale, at, stats, chunks, [far], None, [])
+    chunks = [chunk]
     own, sent = lax.optimization_barrier((own, sent))
     kv_blocks[2] = send(own, along_blocks(2))
     got = [send(sent, along_z())]

time: 114 us -> 113 us (level)
  starting transfers between devices: 51.1 us -> 47.1 us
  waiting for transfers between devices: 10.4 us -> 13.5 us
    ppermute x28, starting transfers between devices: 51.1 us -> 47.1 us  [send(): return lax.ppermute(value, AXES, pairs)]
    ppermute x28, waiting for transfers between devices: 10.4 us -> 13.5 us  [send(): return lax.ppermute(value, AXES, pairs)]
  transfers between devices with their start and end apart: 28 -> 28, of which waited for: 7 -> 6; matrix products, arithmetic and copies ran while one was open for 8% -> 8% of each run, Pallas kernels for 35% -> 35%
where the time goes in v4:
time: 113 us; the launch traced here: 112 us
  starting transfers between devices  47.1 us (42%)
  Pallas kernels  39.4 us (35%)
  waiting for transfers between devices  13.5 us (12%)
  local copies, waits for them, and re-layouts  5.82 us (5%)
  other arithmetic  4.3 us (4%)
  between operations  1.76 us (2%)
    ppermute x28, starting transfers between devices, send(): return lax.ppermute(value, AXES, pairs)  47.1 us
    pallas_call x4, Pallas kernels, block_grads(): pl.pallas_call(functools.partial(grads_kernel, halves, len(kv), first, la...  36.7 us
    ppermute x28, waiting for transfers between devices, send(): return lax.ppermute(value, AXES, pairs)  13.5 us
    pallas_call x1, Pallas kernels, make_chunks(): pl.pallas_call(chunks_kernel, out_shape=[jax.ShapeDtypeStruct((336, 128),...  2.67 us
    concatenate x4, other arithmetic, q_chunk(): return jnp.concatenate([q, do], axis=0)  2.55 us
  transfers between devices with their start and end apart: 28, of which 6 were waited for; matrix products, arithmetic and copies ran while one was open for 8% of the time, Pallas kernels for 35%

profile of v4, /device:TPU:1, one launch (start us, length us, event | category | flops | bytes accessed | tf_op | source)
XLA Modules:
  0.0 111.9 jit_solution(2174957502717590477)
XLA Ops:
  0.6 0.8 pad_maximum_fusion.6.p0_ref
  1.4 1.4 %collective-permute-start.2 = (bf16[32,128]{1,0:T(8,128)(2,1)S(1)}, bf16[32,128]{1,0:T(8,128)(2,1)S(1)}, u32[]{:S(2)}, u32[]{:S(2)}) collective-permute-start(bf16[32,128]{1,0:T(8,128)(2,1)S(1)} %pad_maximum_fusion.6.p0_ref), channel_id=1, source_target_pairs={{0,96},{1,97},{2,98},{3,99},{4,100},{5,101},{6,102},{7,103},{8,104... | collective-permute-start | bytes 24584 | tf_op jit(solution)/shard_map/ppermute | solution.py:63
  2.9 3.7 %collective-permute-start.1 = (bf16[32,128]{1,0:T(8,128)(2,1)S(1)}, bf16[32,128]{1,0:T(8,128)(2,1)S(1)}, u32[]{:S(2)}, u32[]{:S(2)}) collective-permute-start(bf16[32,128]{1,0:T(8,128)(2,1)S(1)} %pad_maximum_fusion.6.p0_ref), channel_id=1, source_target_pairs={{0,64},{1,65},{2,66},{3,67},{4,68},{5,69},{6,70},{7,71},{8,72},{9,... | collective-permute-start | bytes 24584 | tf_op jit(solution)/shard_map/ppermute | solution.py:63
  6.5 2.9 %collective-permute-start = (bf16[32,128]{1,0:T(8,128)(2,1)S(1)}, bf16[32,128]{1,0:T(8,128)(2,1)S(1)}, u32[]{:S(2)}, u32[]{:S(2)}) collective-permute-start(bf16[32,128]{1,0:T(8,128)(2,1)S(1)} %pad_maximum_fusion.6.p0_ref), channel_id=1, source_target_pairs={{0,32},{1,33},{2,34},{3,35},{4,36},{5,37},{6,38},{7,39},{8,40},{9,... | collective-permute-start | bytes 24584 | tf_op jit(solution)/shard_map/ppermute | solution.py:63
  9.4 1.2 %dynamic-slice_bitcast_fusion.4 = (bf16[1024,128]{1,0:T(8,128)(2,1)S(1)}, bf16[1024,128]{1,0:T(8,128)(2,1)S(1)}, bf16[1024,128]{1,0:T(8,128)(2,1)S(1)}) fusion(bf16[128,4,8,128]{3,2,1,0:T(8,128)(2,1)} %bitcast.101, s32[]{:T(128)S(6)} %select_n.95, s32[]{:T(128)S(6)} %select_n.93, s32[]{:T(128)S(6)} %select_n.91), kind=kLoop, calls=%fused_computation.21 | loop fusion | bytes 1572876 | tf_op jit(solution)/shard_map/reshape | solution.py:357
  10.6 0.0 copy-start.2
  10.6 0.1 dynamic-slice_bitcast_fusion.3
  10.7 0.8 pad_maximum_fusion.1
  11.6 1.2 %collective-permute-start.6 = (bf16[2048,128]{1,0:T(8,128)(2,1)}, bf16[2048,128]{1,0:T(8,128)(2,1)S(1)}, u32[]{:S(2)}, u32[]{:S(2)}) collective-permute-start(bf16[2048,128]{1,0:T(8,128)(2,1)} %pad_maximum_fusion.1), channel_id=1, source_target_pairs={{0,1},{1,2},{2,3},{3,0},{4,5},{5,6},{6,7},{7,4},{8,9},{9,10},{10,1... | collective-permute-start | bytes 1572872 | tf_op jit(solution)/shard_map/ppermute | solution.py:63
  12.8 0.8 pad_maximum_fusion.2
  13.6 2.5 %collective-permute-start.7 = (bf16[2048,128]{1,0:T(8,128)(2,1)}, bf16[2048,128]{1,0:T(8,128)(2,1)S(1)}, u32[]{:S(2)}, u32[]{:S(2)}) collective-permute-start(bf16[2048,128]{1,0:T(8,128)(2,1)} %pad_maximum_fusion.2), channel_id=1, source_target_pairs={{0,2},{1,3},{2,0},{3,1},{4,6},{5,7},{6,4},{7,5},{8,10},{9,11},{10,... | collective-permute-start | bytes 1572872 | tf_op jit(solution)/shard_map/ppermute | solution.py:63
  16.1 0.6 multiply_reduce_fusion.delta_ref
  16.7 0.2 maximum_bitcast_fusion
  17.6 0.1 copy.15
  17.8 0.1 stack.53.me_ref
  17.9 2.7 %shard_map.137 = (bf16[336,128]{1,0:T(8,128)(2,1)S(1)}, bf16[336,128]{1,0:T(8,128)(2,1)S(1)}, bf16[336,128]{1,0:T(8,128)(2,1)S(1)}, bf16[336,128]{1,0:T(8,128)(2,1)S(1)}, s32[72]{0:T(128)S(1)}) custom-call(s32[6]{0:T(128)S(1)} %stack.53.me_ref, s32[1,4096]{1,0:T(1,128)S(1)} %copy-done, s32[1]{0:T(128)S(6)} %copy.51.lengths_ref, f32[128,32]{1,0:T(8,128)S(1)} %bitcast.97, ...), custom_call_target="tpu_custom_call" | custom-call | flops 200000000 | bytes 1000000 | tf_op jit(solution)/shard_map/pallas_call | solution.py:323
  20.6 0.1 collective-permute-start.3
  20.6 2.3 %collective-permute-start.4 = (bf16[336,128]{1,0:T(8,128)(2,1)S(1)}, bf16[336,128]{1,0:T(8,128)(2,1)S(1)}, u32[]{:S(2)}, u32[]{:S(2)}) collective-permute-start(bf16[336,128]{1,0:T(8,128)(2,1)S(1)} %get-tuple-element.44), channel_id=1, source_target_pairs={{0,2},{1,3},{2,0},{3,1},{4,6},{5,7},{6,4},{7,5},{8,10},{9,11},{10,... | collective-permute-start | bytes 258056 | tf_op jit(solution)/shard_map/ppermute | solution.py:63
  23.0 0.3 collective-permute-start.5
  23.3 0.9 pad_maximum_fusion
  24.2 4.4 %collective-permute-done.3 = bf16[336,128]{1,0:T(8,128)(2,1)S(1)} collective-permute-done((bf16[336,128]{1,0:T(8,128)(2,1)S(1)}, bf16[336,128]{1,0:T(8,128)(2,1)S(1)}, u32[]{:S(2)}, u32[]{:S(2)}) %collective-permute-start.3) | collective-permute-done | bytes 86048 | tf_op jit(solution)/shard_map/ppermute | solution.py:63
  28.6 1.0 collective-permute-done.4
  29.6 0.0 collective-permute-done.6.rest_1_
  29.6 0.0 collective-permute-done.7.rest_2_
  29.6 0.8 collective-permute-start.9
  30.5 1.0 dynamic-slice_bitcast_fusion.1
  31.5 6.8 %collective-permute-done.9.rest_4_ = bf16[1152,128]{1,0:T(8,128)(2,1)S(1)} collective-permute-done((bf16[1152,128]{1,0:T(8,128)(2,1)S(1)}, bf16[1152,128]{1,0:T(8,128)(2,1)S(1)}, u32[]{:S(2)}, u32[]{:S(2)}) %collective-permute-start.9) | collective-permute-done | bytes 294944 | tf_op jit(solution)/shard_map/ppermute | solution.py:63
  38.3 0.1 collective-permute-start.12
  38.5 1.4 %collective-permute-start.11 = (bf16[2304,128]{1,0:T(8,128)(2,1)S(1)}, bf16[2304,128]{1,0:T(8,128)(2,1)S(1)}, u32[]{:S(2)}, u32[]{:S(2)}) collective-permute-start(bf16[2304,128]{1,0:T(8,128)(2,1)S(1)} %constant_dynamic-update-slice_fusion), channel_id=1, source_target_pairs={{0,8},{1,9},{2,10},{3,11},{4,12},{5,13},{6,14},{7,15},{8,16},{9,17... | collective-permute-start | bytes 1769480 | tf_op jit(solution)/shard_map/ppermute | solution.py:63
  39.9 5.6 %shard_map.138 = (f32[1024,512]{1,0:T(8,128)S(1)}, bf16[1152,128]{1,0:T(8,128)(2,1)S(1)}, bf16[8192,128]{1,0:T(8,128)(2,1)S(1)}) custom-call(s32[72]{0:T(128)S(1)} %get-tuple-element.41.at_ref, bf16[192,128]{1,0:T(8,128)(2,1)S(1)} %pad_maximum_fusion.5.stats_ref, bf16[2048,128]{1,0:T(8,128)(2,1)S(1)} %pad_maximum_fusion.3.rest_0_, ...), custom_call_target="tpu_custom_call" | custom-call | flops 5000000000 | bytes 8000000 | tf_op jit(solution)/shard_map/pallas_call | solution.py:250
  45.5 0.8 collective-permute-start.13
  46.3 2.1 %collective-permute-start.10 = (bf16[2304,128]{1,0:T(8,128)(2,1)S(1)}, bf16[2304,128]{1,0:T(8,128)(2,1)S(1)}, u32[]{:S(2)}, u32[]{:S(2)}) collective-permute-start(bf16[2304,128]{1,0:T(8,128)(2,1)S(1)} %constant_dynamic-update-slice_fusion), channel_id=1, source_target_pairs={{0,16},{1,17},{2,18},{3,19},{4,20},{5,21},{6,22},{7,23},{8,24},{9,... | collective-permute-start | bytes 1769480 | tf_op jit(solution)/shard_map/ppermute | solution.py:63
  48.4 0.3 collective-permute-done.11.rest_1_
  48.7 16.0 %shard_map.139 = (f32[1024,512]{1,0:T(8,128)S(1)}, bf16[1152,128]{1,0:T(8,128)(2,1)S(1)}, bf16[1152,128]{1,0:T(8,128)(2,1)S(1)}, bf16[1152,128]{1,0:T(8,128)(2,1)S(1)}, bf16[1152,128]{1,0:T(8,128)(2,1)S(1)}) custom-call(s32[72]{0:T(128)S(1)} %get-tuple-element.41.at_ref, bf16[192,128]{1,0:T(8,128)(2,1)S(1)} %pad_maximum_fusion.5.stats_ref, ...), custom_call_target="tpu_custom_call" | custom-call | flops 20000000000 | bytes 8000000 | tf_op jit(solution)/shard_map/pallas_call | solution.py:250
  64.8 0.5 collective-permute-start.14
  65.3 0.8 collective-permute-start.15
  66.1 1.1 collective-permute-start.16
  67.2 0.0 collective-permute-done.13.rest_3_
  67.2 1.4 %collective-permute-start.17 = (bf16[1152,128]{1,0:T(8,128)(2,1)S(1)}, bf16[1152,128]{1,0:T(8,128)(2,1)S(1)}, u32[]{:S(2)}, u32[]{:S(2)}) collective-permute-start(bf16[1152,128]{1,0:T(8,128)(2,1)S(1)} %get-tuple-element.61), channel_id=1, source_target_pairs={{0,12},{1,13},{2,14},{3,15},{4,8},{5,9},{6,10},{7,11},{8,20},{9,21... | collective-permute-start | bytes 884744 | tf_op jit(solution)/shard_map/ppermute | solution.py:63
  68.7 0.0 collective-permute-done.10.rest_1_
  68.7 8.8 %shard_map.140 = (f32[1024,512]{1,0:T(8,128)S(1)}, bf16[1152,128]{1,0:T(8,128)(2,1)S(1)}, bf16[1152,128]{1,0:T(8,128)(2,1)S(1)}) custom-call(s32[72]{0:T(128)S(1)} %get-tuple-element.41.at_ref, bf16[192,128]{1,0:T(8,128)(2,1)S(1)} %pad_maximum_fusion.5.stats_ref, bf16[8192,128]{1,0:T(8,128)(2,1)S(1)} %get-tuple-element.51.rest_0_, ...), custom_call_target="tpu_custom_call" | custom-call | flops 10000000000 | bytes 8000000 | tf_op jit(solution)/shard_map/pallas_call | solution.py:250
  77.4 1.9 %collective-permute-start.18 = (bf16[1152,128]{1,0:T(8,128)(2,1)S(1)}, bf16[1152,128]{1,0:T(8,128)(2,1)S(1)}, u32[]{:S(2)}, u32[]{:S(2)}) collective-permute-start(bf16[1152,128]{1,0:T(8,128)(2,1)S(1)} %get-tuple-element.67), channel_id=1, source_target_pairs={{0,16},{1,17},{2,18},{3,19},{4,20},{5,21},{6,22},{7,23},{8,24},{9,... | collective-permute-start | bytes 884744 | tf_op jit(solution)/shard_map/ppermute | solution.py:63
  79.3 1.6 %collective-permute-start.19 = (bf16[1152,128]{1,0:T(8,128)(2,1)S(1)}, bf16[1152,128]{1,0:T(8,128)(2,1)S(1)}, u32[]{:S(2)}, u32[]{:S(2)}) collective-permute-start(bf16[1152,128]{1,0:T(8,128)(2,1)S(1)} %get-tuple-element.68), channel_id=1, source_target_pairs={{0,20},{1,21},{2,22},{3,23},{4,16},{5,17},{6,18},{7,19},{8,28},{9,... | collective-permute-start | bytes 884744 | tf_op jit(solution)/shard_map/ppermute | solution.py:63
  80.9 0.0 collective-permute-done.16.rest_6_
  80.9 0.9 collective-permute-done.17.rest_7_
  81.9 6.3 %shard_map.141 = (bf16[1024,128]{1,0:T(8,128)(2,1)S(1)}, bf16[1024,128]{1,0:T(8,128)(2,1)S(1)}, bf16[1024,128]{1,0:T(8,128)(2,1)S(1)}, bf16[1024,128]{1,0:T(8,128)(2,1)S(1)}, f32[1152,128]{1,0:T(8,128)S(1)}) custom-call(s32[72]{0:T(128)S(1)} %get-tuple-element.41.at_ref, bf16[192,128]{1,0:T(8,128)(2,1)S(1)} %pad_maximum_fusion.5.stats_ref, ...), custom_call_target="tpu_custom_call" | custom-call | flops 5000000000 | bytes 8000000 | tf_op jit(solution)/shard_map/pallas_call | solution.py:250
  88.2 0.0 collective-permute-done.18
  88.2 0.1 add_convert_fusion
  88.4 2.0 %collective-permute-start.22 = (bf16[288,128]{1,0:T(8,128)(2,1)S(1)}, bf16[288,128]{1,0:T(8,128)(2,1)S(1)}, u32[]{:S(2)}, u32[]{:S(2)}) collective-permute-start(bf16[288,128]{1,0:T(8,128)(2,1)S(1)} %get-tuple-element.83), channel_id=1, source_target_pairs={{0,1},{1,2},{2,3},{3,0},{4,5},{5,6},{6,7},{7,4},{8,9},{9,10},{10,1... | collective-permute-start | bytes 221192 | tf_op jit(solution)/shard_map/ppermute | solution.py:63
  90.4 2.1 %collective-permute-start.21 = (bf16[288,128]{1,0:T(8,128)(2,1)S(1)}, bf16[288,128]{1,0:T(8,128)(2,1)S(1)}, u32[]{:S(2)}, u32[]{:S(2)}) collective-permute-start(bf16[288,128]{1,0:T(8,128)(2,1)S(1)} %get-tuple-element.84), channel_id=1, source_target_pairs={{0,2},{1,3},{2,0},{3,1},{4,6},{5,7},{6,4},{7,5},{8,10},{9,11},{10,... | collective-permute-start | bytes 221192 | tf_op jit(solution)/shard_map/ppermute | solution.py:63
  92.5 2.0 %collective-permute-start.20 = (bf16[288,128]{1,0:T(8,128)(2,1)S(1)}, bf16[288,128]{1,0:T(8,128)(2,1)S(1)}, u32[]{:S(2)}, u32[]{:S(2)}) collective-permute-start(bf16[288,128]{1,0:T(8,128)(2,1)S(1)} %get-tuple-element.85), channel_id=1, source_target_pairs={{0,3},{1,0},{2,1},{3,2},{4,7},{5,4},{6,5},{7,6},{8,11},{9,8},{10,9... | collective-permute-start | bytes 221192 | tf_op jit(solution)/shard_map/ppermute | solution.py:63
  94.5 0.0 collective-permute-start.25
  94.5 1.2 %collective-permute-start.26 = (bf16[1024,128]{1,0:T(8,128)(2,1)S(1)}, bf16[1024,128]{1,0:T(8,128)(2,1)S(1)}, u32[]{:S(2)}, u32[]{:S(2)}) collective-permute-start(bf16[1024,128]{1,0:T(8,128)(2,1)S(1)} %get-tuple-element.73), channel_id=1, source_target_pairs={{0,2},{1,3},{2,0},{3,1},{4,6},{5,7},{6,4},{7,5},{8,10},{9,11},{10,... | collective-permute-start | bytes 786440 | tf_op jit(solution)/shard_map/ppermute | solution.py:63
  95.8 0.1 collective-permute-done.20
  95.9 0.2 collective-permute-start.27
  96.1 0.0 collective-permute-done.22
  96.2 0.2 copy.37
  96.5 5.8 %collective-permute-start.23 = (bf16[2,32,128]{2,1,0:T(8,128)(2,1)S(1)}, bf16[2,32,128]{2,1,0:T(8,128)(2,1)S(1)}, u32[]{:S(2)}, u32[]{:S(2)}) collective-permute-start(bf16[2,32,128]{2,1,0:T(8,128)(2,1)S(1)} %dynamic-slice_bitcast_fusion.10), channel_id=1, source_target_pairs={{0,32},{1,33},{2,34},{3,35},{4,36},{5,37},{6,38},{7,39},{8,40},{9,... | collective-permute-start | bytes 49160 | tf_op jit(solution)/shard_map/ppermute | solution.py:63
  102.3 0.8 fusion.4
  103.1 0.0 collective-permute-done.23
  103.1 6.7 %collective-permute-start.24 = (f32[32,128]{1,0:T(8,128)S(1)}, f32[32,128]{1,0:T(8,128)S(1)}, u32[]{:S(2)}, u32[]{:S(2)}) collective-permute-start(f32[32,128]{1,0:T(8,128)S(1)} %dynamic-slice_bitcast_fusion.9), channel_id=1, source_target_pairs={{0,64},{1,65},{2,66},{3,67},{4,68},{5,69},{6,70},{7,71},{8,72},{9,... | collective-permute-start | bytes 49160 | tf_op jit(solution)/shard_map/ppermute | solution.py:63
  109.9 0.0 collective-permute-done.26
  110.1 1.2 %copy_bitcast_fusion = bf16[1,128,32,128]{3,2,1,0:T(8,128)(2,1)} fusion(bf16[7,128,8,128]{3,2,1,0:T(8,128)(2,1)S(1)} %bitcast_dynamic-update-slice_fusion.2, s32[]{:T(128)S(6)} %select_n.98), kind=kLoop, calls=%fused_computation.1 | loop fusion | bytes 2097156 | tf_op jit(solution)/shard_map/reshape | solution.py:411
  111.3 0.6 slice_bitcast_fusion.1
  (60 shorter events, 0.7 us)
Async XLA Ops:
  0.6 9.9 %copy-start.1 = (bf16[1,128,32,128]{3,2,1,0:T(8,128)(2,1)S(1)}, bf16[1,128,32,128]{3,2,1,0:T(8,128)(2,1)}, u32[]{:S(2)}) copy-start(bf16[1,128,32,128]{3,2,1,0:T(8,128)(2,1)} %param.15) | copy-start | bytes 3145732
  1.4 16.4 %collective-permute-start.2 = (bf16[32,128]{1,0:T(8,128)(2,1)S(1)}, bf16[32,128]{1,0:T(8,128)(2,1)S(1)}, u32[]{:S(2)}, u32[]{:S(2)}) collective-permute-start(bf16[32,128]{1,0:T(8,128)(2,1)S(1)} %pad_maximum_fusion.6.p0_ref), channel_id=1, source_target_pairs={{0,96},{1,97},{2,98},{3,99},{4,100},{5,101},{6,102},{7,103},{8,104... | collective-permute-start | bytes 24584 | tf_op jit(solution)/shard_map/ppermute | solution.py:63
  2.9 15.0 %collective-permute-start.1 = (bf16[32,128]{1,0:T(8,128)(2,1)S(1)}, bf16[32,128]{1,0:T(8,128)(2,1)S(1)}, u32[]{:S(2)}, u32[]{:S(2)}) collective-permute-start(bf16[32,128]{1,0:T(8,128)(2,1)S(1)} %pad_maximum_fusion.6.p0_ref), channel_id=1, source_target_pairs={{0,64},{1,65},{2,66},{3,67},{4,68},{5,69},{6,70},{7,71},{8,72},{9,... | collective-permute-start | bytes 24584 | tf_op jit(solution)/shard_map/ppermute | solution.py:63
  6.5 11.3 %collective-permute-start = (bf16[32,128]{1,0:T(8,128)(2,1)S(1)}, bf16[32,128]{1,0:T(8,128)(2,1)S(1)}, u32[]{:S(2)}, u32[]{:S(2)}) collective-permute-start(bf16[32,128]{1,0:T(8,128)(2,1)S(1)} %pad_maximum_fusion.6.p0_ref), channel_id=1, source_target_pairs={{0,32},{1,33},{2,34},{3,35},{4,36},{5,37},{6,38},{7,39},{8,40},{9,... | collective-permute-start | bytes 24584 | tf_op jit(solution)/shard_map/ppermute | solution.py:63
  10.6 5.5 %copy-start.2 = (bf16[1,128,32,128]{3,2,1,0:T(8,128)(2,1)S(1)}, bf16[1,128,32,128]{3,2,1,0:T(8,128)(2,1)}, u32[]{:S(2)}) copy-start(bf16[1,128,32,128]{3,2,1,0:T(8,128)(2,1)} %param.16) | copy-start | bytes 3145732
  11.6 5.1 %copy-start.3 = (bf16[1,128,4,128]{3,2,1,0:T(4,128)(2,1)S(1)}, bf16[1,128,4,128]{3,2,1,0:T(4,128)(2,1)}, u32[]{:S(2)}) copy-start(bf16[1,128,4,128]{3,2,1,0:T(4,128)(2,1)} %param.12) | copy-start | bytes 393220
  11.6 5.1 %copy-start.4 = (bf16[1,128,4,128]{3,2,1,0:T(4,128)(2,1)S(1)}, bf16[1,128,4,128]{3,2,1,0:T(4,128)(2,1)}, u32[]{:S(2)}) copy-start(bf16[1,128,4,128]{3,2,1,0:T(4,128)(2,1)} %param.11) | copy-start | bytes 393220
  11.6 18.0 %collective-permute-start.6 = (bf16[2048,128]{1,0:T(8,128)(2,1)}, bf16[2048,128]{1,0:T(8,128)(2,1)S(1)}, u32[]{:S(2)}, u32[]{:S(2)}) collective-permute-start(bf16[2048,128]{1,0:T(8,128)(2,1)} %pad_maximum_fusion.1), channel_id=1, source_target_pairs={{0,1},{1,2},{2,3},{3,0},{4,5},{5,6},{6,7},{7,4},{8,9},{9,10},{10,1... | collective-permute-start | bytes 1572872 | tf_op jit(solution)/shard_map/ppermute | solution.py:63
  12.8 4.8 %copy-start.5 = (f32[1,128,32]{1,2,0:T(8,128)S(1)}, f32[1,128,32]{1,2,0:T(8,128)}, u32[]{:S(2)}) copy-start(f32[1,128,32]{1,2,0:T(8,128)} %param.17) | copy-start | bytes 49156
  13.6 4.3 %copy-start = (s32[1,4096]{1,0:T(1,128)S(1)}, s32[1,4096]{1,0:T(1,128)}, u32[]{:S(2)}) copy-start(s32[1,4096]{1,0:T(1,128)} %order_ref.1) | copy-start | bytes 49156
  13.6 16.0 %collective-permute-start.7 = (bf16[2048,128]{1,0:T(8,128)(2,1)}, bf16[2048,128]{1,0:T(8,128)(2,1)S(1)}, u32[]{:S(2)}, u32[]{:S(2)}) collective-permute-start(bf16[2048,128]{1,0:T(8,128)(2,1)} %pad_maximum_fusion.2), channel_id=1, source_target_pairs={{0,2},{1,3},{2,0},{3,1},{4,6},{5,7},{6,4},{7,5},{8,10},{9,11},{10,... | collective-permute-start | bytes 1572872 | tf_op jit(solution)/shard_map/ppermute | solution.py:63
  20.6 8.0 %collective-permute-start.3 = (bf16[336,128]{1,0:T(8,128)(2,1)S(1)}, bf16[336,128]{1,0:T(8,128)(2,1)S(1)}, u32[]{:S(2)}, u32[]{:S(2)}) collective-permute-start(bf16[336,128]{1,0:T(8,128)(2,1)S(1)} %get-tuple-element.43), channel_id=1, source_target_pairs={{0,1},{1,2},{2,3},{3,0},{4,5},{5,6},{6,7},{7,4},{8,9},{9,10},{10,1... | collective-permute-start | bytes 258056 | tf_op jit(solution)/shard_map/ppermute | solution.py:63
  20.6 8.9 %collective-permute-start.4 = (bf16[336,128]{1,0:T(8,128)(2,1)S(1)}, bf16[336,128]{1,0:T(8,128)(2,1)S(1)}, u32[]{:S(2)}, u32[]{:S(2)}) collective-permute-start(bf16[336,128]{1,0:T(8,128)(2,1)S(1)} %get-tuple-element.44), channel_id=1, source_target_pairs={{0,2},{1,3},{2,0},{3,1},{4,6},{5,7},{6,4},{7,5},{8,10},{9,11},{10,... | collective-permute-start | bytes 258056 | tf_op jit(solution)/shard_map/ppermute | solution.py:63
  23.0 6.6 %collective-permute-start.5 = (bf16[336,128]{1,0:T(8,128)(2,1)S(1)}, bf16[336,128]{1,0:T(8,128)(2,1)S(1)}, u32[]{:S(2)}, u32[]{:S(2)}) collective-permute-start(bf16[336,128]{1,0:T(8,128)(2,1)S(1)} %get-tuple-element.45), channel_id=1, source_target_pairs={{0,3},{1,0},{2,1},{3,2},{4,7},{5,4},{6,5},{7,6},{8,11},{9,8},{10,9... | collective-permute-start | bytes 258056 | tf_op jit(solution)/shard_map/ppermute | solution.py:63
  29.6 8.6 %collective-permute-start.9 = (bf16[1152,128]{1,0:T(8,128)(2,1)S(1)}, bf16[1152,128]{1,0:T(8,128)(2,1)S(1)}, u32[]{:S(2)}, u32[]{:S(2)}) collective-permute-start(bf16[1152,128]{1,0:T(8,128)(2,1)S(1)} %pad_maximum_fusion.4.rest_1_), channel_id=1, source_target_pairs={{0,4},{1,5},{2,6},{3,7},{4,0},{5,1},{6,2},{7,3},{8,12},{9,13},{10,... | collective-permute-start | bytes 884744 | tf_op jit(solution)/shard_map/ppermute | solution.py:63
  30.5 9.4 %collective-permute-start.8 = (bf16[2048,128]{1,0:T(8,128)(2,1)}, bf16[2048,128]{1,0:T(8,128)(2,1)S(1)}, u32[]{:S(2)}, u32[]{:S(2)}) collective-permute-start(bf16[2048,128]{1,0:T(8,128)(2,1)} %pad_maximum_fusion), channel_id=1, source_target_pairs={{0,3},{1,0},{2,1},{3,2},{4,7},{5,4},{6,5},{7,6},{8,11},{9,8},{10,9... | collective-permute-start | bytes 1572872 | tf_op jit(solution)/shard_map/ppermute | solution.py:63
  38.3 10.1 %collective-permute-start.12 = (bf16[2304,128]{1,0:T(8,128)(2,1)S(1)}, bf16[2304,128]{1,0:T(8,128)(2,1)S(1)}, u32[]{:S(2)}, u32[]{:S(2)}) collective-permute-start(bf16[2304,128]{1,0:T(8,128)(2,1)S(1)} %constant_dynamic-update-slice_fusion), channel_id=1, source_target_pairs={{0,24},{1,25},{2,26},{3,27},{4,28},{5,29},{6,30},{7,31},{8,0},{9,1... | collective-permute-start | bytes 1769480 | tf_op jit(solution)/shard_map/ppermute | solution.py:63
  38.5 10.2 %collective-permute-start.11 = (bf16[2304,128]{1,0:T(8,128)(2,1)S(1)}, bf16[2304,128]{1,0:T(8,128)(2,1)S(1)}, u32[]{:S(2)}, u32[]{:S(2)}) collective-permute-start(bf16[2304,128]{1,0:T(8,128)(2,1)S(1)} %constant_dynamic-update-slice_fusion), channel_id=1, source_target_pairs={{0,8},{1,9},{2,10},{3,11},{4,12},{5,13},{6,14},{7,15},{8,16},{9,17... | collective-permute-start | bytes 1769480 | tf_op jit(solution)/shard_map/ppermute | solution.py:63
  45.5 21.8 %collective-permute-start.13 = (bf16[1152,128]{1,0:T(8,128)(2,1)S(1)}, bf16[1152,128]{1,0:T(8,128)(2,1)S(1)}, u32[]{:S(2)}, u32[]{:S(2)}) collective-permute-start(bf16[1152,128]{1,0:T(8,128)(2,1)S(1)} %get-tuple-element.56), channel_id=1, source_target_pairs={{0,4},{1,5},{2,6},{3,7},{4,0},{5,1},{6,2},{7,3},{8,12},{9,13},{10,... | collective-permute-start | bytes 884744 | tf_op jit(solution)/shard_map/ppermute | solution.py:63
  46.3 22.4 %collective-permute-start.10 = (bf16[2304,128]{1,0:T(8,128)(2,1)S(1)}, bf16[2304,128]{1,0:T(8,128)(2,1)S(1)}, u32[]{:S(2)}, u32[]{:S(2)}) collective-permute-start(bf16[2304,128]{1,0:T(8,128)(2,1)S(1)} %constant_dynamic-update-slice_fusion), channel_id=1, source_target_pairs={{0,16},{1,17},{2,18},{3,19},{4,20},{5,21},{6,22},{7,23},{8,24},{9,... | collective-permute-start | bytes 1769480 | tf_op jit(solution)/shard_map/ppermute | solution.py:63
  64.8 14.5 %collective-permute-start.14 = (bf16[1152,128]{1,0:T(8,128)(2,1)S(1)}, bf16[1152,128]{1,0:T(8,128)(2,1)S(1)}, u32[]{:S(2)}, u32[]{:S(2)}) collective-permute-start(bf16[1152,128]{1,0:T(8,128)(2,1)S(1)} %get-tuple-element.58), channel_id=1, source_target_pairs={{0,24},{1,25},{2,26},{3,27},{4,28},{5,29},{6,30},{7,31},{8,0},{9,1... | collective-permute-start | bytes 884744 | tf_op jit(solution)/shard_map/ppermute | solution.py:63
  65.3 15.6 %collective-permute-start.15 = (bf16[1152,128]{1,0:T(8,128)(2,1)S(1)}, bf16[1152,128]{1,0:T(8,128)(2,1)S(1)}, u32[]{:S(2)}, u32[]{:S(2)}) collective-permute-start(bf16[1152,128]{1,0:T(8,128)(2,1)S(1)} %get-tuple-element.59), channel_id=1, source_target_pairs={{0,28},{1,29},{2,30},{3,31},{4,24},{5,25},{6,26},{7,27},{8,4},{9,5... | collective-permute-start | bytes 884744 | tf_op jit(solution)/shard_map/ppermute | solution.py:63
  66.1 14.8 %collective-permute-start.16 = (bf16[1152,128]{1,0:T(8,128)(2,1)S(1)}, bf16[1152,128]{1,0:T(8,128)(2,1)S(1)}, u32[]{:S(2)}, u32[]{:S(2)}) collective-permute-start(bf16[1152,128]{1,0:T(8,128)(2,1)S(1)} %get-tuple-element.60), channel_id=1, source_target_pairs={{0,8},{1,9},{2,10},{3,11},{4,12},{5,13},{6,14},{7,15},{8,16},{9,17... | collective-permute-start | bytes 884744 | tf_op jit(solution)/shard_map/ppermute | solution.py:63
  67.2 14.6 %collective-permute-start.17 = (bf16[1152,128]{1,0:T(8,128)(2,1)S(1)}, bf16[1152,128]{1,0:T(8,128)(2,1)S(1)}, u32[]{:S(2)}, u32[]{:S(2)}) collective-permute-start(bf16[1152,128]{1,0:T(8,128)(2,1)S(1)} %get-tuple-element.61), channel_id=1, source_target_pairs={{0,12},{1,13},{2,14},{3,15},{4,8},{5,9},{6,10},{7,11},{8,20},{9,21... | collective-permute-start | bytes 884744 | tf_op jit(solution)/shard_map/ppermute | solution.py:63
  77.4 10.8 %collective-permute-start.18 = (bf16[1152,128]{1,0:T(8,128)(2,1)S(1)}, bf16[1152,128]{1,0:T(8,128)(2,1)S(1)}, u32[]{:S(2)}, u32[]{:S(2)}) collective-permute-start(bf16[1152,128]{1,0:T(8,128)(2,1)S(1)} %get-tuple-element.67), channel_id=1, source_target_pairs={{0,16},{1,17},{2,18},{3,19},{4,20},{5,21},{6,22},{7,23},{8,24},{9,... | collective-permute-start | bytes 884744 | tf_op jit(solution)/shard_map/ppermute | solution.py:63
  79.3 8.9 %collective-permute-start.19 = (bf16[1152,128]{1,0:T(8,128)(2,1)S(1)}, bf16[1152,128]{1,0:T(8,128)(2,1)S(1)}, u32[]{:S(2)}, u32[]{:S(2)}) collective-permute-start(bf16[1152,128]{1,0:T(8,128)(2,1)S(1)} %get-tuple-element.68), channel_id=1, source_target_pairs={{0,20},{1,21},{2,22},{3,23},{4,16},{5,17},{6,18},{7,19},{8,28},{9,... | collective-permute-start | bytes 884744 | tf_op jit(solution)/shard_map/ppermute | solution.py:63
  88.4 7.7 %collective-permute-start.22 = (bf16[288,128]{1,0:T(8,128)(2,1)S(1)}, bf16[288,128]{1,0:T(8,128)(2,1)S(1)}, u32[]{:S(2)}, u32[]{:S(2)}) collective-permute-start(bf16[288,128]{1,0:T(8,128)(2,1)S(1)} %get-tuple-element.83), channel_id=1, source_target_pairs={{0,1},{1,2},{2,3},{3,0},{4,5},{5,6},{6,7},{7,4},{8,9},{9,10},{10,1... | collective-permute-start | bytes 221192 | tf_op jit(solution)/shard_map/ppermute | solution.py:63
  90.4 5.7 %collective-permute-start.21 = (bf16[288,128]{1,0:T(8,128)(2,1)S(1)}, bf16[288,128]{1,0:T(8,128)(2,1)S(1)}, u32[]{:S(2)}, u32[]{:S(2)}) collective-permute-start(bf16[288,128]{1,0:T(8,128)(2,1)S(1)} %get-tuple-element.84), channel_id=1, source_target_pairs={{0,2},{1,3},{2,0},{3,1},{4,6},{5,7},{6,4},{7,5},{8,10},{9,11},{10,... | collective-permute-start | bytes 221192 | tf_op jit(solution)/shard_map/ppermute | solution.py:63
  92.5 3.4 %collective-permute-start.20 = (bf16[288,128]{1,0:T(8,128)(2,1)S(1)}, bf16[288,128]{1,0:T(8,128)(2,1)S(1)}, u32[]{:S(2)}, u32[]{:S(2)}) collective-permute-start(bf16[288,128]{1,0:T(8,128)(2,1)S(1)} %get-tuple-element.85), channel_id=1, source_target_pairs={{0,3},{1,0},{2,1},{3,2},{4,7},{5,4},{6,5},{7,6},{8,11},{9,8},{10,9... | collective-permute-start | bytes 221192 | tf_op jit(solution)/shard_map/ppermute | solution.py:63
  94.5 15.3 %collective-permute-start.25 = (bf16[1024,128]{1,0:T(8,128)(2,1)S(1)}, bf16[1024,128]{1,0:T(8,128)(2,1)S(1)}, u32[]{:S(2)}, u32[]{:S(2)}) collective-permute-start(bf16[1024,128]{1,0:T(8,128)(2,1)S(1)} %get-tuple-element.72), channel_id=1, source_target_pairs={{0,3},{1,0},{2,1},{3,2},{4,7},{5,4},{6,5},{7,6},{8,11},{9,8},{10,9... | collective-permute-start | bytes 786440 | tf_op jit(solution)/shard_map/ppermute | solution.py:63
  94.5 15.4 %collective-permute-start.26 = (bf16[1024,128]{1,0:T(8,128)(2,1)S(1)}, bf16[1024,128]{1,0:T(8,128)(2,1)S(1)}, u32[]{:S(2)}, u32[]{:S(2)}) collective-permute-start(bf16[1024,128]{1,0:T(8,128)(2,1)S(1)} %get-tuple-element.73), channel_id=1, source_target_pairs={{0,2},{1,3},{2,0},{3,1},{4,6},{5,7},{6,4},{7,5},{8,10},{9,11},{10,... | collective-permute-start | bytes 786440 | tf_op jit(solution)/shard_map/ppermute | solution.py:63
  95.9 14.0 %collective-permute-start.27 = (bf16[1024,128]{1,0:T(8,128)(2,1)S(1)}, bf16[1024,128]{1,0:T(8,128)(2,1)S(1)}, u32[]{:S(2)}, u32[]{:S(2)}) collective-permute-start(bf16[1024,128]{1,0:T(8,128)(2,1)S(1)} %get-tuple-element.74), channel_id=1, source_target_pairs={{0,1},{1,2},{2,3},{3,0},{4,5},{5,6},{6,7},{7,4},{8,9},{9,10},{10,1... | collective-permute-start | bytes 786440 | tf_op jit(solution)/shard_map/ppermute | solution.py:63
  96.5 6.7 %collective-permute-start.23 = (bf16[2,32,128]{2,1,0:T(8,128)(2,1)S(1)}, bf16[2,32,128]{2,1,0:T(8,128)(2,1)S(1)}, u32[]{:S(2)}, u32[]{:S(2)}) collective-permute-start(bf16[2,32,128]{2,1,0:T(8,128)(2,1)S(1)} %dynamic-slice_bitcast_fusion.10), channel_id=1, source_target_pairs={{0,32},{1,33},{2,34},{3,35},{4,36},{5,37},{6,38},{7,39},{8,40},{9,... | collective-permute-start | bytes 49160 | tf_op jit(solution)/shard_map/ppermute | solution.py:63
  103.1 8.1 %collective-permute-start.24 = (f32[32,128]{1,0:T(8,128)S(1)}, f32[32,128]{1,0:T(8,128)S(1)}, u32[]{:S(2)}, u32[]{:S(2)}) collective-permute-start(f32[32,128]{1,0:T(8,128)S(1)} %dynamic-slice_bitcast_fusion.9), channel_id=1, source_target_pairs={{0,64},{1,65},{2,66},{3,67},{4,68},{5,69},{6,70},{7,71},{8,72},{9,... | collective-permute-start | bytes 49160 | tf_op jit(solution)/shard_map/ppermute | solution.py:63

commit v5 on v4

--- a/solution.py
+++ b/solution.py
@@ -45,10 +45,6 @@
 
 def along_both(s):
     return device_pairs(lambda r, x, z, y: (r, x + s, z + 1, y) if r % 2 == 0 else (r, x, z + 1, y + s))
-
-
-def along_resp(s):
-    return device_pairs(lambda r, x, z, y: (r + s, x, z, y))
 
 
 def across_cores():
@@ -267,10 +263,8 @@
     lse_ref,
     delta_ref,
     kv_ref,
-    p0_ref,
-    p1_ref,
-    p2_ref,
-    p3_ref,
+    near_ref,
+    far_ref,
     o0_ref,
     o1_ref,
     o2_ref,
@@ -287,8 +281,9 @@
     run = jnp.where(slots < RUN, order_ref[0, 128 * c], order_ref[0, 128 * c + RUN])
     live = run + (slots & (RUN - 1)) < lengths_ref[0]
     stats = (jnp.where(live, lse_ref[...] * LOG2E, 1e30), delta_ref[...])
-    for i, ref in enumerate((p0_ref, p1_ref, p2_ref, p3_ref)):
-        prompts[i] = ref[...]
+    for i, ref in enumerate((near_ref, far_ref)):
+        prompts[2 * i] = ref[pl.ds(0, 32), :]
+        prompts[2 * i + 1] = ref[pl.ds(32, 32), :]
     terms = []
     for j in range(2):
         rest = stats[j]
@@ -309,7 +304,7 @@
         g = (head + s) & 3
         spread = dot(terms, (from_head == to_head + 8 * g).astype(BF16), NN)
         ref[pl.ds(0, 256), :] = kv_ref[g]
-        ref[pl.ds(256, 32), :] = prompts[(r - g) & 3]
+        ref[pl.ds(256, 32), :] = prompts[r ^ g]
         ref[pl.ds(288, 48), :] = dot(gather, jnp.where(here, spread, 0.0).astype(BF16), NN).astype(BF16)
 
 
@@ -323,7 +318,7 @@
     return pl.pallas_call(
         chunks_kernel,
         out_shape=[jax.ShapeDtypeStruct((336, 128), BF16)] * 4 + [jax.ShapeDtypeStruct((72,), jnp.int32)],
-        in_specs=[smem] * 3 + [vmem] * 7,
+        in_specs=[smem] * 3 + [vmem] * 5,
         out_specs=[vmem] * 4 + [smem],
         scratch_shapes=[pltpu.VMEM((4, 32, 128), BF16)],
         compiler_params=pltpu.CompilerParams(vmem_limit_bytes=16 * 2**20),
@@ -362,7 +357,8 @@
     last_chunk = q_chunk((head + 3) % 4)
 
     prompt = jnp.concatenate([prompt_keys[:, 0], prompt_values[:, 0]], axis=0)
-    prompts = [prompt] + [send(prompt, along_resp(s)) for s in (1, 2, 3)]
+    prompt = jnp.concatenate([prompt, send(prompt, across_cores())], axis=0)
+    prompts = [prompt, send(prompt, across_z_hi())]
     delta = jnp.sum(grad_out[0].astype(F32) * attn_out[0].astype(F32), axis=-1)
     resp_kv = jnp.stack([resp_keys[0], resp_values[0]]).transpose(2, 0, 1, 3).reshape(4, 256, 128)
     me = jnp.stack([core, head, block, z, r, c]).astype(jnp.int32)

time: 113 us -> 124 us (1.097)
  starting transfers between devices: 47.1 us -> 59.6 us
  waiting for transfers between devices: 13.5 us -> 11.3 us
    ppermute x28 -> x27, starting transfers between devices: 47.1 us -> 59.6 us  [send(): return lax.ppermute(value, AXES, pairs)]
    ppermute x28 -> x27, waiting for transfers between devices: 13.5 us -> 11.3 us  [send(): return lax.ppermute(value, AXES, pairs)]
  transfers between devices with their start and end apart: 28 -> 27, of which waited for: 6 -> 8; matrix products, arithmetic and copies ran while one was open for 8% -> 7% of each run, Pallas kernels for 35% -> 32%
where the time goes in v5:
time: 124 us; the launch traced here: 122 us
  starting transfers between devices  59.6 us (48%)
  Pallas kernels  39.4 us (32%)
  waiting for transfers between devices  11.3 us (9%)
  local copies, waits for them, and re-layouts  5.83 us (5%)
  other arithmetic  4.28 us (3%)
  between operations  1.74 us (1%)
    ppermute x27, starting transfers between devices, send(): return lax.ppermute(value, AXES, pairs)  59.6 us
    pallas_call x4, Pallas kernels, block_grads(): pl.pallas_call(functools.partial(grads_kernel, halves, len(kv), first, la...  36.7 us
    ppermute x27, waiting for transfers between devices, send(): return lax.ppermute(value, AXES, pairs)  11.3 us
    pallas_call x1, Pallas kernels, make_chunks(): pl.pallas_call(chunks_kernel, out_shape=[jax.ShapeDtypeStruct((336, 128),...  2.67 us
    concatenate x4, other arithmetic, q_chunk(): return jnp.concatenate([q, do], axis=0)  2.53 us
  transfers between devices with their start and end apart: 27, of which 8 were waited for; matrix products, arithmetic and copies ran while one was open for 7% of the time, Pallas kernels for 32%

profile of v5, /device:TPU:1, one launch (start us, length us, event | category | flops | bytes accessed | tf_op | source)
XLA Modules:
  0.0 122.1 jit_solution(11344599673328121585)
XLA Ops:
  0.6 0.8 pad_maximum_fusion.7
  1.4 1.4 %collective-permute-start = (bf16[32,128]{1,0:T(8,128)(2,1)S(1)}, bf16[32,128]{1,0:T(8,128)(2,1)S(1)}, u32[]{:S(2)}, u32[]{:S(2)}) collective-permute-start(bf16[32,128]{1,0:T(8,128)(2,1)S(1)} %pad_maximum_fusion.7), channel_id=1, source_target_pairs={{0,32},{1,33},{2,34},{3,35},{4,36},{5,37},{6,38},{7,39},{8,40},{9,... | collective-permute-start | bytes 24584 | tf_op jit(solution)/shard_map/ppermute | solution.py:59
  2.9 1.2 dynamic-slice_bitcast_fusion.4
  4.0 0.0 copy-start.2
  4.1 0.1 dynamic-slice_bitcast_fusion.3
  4.2 0.8 pad_maximum_fusion.1
  5.1 1.4 %collective-permute-start.5 = (bf16[2048,128]{1,0:T(8,128)(2,1)}, bf16[2048,128]{1,0:T(8,128)(2,1)S(1)}, u32[]{:S(2)}, u32[]{:S(2)}) collective-permute-start(bf16[2048,128]{1,0:T(8,128)(2,1)} %pad_maximum_fusion.1), channel_id=1, source_target_pairs={{0,1},{1,2},{2,3},{3,0},{4,5},{5,6},{6,7},{7,4},{8,9},{9,10},{10,1... | collective-permute-start | bytes 1572872 | tf_op jit(solution)/shard_map/ppermute | solution.py:59
  6.4 0.8 pad_maximum_fusion.2
  7.2 2.5 %collective-permute-start.6 = (bf16[2048,128]{1,0:T(8,128)(2,1)}, bf16[2048,128]{1,0:T(8,128)(2,1)S(1)}, u32[]{:S(2)}, u32[]{:S(2)}) collective-permute-start(bf16[2048,128]{1,0:T(8,128)(2,1)} %pad_maximum_fusion.2), channel_id=1, source_target_pairs={{0,2},{1,3},{2,0},{3,1},{4,6},{5,7},{6,4},{7,5},{8,10},{9,11},{10,... | collective-permute-start | bytes 1572872 | tf_op jit(solution)/shard_map/ppermute | solution.py:59
  9.7 0.6 multiply_reduce_fusion.delta_ref
  10.4 3.7 %collective-permute-start.1 = (bf16[64,128]{1,0:T(8,128)(2,1)S(1)}, bf16[64,128]{1,0:T(8,128)(2,1)S(1)}, u32[]{:S(2)}, u32[]{:S(2)}) collective-permute-start(bf16[64,128]{1,0:T(8,128)(2,1)S(1)} %pad_maximum_fusion.6.near_ref), channel_id=1, source_target_pairs={{0,64},{1,65},{2,66},{3,67},{4,68},{5,69},{6,70},{7,71},{8,72},{9,... | collective-permute-start | bytes 49160 | tf_op jit(solution)/shard_map/ppermute | solution.py:59
  14.0 0.2 maximum_bitcast_fusion
  14.9 0.1 copy.15
  15.1 0.1 stack.53.me_ref
  15.2 0.0 collective-permute-done.1.far_ref
  15.2 2.7 %shard_map.137 = (bf16[336,128]{1,0:T(8,128)(2,1)S(1)}, bf16[336,128]{1,0:T(8,128)(2,1)S(1)}, bf16[336,128]{1,0:T(8,128)(2,1)S(1)}, bf16[336,128]{1,0:T(8,128)(2,1)S(1)}, s32[72]{0:T(128)S(1)}) custom-call(s32[6]{0:T(128)S(1)} %stack.53.me_ref, s32[1,4096]{1,0:T(1,128)S(1)} %copy-done, s32[1]{0:T(128)S(6)} %copy.51.lengths_ref, f32[128,32]{1,0:T(8,128)S(1)} %bitcast.97, ...), custom_call_target="tpu_custom_call" | custom-call | flops 200000000 | bytes 1000000 | tf_op jit(solution)/shard_map/pallas_call | solution.py:318
  17.9 0.1 collective-permute-start.2
  17.9 2.3 %collective-permute-start.3 = (bf16[336,128]{1,0:T(8,128)(2,1)S(1)}, bf16[336,128]{1,0:T(8,128)(2,1)S(1)}, u32[]{:S(2)}, u32[]{:S(2)}) collective-permute-start(bf16[336,128]{1,0:T(8,128)(2,1)S(1)} %get-tuple-element.44), channel_id=1, source_target_pairs={{0,2},{1,3},{2,0},{3,1},{4,6},{5,7},{6,4},{7,5},{8,10},{9,11},{10,... | collective-permute-start | bytes 258056 | tf_op jit(solution)/shard_map/ppermute | solution.py:59
  20.3 0.3 collective-permute-start.4
  20.6 0.9 pad_maximum_fusion
  21.5 1.9 %collective-permute-done.2 = bf16[336,128]{1,0:T(8,128)(2,1)S(1)} collective-permute-done((bf16[336,128]{1,0:T(8,128)(2,1)S(1)}, bf16[336,128]{1,0:T(8,128)(2,1)S(1)}, u32[]{:S(2)}, u32[]{:S(2)}) %collective-permute-start.2) | collective-permute-done | bytes 86048 | tf_op jit(solution)/shard_map/ppermute | solution.py:59
  23.4 0.8 collective-permute-done.4
  24.3 0.0 collective-permute-done.6.rest_2_
  24.3 1.4 %collective-permute-start.8 = (bf16[1152,128]{1,0:T(8,128)(2,1)S(1)}, bf16[1152,128]{1,0:T(8,128)(2,1)S(1)}, u32[]{:S(2)}, u32[]{:S(2)}) collective-permute-start(bf16[1152,128]{1,0:T(8,128)(2,1)S(1)} %pad_maximum_fusion.4.rest_1_), channel_id=1, source_target_pairs={{0,4},{1,5},{2,6},{3,7},{4,0},{5,1},{6,2},{7,3},{8,12},{9,13},{10,... | collective-permute-start | bytes 884744 | tf_op jit(solution)/shard_map/ppermute | solution.py:59
  25.7 1.8 %collective-permute-start.7 = (bf16[2048,128]{1,0:T(8,128)(2,1)}, bf16[2048,128]{1,0:T(8,128)(2,1)S(1)}, u32[]{:S(2)}, u32[]{:S(2)}) collective-permute-start(bf16[2048,128]{1,0:T(8,128)(2,1)} %pad_maximum_fusion), channel_id=1, source_target_pairs={{0,3},{1,0},{2,1},{3,2},{4,7},{5,4},{6,5},{7,6},{8,11},{9,8},{10,9... | collective-permute-start | bytes 1572872 | tf_op jit(solution)/shard_map/ppermute | solution.py:59
  27.6 1.0 dynamic-slice_bitcast_fusion.1
  28.6 1.4 %collective-permute-done.8.rest_4_ = bf16[1152,128]{1,0:T(8,128)(2,1)S(1)} collective-permute-done((bf16[1152,128]{1,0:T(8,128)(2,1)S(1)}, bf16[1152,128]{1,0:T(8,128)(2,1)S(1)}, u32[]{:S(2)}, u32[]{:S(2)}) %collective-permute-start.8) | collective-permute-done | bytes 294944 | tf_op jit(solution)/shard_map/ppermute | solution.py:59
  30.0 4.1 %collective-permute-start.11 = (bf16[2304,128]{1,0:T(8,128)(2,1)S(1)}, bf16[2304,128]{1,0:T(8,128)(2,1)S(1)}, u32[]{:S(2)}, u32[]{:S(2)}) collective-permute-start(bf16[2304,128]{1,0:T(8,128)(2,1)S(1)} %constant_dynamic-update-slice_fusion), channel_id=1, source_target_pairs={{0,24},{1,25},{2,26},{3,27},{4,28},{5,29},{6,30},{7,31},{8,0},{9,1... | collective-permute-start | bytes 1769480 | tf_op jit(solution)/shard_map/ppermute | solution.py:59
  34.2 0.0 collective-permute-start.10
  34.2 0.1 collective-permute-done.7.rest_3_
  34.3 5.6 %shard_map.138 = (f32[1024,512]{1,0:T(8,128)S(1)}, bf16[1152,128]{1,0:T(8,128)(2,1)S(1)}, bf16[8192,128]{1,0:T(8,128)(2,1)S(1)}) custom-call(s32[72]{0:T(128)S(1)} %get-tuple-element.41.at_ref, bf16[192,128]{1,0:T(8,128)(2,1)S(1)} %pad_maximum_fusion.5.stats_ref, bf16[2048,128]{1,0:T(8,128)(2,1)S(1)} %pad_maximum_fusion.3.rest_0_, ...), custom_call_target="tpu_custom_call" | custom-call | flops 5000000000 | bytes 8000000 | tf_op jit(solution)/shard_map/pallas_call | solution.py:246
  39.8 0.7 collective-permute-start.12
  40.6 2.9 %collective-permute-start.9 = (bf16[2304,128]{1,0:T(8,128)(2,1)S(1)}, bf16[2304,128]{1,0:T(8,128)(2,1)S(1)}, u32[]{:S(2)}, u32[]{:S(2)}) collective-permute-start(bf16[2304,128]{1,0:T(8,128)(2,1)S(1)} %constant_dynamic-update-slice_fusion), channel_id=1, source_target_pairs={{0,16},{1,17},{2,18},{3,19},{4,20},{5,21},{6,22},{7,23},{8,24},{9,... | collective-permute-start | bytes 1769480 | tf_op jit(solution)/shard_map/ppermute | solution.py:59
  43.5 0.7 collective-permute-done.11.rest_2_
  44.1 0.3 collective-permute-done.10.rest_1_
  44.4 16.0 %shard_map.139 = (f32[1024,512]{1,0:T(8,128)S(1)}, bf16[1152,128]{1,0:T(8,128)(2,1)S(1)}, bf16[1152,128]{1,0:T(8,128)(2,1)S(1)}, bf16[1152,128]{1,0:T(8,128)(2,1)S(1)}, bf16[1152,128]{1,0:T(8,128)(2,1)S(1)}) custom-call(s32[72]{0:T(128)S(1)} %get-tuple-element.41.at_ref, bf16[192,128]{1,0:T(8,128)(2,1)S(1)} %pad_maximum_fusion.5.stats_ref, ...), custom_call_target="tpu_custom_call" | custom-call | flops 20000000000 | bytes 8000000 | tf_op jit(solution)/shard_map/pallas_call | solution.py:246
  60.4 3.2 %collective-permute-start.13 = (bf16[1152,128]{1,0:T(8,128)(2,1)S(1)}, bf16[1152,128]{1,0:T(8,128)(2,1)S(1)}, u32[]{:S(2)}, u32[]{:S(2)}) collective-permute-start(bf16[1152,128]{1,0:T(8,128)(2,1)S(1)} %get-tuple-element.58), channel_id=1, source_target_pairs={{0,24},{1,25},{2,26},{3,27},{4,28},{5,29},{6,30},{7,31},{8,0},{9,1... | collective-permute-start | bytes 884744 | tf_op jit(solution)/shard_map/ppermute | solution.py:59
  63.6 0.0 collective-permute-start.14
  63.6 1.4 %collective-permute-start.15 = (bf16[1152,128]{1,0:T(8,128)(2,1)S(1)}, bf16[1152,128]{1,0:T(8,128)(2,1)S(1)}, u32[]{:S(2)}, u32[]{:S(2)}) collective-permute-start(bf16[1152,128]{1,0:T(8,128)(2,1)S(1)} %get-tuple-element.60), channel_id=1, source_target_pairs={{0,8},{1,9},{2,10},{3,11},{4,12},{5,13},{6,14},{7,15},{8,16},{9,17... | collective-permute-start | bytes 884744 | tf_op jit(solution)/shard_map/ppermute | solution.py:59
  65.0 1.0 collective-permute-start.16
  66.0 0.0 collective-permute-done.9.rest_1_
  66.0 8.7 %shard_map.140 = (f32[1024,512]{1,0:T(8,128)S(1)}, bf16[1152,128]{1,0:T(8,128)(2,1)S(1)}, bf16[1152,128]{1,0:T(8,128)(2,1)S(1)}) custom-call(s32[72]{0:T(128)S(1)} %get-tuple-element.41.at_ref, bf16[192,128]{1,0:T(8,128)(2,1)S(1)} %pad_maximum_fusion.5.stats_ref, bf16[8192,128]{1,0:T(8,128)(2,1)S(1)} %get-tuple-element.51.rest_0_, ...), custom_call_target="tpu_custom_call" | custom-call | flops 10000000000 | bytes 8000000 | tf_op jit(solution)/shard_map/pallas_call | solution.py:246
  74.7 2.6 %collective-permute-start.17 = (bf16[1152,128]{1,0:T(8,128)(2,1)S(1)}, bf16[1152,128]{1,0:T(8,128)(2,1)S(1)}, u32[]{:S(2)}, u32[]{:S(2)}) collective-permute-start(bf16[1152,128]{1,0:T(8,128)(2,1)S(1)} %get-tuple-element.67), channel_id=1, source_target_pairs={{0,16},{1,17},{2,18},{3,19},{4,20},{5,21},{6,22},{7,23},{8,24},{9,... | collective-permute-start | bytes 884744 | tf_op jit(solution)/shard_map/ppermute | solution.py:59
  77.3 0.0 collective-permute-done.13.rest_4_
  77.3 0.5 collective-permute-start.18
  77.8 0.0 collective-permute-done.14.rest_5_
  77.8 0.0 collective-permute-done.15.rest_6_
  77.8 6.3 %shard_map.141 = (bf16[1024,128]{1,0:T(8,128)(2,1)S(1)}, bf16[1024,128]{1,0:T(8,128)(2,1)S(1)}, bf16[1024,128]{1,0:T(8,128)(2,1)S(1)}, bf16[1024,128]{1,0:T(8,128)(2,1)S(1)}, f32[1152,128]{1,0:T(8,128)S(1)}) custom-call(s32[72]{0:T(128)S(1)} %get-tuple-element.41.at_ref, bf16[192,128]{1,0:T(8,128)(2,1)S(1)} %pad_maximum_fusion.5.stats_ref, ...), custom_call_target="tpu_custom_call" | custom-call | flops 5000000000 | bytes 8000000 | tf_op jit(solution)/shard_map/pallas_call | solution.py:246
  84.2 5.0 %collective-permute-done.18 = bf16[1152,128]{1,0:T(8,128)(2,1)S(1)} collective-permute-done((bf16[1152,128]{1,0:T(8,128)(2,1)S(1)}, bf16[1152,128]{1,0:T(8,128)(2,1)S(1)}, u32[]{:S(2)}, u32[]{:S(2)}) %collective-permute-start.18) | collective-permute-done | bytes 294944 | tf_op jit(solution)/shard_map/ppermute | solution.py:59
  89.1 0.1 add_convert_fusion
  89.3 3.5 %collective-permute-start.21 = (bf16[288,128]{1,0:T(8,128)(2,1)S(1)}, bf16[288,128]{1,0:T(8,128)(2,1)S(1)}, u32[]{:S(2)}, u32[]{:S(2)}) collective-permute-start(bf16[288,128]{1,0:T(8,128)(2,1)S(1)} %get-tuple-element.83), channel_id=1, source_target_pairs={{0,1},{1,2},{2,3},{3,0},{4,5},{5,6},{6,7},{7,4},{8,9},{9,10},{10,1... | collective-permute-start | bytes 221192 | tf_op jit(solution)/shard_map/ppermute | solution.py:59
  92.7 1.3 %collective-permute-start.20 = (bf16[288,128]{1,0:T(8,128)(2,1)S(1)}, bf16[288,128]{1,0:T(8,128)(2,1)S(1)}, u32[]{:S(2)}, u32[]{:S(2)}) collective-permute-start(bf16[288,128]{1,0:T(8,128)(2,1)S(1)} %get-tuple-element.84), channel_id=1, source_target_pairs={{0,2},{1,3},{2,0},{3,1},{4,6},{5,7},{6,4},{7,5},{8,10},{9,11},{10,... | collective-permute-start | bytes 221192 | tf_op jit(solution)/shard_map/ppermute | solution.py:59
  94.0 2.0 %collective-permute-start.19 = (bf16[288,128]{1,0:T(8,128)(2,1)S(1)}, bf16[288,128]{1,0:T(8,128)(2,1)S(1)}, u32[]{:S(2)}, u32[]{:S(2)}) collective-permute-start(bf16[288,128]{1,0:T(8,128)(2,1)S(1)} %get-tuple-element.85), channel_id=1, source_target_pairs={{0,3},{1,0},{2,1},{3,2},{4,7},{5,4},{6,5},{7,6},{8,11},{9,8},{10,9... | collective-permute-start | bytes 221192 | tf_op jit(solution)/shard_map/ppermute | solution.py:59
  96.0 0.0 collective-permute-start.24
  96.0 1.2 %collective-permute-start.25 = (bf16[1024,128]{1,0:T(8,128)(2,1)S(1)}, bf16[1024,128]{1,0:T(8,128)(2,1)S(1)}, u32[]{:S(2)}, u32[]{:S(2)}) collective-permute-start(bf16[1024,128]{1,0:T(8,128)(2,1)S(1)} %get-tuple-element.73), channel_id=1, source_target_pairs={{0,2},{1,3},{2,0},{3,1},{4,6},{5,7},{6,4},{7,5},{8,10},{9,11},{10,... | collective-permute-start | bytes 786440 | tf_op jit(solution)/shard_map/ppermute | solution.py:59
  97.3 1.0 collective-permute-done.19
  98.3 2.7 %collective-permute-start.26 = (bf16[1024,128]{1,0:T(8,128)(2,1)S(1)}, bf16[1024,128]{1,0:T(8,128)(2,1)S(1)}, u32[]{:S(2)}, u32[]{:S(2)}) collective-permute-start(bf16[1024,128]{1,0:T(8,128)(2,1)S(1)} %get-tuple-element.74), channel_id=1, source_target_pairs={{0,1},{1,2},{2,3},{3,0},{4,5},{5,6},{6,7},{7,4},{8,9},{9,10},{10,1... | collective-permute-start | bytes 786440 | tf_op jit(solution)/shard_map/ppermute | solution.py:59
  101.2 0.2 copy.37
  101.4 14.5 %collective-permute-start.22 = (bf16[2,32,128]{2,1,0:T(8,128)(2,1)S(1)}, bf16[2,32,128]{2,1,0:T(8,128)(2,1)S(1)}, u32[]{:S(2)}, u32[]{:S(2)}) collective-permute-start(bf16[2,32,128]{2,1,0:T(8,128)(2,1)S(1)} %dynamic-slice_bitcast_fusion.10), channel_id=1, source_target_pairs={{0,32},{1,33},{2,34},{3,35},{4,36},{5,37},{6,38},{7,39},{8,40},{9,... | collective-permute-start | bytes 49160 | tf_op jit(solution)/shard_map/ppermute | solution.py:59
  115.9 0.8 fusion.4
  116.7 0.0 collective-permute-done.22
  116.7 3.3 %collective-permute-start.23 = (f32[32,128]{1,0:T(8,128)S(1)}, f32[32,128]{1,0:T(8,128)S(1)}, u32[]{:S(2)}, u32[]{:S(2)}) collective-permute-start(f32[32,128]{1,0:T(8,128)S(1)} %dynamic-slice_bitcast_fusion.9), channel_id=1, source_target_pairs={{0,64},{1,65},{2,66},{3,67},{4,68},{5,69},{6,70},{7,71},{8,72},{9,... | collective-permute-start | bytes 49160 | tf_op jit(solution)/shard_map/ppermute | solution.py:59
  120.4 1.2 copy_bitcast_fusion
  121.5 0.6 slice_bitcast_fusion.1
  (63 shorter events, 0.7 us)
Async XLA Ops:
  0.6 3.4 %copy-start.1 = (bf16[1,128,32,128]{3,2,1,0:T(8,128)(2,1)S(1)}, bf16[1,128,32,128]{3,2,1,0:T(8,128)(2,1)}, u32[]{:S(2)}) copy-start(bf16[1,128,32,128]{3,2,1,0:T(8,128)(2,1)} %param.15) | copy-start | bytes 3145732
  1.4 8.9 %collective-permute-start = (bf16[32,128]{1,0:T(8,128)(2,1)S(1)}, bf16[32,128]{1,0:T(8,128)(2,1)S(1)}, u32[]{:S(2)}, u32[]{:S(2)}) collective-permute-start(bf16[32,128]{1,0:T(8,128)(2,1)S(1)} %pad_maximum_fusion.7), channel_id=1, source_target_pairs={{0,32},{1,33},{2,34},{3,35},{4,36},{5,37},{6,38},{7,39},{8,40},{9,... | collective-permute-start | bytes 24584 | tf_op jit(solution)/shard_map/ppermute | solution.py:59
  4.0 5.6 %copy-start.2 = (bf16[1,128,32,128]{3,2,1,0:T(8,128)(2,1)S(1)}, bf16[1,128,32,128]{3,2,1,0:T(8,128)(2,1)}, u32[]{:S(2)}) copy-start(bf16[1,128,32,128]{3,2,1,0:T(8,128)(2,1)} %param.16) | copy-start | bytes 3145732
  5.0 5.3 %copy-start.6 = (bf16[16,1,128]{2,0,1:T(8,128)(2,1)S(1)}, bf16[16,1,128]{2,0,1:T(8,128)(2,1)}, u32[]{:S(2)}) copy-start(bf16[16,1,128]{2,0,1:T(8,128)(2,1)} %param.14) | copy-start | bytes 12292
  5.0 5.3 %copy-start.7 = (bf16[16,1,128]{2,0,1:T(8,128)(2,1)S(1)}, bf16[16,1,128]{2,0,1:T(8,128)(2,1)}, u32[]{:S(2)}) copy-start(bf16[16,1,128]{2,0,1:T(8,128)(2,1)} %param.13) | copy-start | bytes 12292
  5.0 9.0 %copy-start.3 = (bf16[1,128,4,128]{3,2,1,0:T(4,128)(2,1)S(1)}, bf16[1,128,4,128]{3,2,1,0:T(4,128)(2,1)}, u32[]{:S(2)}) copy-start(bf16[1,128,4,128]{3,2,1,0:T(4,128)(2,1)} %param.12) | copy-start | bytes 393220
  5.0 9.0 %copy-start.4 = (bf16[1,128,4,128]{3,2,1,0:T(4,128)(2,1)S(1)}, bf16[1,128,4,128]{3,2,1,0:T(4,128)(2,1)}, u32[]{:S(2)}) copy-start(bf16[1,128,4,128]{3,2,1,0:T(4,128)(2,1)} %param.11) | copy-start | bytes 393220
  5.1 19.3 %collective-permute-start.5 = (bf16[2048,128]{1,0:T(8,128)(2,1)}, bf16[2048,128]{1,0:T(8,128)(2,1)S(1)}, u32[]{:S(2)}, u32[]{:S(2)}) collective-permute-start(bf16[2048,128]{1,0:T(8,128)(2,1)} %pad_maximum_fusion.1), channel_id=1, source_target_pairs={{0,1},{1,2},{2,3},{3,0},{4,5},{5,6},{6,7},{7,4},{8,9},{9,10},{10,1... | collective-permute-start | bytes 1572872 | tf_op jit(solution)/shard_map/ppermute | solution.py:59
  6.4 8.5 %copy-start.5 = (f32[1,128,32]{1,2,0:T(8,128)S(1)}, f32[1,128,32]{1,2,0:T(8,128)}, u32[]{:S(2)}) copy-start(f32[1,128,32]{1,2,0:T(8,128)} %param.17) | copy-start | bytes 49156
  7.2 7.9 %copy-start = (s32[1,4096]{1,0:T(1,128)S(1)}, s32[1,4096]{1,0:T(1,128)}, u32[]{:S(2)}) copy-start(s32[1,4096]{1,0:T(1,128)} %order_ref.1) | copy-start | bytes 49156
  7.2 17.1 %collective-permute-start.6 = (bf16[2048,128]{1,0:T(8,128)(2,1)}, bf16[2048,128]{1,0:T(8,128)(2,1)S(1)}, u32[]{:S(2)}, u32[]{:S(2)}) collective-permute-start(bf16[2048,128]{1,0:T(8,128)(2,1)} %pad_maximum_fusion.2), channel_id=1, source_target_pairs={{0,2},{1,3},{2,0},{3,1},{4,6},{5,7},{6,4},{7,5},{8,10},{9,11},{10,... | collective-permute-start | bytes 1572872 | tf_op jit(solution)/shard_map/ppermute | solution.py:59
  10.4 4.8 %collective-permute-start.1 = (bf16[64,128]{1,0:T(8,128)(2,1)S(1)}, bf16[64,128]{1,0:T(8,128)(2,1)S(1)}, u32[]{:S(2)}, u32[]{:S(2)}) collective-permute-start(bf16[64,128]{1,0:T(8,128)(2,1)S(1)} %pad_maximum_fusion.6.near_ref), channel_id=1, source_target_pairs={{0,64},{1,65},{2,66},{3,67},{4,68},{5,69},{6,70},{7,71},{8,72},{9,... | collective-permute-start | bytes 49160 | tf_op jit(solution)/shard_map/ppermute | solution.py:59
  17.9 5.5 %collective-permute-start.2 = (bf16[336,128]{1,0:T(8,128)(2,1)S(1)}, bf16[336,128]{1,0:T(8,128)(2,1)S(1)}, u32[]{:S(2)}, u32[]{:S(2)}) collective-permute-start(bf16[336,128]{1,0:T(8,128)(2,1)S(1)} %get-tuple-element.43), channel_id=1, source_target_pairs={{0,1},{1,2},{2,3},{3,0},{4,5},{5,6},{6,7},{7,4},{8,9},{9,10},{10,1... | collective-permute-start | bytes 258056 | tf_op jit(solution)/shard_map/ppermute | solution.py:59
  17.9 5.5 %collective-permute-start.3 = (bf16[336,128]{1,0:T(8,128)(2,1)S(1)}, bf16[336,128]{1,0:T(8,128)(2,1)S(1)}, u32[]{:S(2)}, u32[]{:S(2)}) collective-permute-start(bf16[336,128]{1,0:T(8,128)(2,1)S(1)} %get-tuple-element.44), channel_id=1, source_target_pairs={{0,2},{1,3},{2,0},{3,1},{4,6},{5,7},{6,4},{7,5},{8,10},{9,11},{10,... | collective-permute-start | bytes 258056 | tf_op jit(solution)/shard_map/ppermute | solution.py:59
  20.3 4.0 %collective-permute-start.4 = (bf16[336,128]{1,0:T(8,128)(2,1)S(1)}, bf16[336,128]{1,0:T(8,128)(2,1)S(1)}, u32[]{:S(2)}, u32[]{:S(2)}) collective-permute-start(bf16[336,128]{1,0:T(8,128)(2,1)S(1)} %get-tuple-element.45), channel_id=1, source_target_pairs={{0,3},{1,0},{2,1},{3,2},{4,7},{5,4},{6,5},{7,6},{8,11},{9,8},{10,9... | collective-permute-start | bytes 258056 | tf_op jit(solution)/shard_map/ppermute | solution.py:59
  24.3 5.7 %collective-permute-start.8 = (bf16[1152,128]{1,0:T(8,128)(2,1)S(1)}, bf16[1152,128]{1,0:T(8,128)(2,1)S(1)}, u32[]{:S(2)}, u32[]{:S(2)}) collective-permute-start(bf16[1152,128]{1,0:T(8,128)(2,1)S(1)} %pad_maximum_fusion.4.rest_1_), channel_id=1, source_target_pairs={{0,4},{1,5},{2,6},{3,7},{4,0},{5,1},{6,2},{7,3},{8,12},{9,13},{10,... | collective-permute-start | bytes 884744 | tf_op jit(solution)/shard_map/ppermute | solution.py:59
  25.7 8.5 %collective-permute-start.7 = (bf16[2048,128]{1,0:T(8,128)(2,1)}, bf16[2048,128]{1,0:T(8,128)(2,1)S(1)}, u32[]{:S(2)}, u32[]{:S(2)}) collective-permute-start(bf16[2048,128]{1,0:T(8,128)(2,1)} %pad_maximum_fusion), channel_id=1, source_target_pairs={{0,3},{1,0},{2,1},{3,2},{4,7},{5,4},{6,5},{7,6},{8,11},{9,8},{10,9... | collective-permute-start | bytes 1572872 | tf_op jit(solution)/shard_map/ppermute | solution.py:59
  30.0 14.1 %collective-permute-start.11 = (bf16[2304,128]{1,0:T(8,128)(2,1)S(1)}, bf16[2304,128]{1,0:T(8,128)(2,1)S(1)}, u32[]{:S(2)}, u32[]{:S(2)}) collective-permute-start(bf16[2304,128]{1,0:T(8,128)(2,1)S(1)} %constant_dynamic-update-slice_fusion), channel_id=1, source_target_pairs={{0,24},{1,25},{2,26},{3,27},{4,28},{5,29},{6,30},{7,31},{8,0},{9,1... | collective-permute-start | bytes 1769480 | tf_op jit(solution)/shard_map/ppermute | solution.py:59
  34.2 10.2 %collective-permute-start.10 = (bf16[2304,128]{1,0:T(8,128)(2,1)S(1)}, bf16[2304,128]{1,0:T(8,128)(2,1)S(1)}, u32[]{:S(2)}, u32[]{:S(2)}) collective-permute-start(bf16[2304,128]{1,0:T(8,128)(2,1)S(1)} %constant_dynamic-update-slice_fusion), channel_id=1, source_target_pairs={{0,8},{1,9},{2,10},{3,11},{4,12},{5,13},{6,14},{7,15},{8,16},{9,17... | collective-permute-start | bytes 1769480 | tf_op jit(solution)/shard_map/ppermute | solution.py:59
  39.8 25.1 %collective-permute-start.12 = (bf16[1152,128]{1,0:T(8,128)(2,1)S(1)}, bf16[1152,128]{1,0:T(8,128)(2,1)S(1)}, u32[]{:S(2)}, u32[]{:S(2)}) collective-permute-start(bf16[1152,128]{1,0:T(8,128)(2,1)S(1)} %get-tuple-element.56), channel_id=1, source_target_pairs={{0,4},{1,5},{2,6},{3,7},{4,0},{5,1},{6,2},{7,3},{8,12},{9,13},{10,... | collective-permute-start | bytes 884744 | tf_op jit(solution)/shard_map/ppermute | solution.py:59
  40.6 25.4 %collective-permute-start.9 = (bf16[2304,128]{1,0:T(8,128)(2,1)S(1)}, bf16[2304,128]{1,0:T(8,128)(2,1)S(1)}, u32[]{:S(2)}, u32[]{:S(2)}) collective-permute-start(bf16[2304,128]{1,0:T(8,128)(2,1)S(1)} %constant_dynamic-update-slice_fusion), channel_id=1, source_target_pairs={{0,16},{1,17},{2,18},{3,19},{4,20},{5,21},{6,22},{7,23},{8,24},{9,... | collective-permute-start | bytes 1769480 | tf_op jit(solution)/shard_map/ppermute | solution.py:59
  60.4 16.8 %collective-permute-start.13 = (bf16[1152,128]{1,0:T(8,128)(2,1)S(1)}, bf16[1152,128]{1,0:T(8,128)(2,1)S(1)}, u32[]{:S(2)}, u32[]{:S(2)}) collective-permute-start(bf16[1152,128]{1,0:T(8,128)(2,1)S(1)} %get-tuple-element.58), channel_id=1, source_target_pairs={{0,24},{1,25},{2,26},{3,27},{4,28},{5,29},{6,30},{7,31},{8,0},{9,1... | collective-permute-start | bytes 884744 | tf_op jit(solution)/shard_map/ppermute | solution.py:59
  63.6 14.2 %collective-permute-start.14 = (bf16[1152,128]{1,0:T(8,128)(2,1)S(1)}, bf16[1152,128]{1,0:T(8,128)(2,1)S(1)}, u32[]{:S(2)}, u32[]{:S(2)}) collective-permute-start(bf16[1152,128]{1,0:T(8,128)(2,1)S(1)} %get-tuple-element.59), channel_id=1, source_target_pairs={{0,28},{1,29},{2,30},{3,31},{4,24},{5,25},{6,26},{7,27},{8,4},{9,5... | collective-permute-start | bytes 884744 | tf_op jit(solution)/shard_map/ppermute | solution.py:59
  63.6 14.2 %collective-permute-start.15 = (bf16[1152,128]{1,0:T(8,128)(2,1)S(1)}, bf16[1152,128]{1,0:T(8,128)(2,1)S(1)}, u32[]{:S(2)}, u32[]{:S(2)}) collective-permute-start(bf16[1152,128]{1,0:T(8,128)(2,1)S(1)} %get-tuple-element.60), channel_id=1, source_target_pairs={{0,8},{1,9},{2,10},{3,11},{4,12},{5,13},{6,14},{7,15},{8,16},{9,17... | collective-permute-start | bytes 884744 | tf_op jit(solution)/shard_map/ppermute | solution.py:59
  65.0 12.8 %collective-permute-start.16 = (bf16[1152,128]{1,0:T(8,128)(2,1)S(1)}, bf16[1152,128]{1,0:T(8,128)(2,1)S(1)}, u32[]{:S(2)}, u32[]{:S(2)}) collective-permute-start(bf16[1152,128]{1,0:T(8,128)(2,1)S(1)} %get-tuple-element.61), channel_id=1, source_target_pairs={{0,12},{1,13},{2,14},{3,15},{4,8},{5,9},{6,10},{7,11},{8,20},{9,21... | collective-permute-start | bytes 884744 | tf_op jit(solution)/shard_map/ppermute | solution.py:59
  74.7 9.4 %collective-permute-start.17 = (bf16[1152,128]{1,0:T(8,128)(2,1)S(1)}, bf16[1152,128]{1,0:T(8,128)(2,1)S(1)}, u32[]{:S(2)}, u32[]{:S(2)}) collective-permute-start(bf16[1152,128]{1,0:T(8,128)(2,1)S(1)} %get-tuple-element.67), channel_id=1, source_target_pairs={{0,16},{1,17},{2,18},{3,19},{4,20},{5,21},{6,22},{7,23},{8,24},{9,... | collective-permute-start | bytes 884744 | tf_op jit(solution)/shard_map/ppermute | solution.py:59
  77.3 11.8 %collective-permute-start.18 = (bf16[1152,128]{1,0:T(8,128)(2,1)S(1)}, bf16[1152,128]{1,0:T(8,128)(2,1)S(1)}, u32[]{:S(2)}, u32[]{:S(2)}) collective-permute-start(bf16[1152,128]{1,0:T(8,128)(2,1)S(1)} %get-tuple-element.68), channel_id=1, source_target_pairs={{0,20},{1,21},{2,22},{3,23},{4,16},{5,17},{6,18},{7,19},{8,28},{9,... | collective-permute-start | bytes 884744 | tf_op jit(solution)/shard_map/ppermute | solution.py:59
  89.3 11.8 %collective-permute-start.21 = (bf16[288,128]{1,0:T(8,128)(2,1)S(1)}, bf16[288,128]{1,0:T(8,128)(2,1)S(1)}, u32[]{:S(2)}, u32[]{:S(2)}) collective-permute-start(bf16[288,128]{1,0:T(8,128)(2,1)S(1)} %get-tuple-element.83), channel_id=1, source_target_pairs={{0,1},{1,2},{2,3},{3,0},{4,5},{5,6},{6,7},{7,4},{8,9},{9,10},{10,1... | collective-permute-start | bytes 221192 | tf_op jit(solution)/shard_map/ppermute | solution.py:59
  92.7 8.3 %collective-permute-start.20 = (bf16[288,128]{1,0:T(8,128)(2,1)S(1)}, bf16[288,128]{1,0:T(8,128)(2,1)S(1)}, u32[]{:S(2)}, u32[]{:S(2)}) collective-permute-start(bf16[288,128]{1,0:T(8,128)(2,1)S(1)} %get-tuple-element.84), channel_id=1, source_target_pairs={{0,2},{1,3},{2,0},{3,1},{4,6},{5,7},{6,4},{7,5},{8,10},{9,11},{10,... | collective-permute-start | bytes 221192 | tf_op jit(solution)/shard_map/ppermute | solution.py:59
  94.0 4.3 %collective-permute-start.19 = (bf16[288,128]{1,0:T(8,128)(2,1)S(1)}, bf16[288,128]{1,0:T(8,128)(2,1)S(1)}, u32[]{:S(2)}, u32[]{:S(2)}) collective-permute-start(bf16[288,128]{1,0:T(8,128)(2,1)S(1)} %get-tuple-element.85), channel_id=1, source_target_pairs={{0,3},{1,0},{2,1},{3,2},{4,7},{5,4},{6,5},{7,6},{8,11},{9,8},{10,9... | collective-permute-start | bytes 221192 | tf_op jit(solution)/shard_map/ppermute | solution.py:59
  96.0 24.1 %collective-permute-start.24 = (bf16[1024,128]{1,0:T(8,128)(2,1)S(1)}, bf16[1024,128]{1,0:T(8,128)(2,1)S(1)}, u32[]{:S(2)}, u32[]{:S(2)}) collective-permute-start(bf16[1024,128]{1,0:T(8,128)(2,1)S(1)} %get-tuple-element.72), channel_id=1, source_target_pairs={{0,3},{1,0},{2,1},{3,2},{4,7},{5,4},{6,5},{7,6},{8,11},{9,8},{10,9... | collective-permute-start | bytes 786440 | tf_op jit(solution)/shard_map/ppermute | solution.py:59
  96.0 24.1 %collective-permute-start.25 = (bf16[1024,128]{1,0:T(8,128)(2,1)S(1)}, bf16[1024,128]{1,0:T(8,128)(2,1)S(1)}, u32[]{:S(2)}, u32[]{:S(2)}) collective-permute-start(bf16[1024,128]{1,0:T(8,128)(2,1)S(1)} %get-tuple-element.73), channel_id=1, source_target_pairs={{0,2},{1,3},{2,0},{3,1},{4,6},{5,7},{6,4},{7,5},{8,10},{9,11},{10,... | collective-permute-start | bytes 786440 | tf_op jit(solution)/shard_map/ppermute | solution.py:59
  98.3 21.8 %collective-permute-start.26 = (bf16[1024,128]{1,0:T(8,128)(2,1)S(1)}, bf16[1024,128]{1,0:T(8,128)(2,1)S(1)}, u32[]{:S(2)}, u32[]{:S(2)}) collective-permute-start(bf16[1024,128]{1,0:T(8,128)(2,1)S(1)} %get-tuple-element.74), channel_id=1, source_target_pairs={{0,1},{1,2},{2,3},{3,0},{4,5},{5,6},{6,7},{7,4},{8,9},{9,10},{10,1... | collective-permute-start | bytes 786440 | tf_op jit(solution)/shard_map/ppermute | solution.py:59
  101.4 15.3 %collective-permute-start.22 = (bf16[2,32,128]{2,1,0:T(8,128)(2,1)S(1)}, bf16[2,32,128]{2,1,0:T(8,128)(2,1)S(1)}, u32[]{:S(2)}, u32[]{:S(2)}) collective-permute-start(bf16[2,32,128]{2,1,0:T(8,128)(2,1)S(1)} %dynamic-slice_bitcast_fusion.10), channel_id=1, source_target_pairs={{0,32},{1,33},{2,34},{3,35},{4,36},{5,37},{6,38},{7,39},{8,40},{9,... | collective-permute-start | bytes 49160 | tf_op jit(solution)/shard_map/ppermute | solution.py:59
  116.7 4.8 %collective-permute-start.23 = (f32[32,128]{1,0:T(8,128)S(1)}, f32[32,128]{1,0:T(8,128)S(1)}, u32[]{:S(2)}, u32[]{:S(2)}) collective-permute-start(f32[32,128]{1,0:T(8,128)S(1)} %dynamic-slice_bitcast_fusion.9), channel_id=1, source_target_pairs={{0,64},{1,65},{2,66},{3,67},{4,68},{5,69},{6,70},{7,71},{8,72},{9,... | collective-permute-start | bytes 49160 | tf_op jit(solution)/shard_map/ppermute | solution.py:59
